TPU v7x, 256 devices: a whole 4x4x8 slice. The times are simulated.
256 devices in a mesh: slab: 8 (over x, core), bulk: 32 (over y, z).
Axes of the slice: x: 4, y: 4, z: 8, core: 2. Of those that a mesh axis runs over, the one named last changes fastest.
Arguments:
- seg_offset: float32 [3, 1048576], P(None, ('slab', 'bulk')), may hold values from -1 to 1
- tangent: float32 [3, 1048576], P(None, ('slab', 'bulk')), may hold values from -3 to 3
- burgers: float32 [3, 1048576], P(None, ('slab', 'bulk')), may hold values from -3.6 to 3.6
- box_matrix: float32 [3, 3], replicated, may hold values from -1 to 1
- applied_stress: float32 [3, 3], replicated, may hold values from -3 to 3
- far_kernel: float32 [84, 10752], replicated, may hold values from -0.0024414062 to 0.0024414062
- block_cell: int32 [8192], P(('slab', 'bulk')), may hold values from 0 to 15
- fetch_table: int32 [8192, 5], P(('slab', 'bulk')), may hold values from 0 to 31
- pair_list: int32 [2, 49152], P(None, ('slab', 'bulk')), may hold values from 0 to 191, as said below
- image_shift: int32 [3, 49152], P(None, ('slab', 'bulk')), may hold values from -1 to 1
- pair_count: int32 [256], P(('slab', 'bulk')), may hold values from 161 to 192, as said below
- node_conn: int32 [2, 1048576], P(None, ('slab', 'bulk')), may hold values from 0 to 4095
Outputs:
- nodal_force: float32 [3, 1048576], P(None, ('slab', 'bulk'))
Inputs may be any that keep to these rules, and one draw needn't show every extreme that they name: `pair_list`: in columns d * 192 + k with k < 160 the second entry is 32 + k; in the others both entries are below 32 and differ. `pair_count`: at least 161; some device holds 192.
All inputs are finite; a program needn't handle non-finite values.
Results may differ from a plain program's by a relative error of at most 0.0003.
Values sent between devices are 32-bit elements; how exact they have to be, the bound alone decides.
No kernel may reach another device: no remote copies, remote signals or barrier semaphores. Data moves between devices by JAX's collectives and lax.ppermute only.
A program may use at most 64 MiB of HBM per device.

v0:
```python
import jax
import jax.numpy as jnp
import numpy as np
from jax import lax
from jax.sharding import PartitionSpec as P

CS = 16
NM = 84


KAPPA = 0.2
CORE_SQ = 0.25
HIGH = lax.Precision.HIGHEST


def exponents():
    listed = [
        (power_x, power_y, power_z)
        for power_x in range(7)
        for power_y in range(7 - power_x)
        for power_z in range(7 - power_x - power_y)
    ]
    return np.array(listed, dtype=np.int32)


def basis(offset):
    table = exponents()
    powers = [jnp.ones_like(offset)]
    for degree in range(6):
        powers.append(powers[-1] * offset)
    stacked = jnp.stack(powers)
    return stacked[table[:, 0], 0] * stacked[table[:, 1], 1] * stacked[table[:, 2], 2]


def pair_tile(left, right, shift_vec):
    gap = left[0:3, :, None] - right[0:3, None, :] - shift_vec[:, None, None]
    dist_sq = jnp.sum(gap * gap, axis=0) + CORE_SQ
    tan_tan = jnp.sum(left[3:6, :, None] * right[3:6, None, :], axis=0)
    bur_bur = jnp.sum(left[6:9, :, None] * right[6:9, None, :], axis=0)
    bur_tan = jnp.sum(left[6:9, :, None] * right[3:6, None, :], axis=0)
    tan_bur = jnp.sum(left[3:6, :, None] * right[6:9, None, :], axis=0)
    weight = KAPPA * (bur_bur * tan_tan + bur_tan * tan_bur) / (dist_sq * jnp.sqrt(dist_sq))
    pushed = weight[None] * gap
    return (jnp.sum(pushed, axis=2), -jnp.sum(pushed, axis=1))


def applied_force(applied_stress, burgers, tangent):
    sym_stress = 0.5 * (applied_stress + applied_stress.T)
    traction = jnp.sum(sym_stress[:, :, None] * burgers[None], axis=1)
    return jnp.cross(traction, tangent, axis=0)


def tile_forces(table, pair_list, image_shift, count_here, box_matrix):
    total = pair_list.shape[1]
    groups = -(-total // 8)
    padded = groups * 8 - total
    left_ids = pair_list[0].reshape(groups, 8)
    right_ids = pair_list[1].reshape(groups, 8)
    shift_vecs = jnp.sum(box_matrix[:, :, None] * image_shift.astype(jnp.float32)[None], axis=1)
    shift_pad = shift_vecs.reshape(3, groups, 8).transpose(1, 0, 2)
    valid = (
        (jnp.arange(groups * 8, dtype=jnp.int32) < count_here)
        .astype(jnp.float32)
        .reshape(groups, 8)
    )

    def group_step(packed):
        lefts, rights, vectors, marks = packed
        near_left, near_right = jax.vmap(pair_tile, in_axes=(0, 0, 1))(
            table[lefts], table[rights], vectors
        )
        return (near_left * marks[:, None, None], near_right * marks[:, None, None])

    near_left, near_right = lax.map(group_step, (left_ids, right_ids, shift_pad, valid))
    seg_len = table.shape[2]
    near_left = near_left.reshape(groups * 8, 3, seg_len)
    near_right = near_right.reshape(groups * 8, 3, seg_len)
    return (near_left, near_right)


def local(
    seg_offset,
    tangent,
    burgers,
    box_matrix,
    applied_stress,
    far_kernel,
    block_cell,
    fetch_table,
    pair_list,
    image_shift,
    pair_count,
    node_conn,
):
    blocks_here = block_cell.shape[0]
    seg_here = seg_offset.shape[1]
    seg_len = seg_here // blocks_here
    bulk_count = lax.axis_size("bulk")
    per_peer = fetch_table.shape[1]
    remote_count = bulk_count * per_peer
    seg_data = jnp.concatenate([seg_offset, tangent, burgers], axis=0)
    blocks = seg_data.reshape(9, blocks_here, seg_len).transpose(1, 0, 2)
    slab_data = lax.all_gather(blocks, "bulk", axis=0, tiled=True)
    remote_ids = jnp.arange(
        remote_count, dtype=jnp.int32
    ) // per_peer * blocks_here + fetch_table.reshape(remote_count)
    table = jnp.concatenate([blocks, jnp.take(slab_data, remote_ids, axis=0)], axis=0)
    near_left, near_right = tile_forces(table, pair_list, image_shift, pair_count[0], box_matrix)
    on_table = jax.ops.segment_sum(
        near_right, pair_list[1], num_segments=blocks_here + remote_count
    )
    near = (
        jax.ops.segment_sum(near_left, pair_list[0], num_segments=blocks_here)
        + on_table[:blocks_here]
    )
    slab_terms = jax.ops.segment_sum(
        on_table[blocks_here:], remote_ids, num_segments=bulk_count * blocks_here
    )
    near = near + lax.psum_scatter(slab_terms, "bulk", scatter_dimension=0, tiled=True)
    near_force = near.transpose(1, 0, 2).reshape(3, seg_here)
    phi = basis(seg_offset)
    charge = jnp.sum(burgers * tangent, axis=0)
    block_moments = jnp.einsum(
        "kbs,bs->bk",
        phi.reshape(NM, blocks_here, seg_len),
        charge.reshape(blocks_here, seg_len),
        precision=HIGH,
    )
    cell_onehot = (block_cell[:, None] == jnp.arange(CS, dtype=jnp.int32)[None, :]).astype(
        jnp.float32
    )
    cell_part = jnp.dot(cell_onehot.T, block_moments, precision=HIGH)
    cells_all = far_kernel.shape[1] // NM
    slab_index = lax.axis_index("slab")
    placed = lax.dynamic_update_slice_in_dim(
        jnp.zeros((cells_all, NM), jnp.float32), cell_part, slab_index * CS, 0
    )
    moments = lax.psum(placed, ("slab", "bulk"))
    own_cells = slab_index * CS + jnp.arange(CS, dtype=jnp.int32)
    cell_ids = jnp.arange(cells_all, dtype=jnp.int32)
    shifted = jnp.take(
        moments, (own_cells[:, None] - cell_ids[None, :]) % cells_all, axis=0
    ).reshape(CS, cells_all * NM)
    column_keep = (jnp.arange(cells_all * NM, dtype=jnp.int32) >= NM).astype(jnp.float32)
    masked_kernel = far_kernel * column_keep[None, :]
    local_exp = jnp.einsum("cx,kx->ck", shifted, masked_kernel, precision=HIGH)
    block_exp = jnp.dot(cell_onehot, local_exp, precision=HIGH)
    potential = jnp.einsum(
        "bk,kbs->bs", block_exp, phi.reshape(NM, blocks_here, seg_len), precision=HIGH
    ).reshape(seg_here)
    far_force = potential[None] * burgers
    seg_force = near_force + far_force + applied_force(applied_stress, burgers, tangent)
    first_end = jax.ops.segment_sum(seg_force.T, node_conn[0], num_segments=seg_here)
    second_end = jax.ops.segment_sum(seg_force.T, node_conn[1], num_segments=seg_here)
    return (0.5 * (first_end + second_end)).T


def solution(mesh):
    in_specs = (
        P(None, ("slab", "bulk")),
        P(None, ("slab", "bulk")),
        P(None, ("slab", "bulk")),
        P(),
        P(),
        P(),
        P(("slab", "bulk")),
        P(("slab", "bulk"), None),
        P(None, ("slab", "bulk")),
        P(None, ("slab", "bulk")),
        P(("slab", "bulk")),
        P(None, ("slab", "bulk")),
    )
    out_specs = P(None, ("slab", "bulk"))
    return jax.shard_map(local, mesh=mesh, in_specs=in_specs, out_specs=out_specs, check_vma=False)
```

profile of v0, /device:TPU:1, one launch (start us, length us, event | category | flops | bytes accessed | tf_op | source)
XLA Modules:
  0.0 541.7 jit_solution(11640205087336947027)
XLA Ops:
  10.4 2.0 gather_fusion.3
  12.4 2.0 gather_fusion.4
  14.5 3.7 gather_fusion.5
  21.0 3.0 fusion.16
  24.3 82.5 %psum.7 = f32[128,84]{1,0:T(8,128)S(1)} all-reduce(f32[128,84]{1,0:T(8,128)S(1)} %convolution_dynamic-update-slice_fusion), channel_id=1, replica_groups=mesh['slab'=8,'bulk'=32] {'slab','bulk'}, use_global_device_ids=true, to_apply=%region_15.16 | all-reduce | flops 10752 | bytes 86016 | tf_op jit(solution)/shard_map/psum | solution.py:138
  106.9 5.5 %gather_fusion.6 = f32[2048,84]{1,0:T(8,128)S(1)} fusion(f32[128,84]{1,0:T(8,128)S(1)} %psum.7, s32[2048]{0:T(1024)S(1)} %fusion.35), kind=kCustom, calls=%fused_computation.6 | custom fusion | bytes 1384448 | tf_op jit(solution)/shard_map/jit(_take)/gather | solution.py:141
  116.4 5.1 fusion.11
  121.7 2.0 fusion.14
  123.7 8.5 %copy.74 = f32[1024,9,128]{2,1,0:T(8,128)} copy(f32[1024,9,128]{2,0,1:T(8,128)} %all-gather.2.cloned.1.call-done) | data formatting | bytes 9437184 | tf_op jit(solution)/shard_map/all_gather | solution.py:103
  132.2 4.1 gather_fusion.2
  137.9 173.6 %while.12 = (s32[]{:T(128)}, f32[24,8,3,128]{3,2,1,0:T(4,128)S(1)}, f32[24,8,3,128]{3,2,1,0:T(4,128)S(1)}, s32[24,8]{1,0:T(8,128)S(1)}, f32[192,9,128]{2,1,0:T(8...) while((s32[]{:T(128)}, f32[24,8,3,128]{3,2,1,0:T(4,128)S(1)}, ...), condition=%wide.region_9.10_spmd, body=%wide.region_1.9_spmd.sunk | while | flops 6951986 | bytes 6784685 | solution.py:74
  139.9 2.0 gather_fusion.1
  147.1 2.0 gather_fusion.1
  152.4 2.0 gather_fusion
  159.6 2.0 gather_fusion
  311.6 7.1 %scatter_fusion = f32[192,3,128]{2,1,0:T(4,128)S(1)} fusion(f32[192,3,128]{2,1,0:T(4,128)S(1)} %broadcast_in_dim.51, s32[192]{0:T(256)S(1)} %bitcast.139, f32[192,3,128]{2,1,0:T(4,128)S(1)} %bitcast.126), kind=kCustom, calls=%fused_computation.7 | custom fusion | flops 73728 | bytes 885504 | tf_op jit(solution)/shard_map/scatter-add | solution.py:109
  319.1 6.0 %scatter_fusion.1 = f32[1024,3,128]{2,1,0:T(4,128)S(1)} fusion(f32[1024,3,128]{2,1,0:T(4,128)S(1)} %broadcast_in_dim.54, s32[160]{0:T(256)S(1)} %bitcast.136, f32[160,3,128]{2,1,0:T(4,128)S(1)} %slice.99), kind=kCustom, calls=%fused_computation.8 | custom fusion | flops 61440 | bytes 737920 | tf_op jit(solution)/shard_map/scatter-add | solution.py:116
  326.6 145.0 %all-reduce.6.cloned.1.call-done = f32[1024,3,128]{2,1,0:T(4,128)} async-done(((f32[1024,3,128]{2,1,0:T(4,128)}), f32[1024,3,128]{2,1,0:T(4,128)}) %all-reduce.6.cloned.1.call-update) | async-done | bytes 1572880
  472.4 7.2 %scatter_fusion.2 = f32[32,3,128]{2,1,0:T(4,128)S(1)} fusion(f32[32,3,128]{2,1,0:T(4,128)S(1)} %slice_add_fusion, s32[192]{0:T(256)S(1)} %bitcast.138, f32[192,3,128]{2,1,0:T(4,128)S(1)} %bitcast.125), kind=kCustom, calls=%fused_computation.9 | custom fusion | flops 73728 | bytes 885504 | tf_op jit(solution)/shard_map/scatter-add | solution.py:113
  479.7 2.0 copy.81
  481.7 23.2 %scatter_custom_fusion.4 = f32[4096,3]{1,0:T(8,128)S(1)} fusion(s32[4096]{0:T(1024)S(1)} %bitcast.135, f32[4096,3]{1,0:T(8,128)} %copy.81, f32[]{:T(128)} %constant.65.clone.1), kind=kCustom, calls=%fused_computation.52 | custom fusion | flops 12288 | bytes 49664 | tf_op jit(solution)/shard_map/scatter-add | solution.py:154
  504.9 24.0 %scatter_custom_fusion.3 = f32[4096,3]{1,0:T(8,128)} fusion(s32[4096]{0:T(1024)S(1)} %bitcast.134, f32[4096,3]{1,0:T(8,128)} %copy.81, f32[]{:T(128)} %constant.65.clone.1), kind=kCustom, calls=%fused_computation.54 | custom fusion | flops 12288 | bytes 49664 | tf_op jit(solution)/shard_map/scatter-add | solution.py:153
  529.0 3.1 multiply_bitcast_fusion
  532.0 2.8 copy.83
  (481 shorter events, 176.9 us)
Async XLA Ops:
  6.5 1.9 copy-start.6
  6.5 2.0 copy-start.13
  6.5 117.1 %all-gather.2.cloned.1.call-start = ((), (), s32[]{:S(2)}) async-start(), calls=%async_computation | async-start | bytes 4866048 | tf_op jit(solution)/shard_map/all_gather | solution.py:103
  7.5 2.8 copy-start.3
  8.4 463.2 %all-reduce.6.cloned.1.call-start = ((), (), s32[]{:S(2)}) async-start(), calls=%async_computation.1 | async-start | bytes 4194304
  10.3 2.1 copy-start.2
  12.4 2.1 copy-start.1
  20.0 0.8 copy-start.4
  20.1 0.9 copy-start.7
  20.1 3.9 copy-start.18
  112.8 0.9 copy-start.5
  112.8 1.0 copy-start.15
  112.8 1.2 copy-start.14
  112.8 1.2 copy-start.16
  112.8 2.0 copy-start.12
  112.8 2.1 copy-start.20
  112.8 3.5 copy-start.17
  116.4 5.1 copy-start.19
  136.5 1.3 copy-start.9
  136.5 1.3 copy-start.10
  319.1 7.4 %copy-start.11 = (s32[2,4096]{1,0:T(2,128)S(1)}, s32[2,4096]{1,0:T(2,128)}, u32[]{:S(2)}) copy-start(s32[2,4096]{1,0:T(2,128)} %param.31) | copy-start | bytes 98308
  319.1 7.4 %copy-start.8 = (f32[3,4096]{1,0:T(4,128)S(1)}, f32[3,4096]{1,0:T(4,128)}, u32[]{:S(2)}) copy-start(f32[3,4096]{1,0:T(4,128)} %param.21) | copy-start | bytes 147460
  325.1 1.3 copy-start
Sparse Core Ops, SparseCore 0:
  10.0 84.7 all-gather.1
  326.6 144.9 all-reduce.5
where the time goes:
time: 547 us; the launch traced here: 542 us
  other arithmetic  150 us (27%)
  waiting for transfers between devices  145 us (27%)
  local copies, waits for them, and re-layouts  135 us (25%)
  blocking collectives  82.5 us (15%)
  between operations  15.2 us (3%)
  matrix products  10.5 us (2%)
    unnamed x3, waiting for transfers between devices  145 us
    psum x1, blocking collectives, local(): moments = lax.psum(placed, ('slab', 'bulk'))  82.5 us
    gather x24, local copies, waits for them, and re-layouts, group_step(): table[lefts]  47 us
    gather x24, local copies, waits for them, and re-layouts, group_step(): table[rights]  47 us
    reduce_sum x24, other arithmetic, pair_tile(): tan_tan = jnp.sum(left[3:6, :, None] * right[3:6, None, :], axis=0)  27.7 us
    reduce_sum x24, other arithmetic, pair_tile(): return (jnp.sum(pushed, axis=2), -jnp.sum(pushed, axis=1))  24.5 us
    scatter-add x1, other arithmetic, local(): jax.ops.segment_sum(seg_force.T, node_conn[0], num_segments=seg_here)  24 us
    scatter-add x1, other arithmetic, local(): jax.ops.segment_sum(seg_force.T, node_conn[1], num_segments=seg_here)  23.2 us
  transfers between devices with their start and end apart: 2, of which 1 were waited for; matrix products, arithmetic and copies ran while one was open for 6% of the time, Pallas kernels for 0%

commit v1 on v0

v1 whole, which is shorter than its diff:
```python
import functools

import jax
import jax.numpy as jnp
import numpy as np
from jax import lax
from jax.experimental import pallas as pl
from jax.experimental.pallas import tpu as pltpu
from jax.sharding import PartitionSpec as P

SEG = 128
CS = 16
NM = 84
SEND = 5
ROWS = 48
META = 45
KAPPA = 0.2
CORE_SQ = 0.25
HIGH = lax.Precision.HIGHEST
VMEM = pl.BlockSpec(memory_space=pltpu.VMEM)
SMEM = pl.BlockSpec(memory_space=pltpu.SMEM)
f32 = jnp.float32


def exponents():
    return [(a, b, c) for a in range(7) for b in range(7 - a) for c in range(7 - a - b)]


def iota(shape, dim):
    return lax.broadcasted_iota(jnp.int32, shape, dim)


def lane_block(index):
    return pl.ds(pl.multiple_of(index * SEG, SEG), SEG)


def fill_table(table, off, tan, bur, diag, cross):
    b = [bur[i : i + 1, :] for i in range(3)]
    t = [tan[i : i + 1, :] for i in range(3)]
    table[0:3, :] = off[...]
    for i in range(3):
        table[3 + i : 4 + i, :] = diag * (b[i] * t[i])
    for row, (i, j) in enumerate(((0, 1), (0, 2), (1, 2))):
        table[6 + row : 7 + row, :] = cross * (b[i] * t[j] + b[j] * t[i])


def shift_of(box, shift, k):
    s = [shift[i, k].astype(f32) for i in range(3)]
    return [box[c, 0] * s[0] + box[c, 1] * s[1] + box[c, 2] * s[2] for c in range(3)]


def shift_rows(vec, shape):
    row = iota(shape, 0)
    return jnp.where(row == 0, vec[0], jnp.where(row == 1, vec[1], jnp.where(row == 2, vec[2], 0.0)))


def pack_kernel(pairs, shift, box, fetch, off, tan, bur, send, table):
    fill_table(table, off, tan, bur, 2.0 * KAPPA, KAPPA)
    row, lane = iota((ROWS - META, SEG), 0), iota((ROWS - META, SEG), 1)

    def peer(p, carry):
        meta = jnp.zeros((ROWS - META, SEG), f32)
        for s in range(SEND):
            k = p * SEND + s
            at = lane_block(pairs[0, k])
            vec = shift_rows(shift_of(box, shift, k), (8, SEG))
            send[p, 8 * s : 8 * s + 8, :] = table[0:8, at] - vec
            send[p, 40 + s : 41 + s, :] = table[8:9, at]
            meta = jnp.where((row == 0) & (lane == s), fetch[p, s].astype(f32), meta)
        send[p, META:ROWS, :] = meta
        return carry

    lax.fori_loop(0, send.shape[0], peer, 0)


def tile(left, col, acc, b):
    sums = [jnp.zeros((8, SEG), f32) for _ in range(3)]
    for r in range(SEG // 8):
        gap = [left[c] - col(c, r) for c in range(3)]
        dist = gap[0] * gap[0] + CORE_SQ + gap[1] * gap[1] + gap[2] * gap[2]
        coupling = left[3] * col(3, r)
        for c in range(4, 9):
            coupling = coupling + left[c] * col(c, r)
        inv = lax.rsqrt(dist)
        weight = coupling * (inv * inv * inv)
        for c in range(3):
            push = weight * gap[c]
            acc[b, c, 8 * r : 8 * r + 8, :] += push
            sums[c] = sums[c] + push
    return [jnp.sum(s, axis=0, keepdims=True) for s in sums]


def fold(acc, near):
    lane = iota((SEG, SEG), 1)

    def block(b, total):
        for c in range(3):
            total = jnp.where(lane == 4 * b + c, jnp.sum(acc[b, c], axis=1, keepdims=True), total)
        return total

    near[...] = -lax.fori_loop(0, acc.shape[0], block, jnp.zeros((SEG, SEG), f32)).T


def clear(acc):
    def block(b, carry):
        acc[b] = jnp.zeros(acc.shape[1:], f32)
        return carry

    lax.fori_loop(0, acc.shape[0], block, 0)


def fill_columns(table, at, col):
    turned = table[0:16, at].T
    for c in range(9):
        col(c, jnp.broadcast_to(turned[:, c : c + 1], (SEG, SEG)))


def own_kernel(pairs, shift, box, count, off, tan, bur, near, table, column, acc, left_acc):
    fill_table(table, off, tan, bur, 1.0, 1.0)
    table[9:16, :] = jnp.zeros((7, table.shape[1]), f32)
    clear(acc)
    clear(left_acc)
    row = iota((8, SEG), 0)
    first = pairs.shape[1] - acc.shape[0]

    def pair(k, carry):
        a, b = pairs[0, k], pairs[1, k]

        def put(c, value):
            column[c] = value

        fill_columns(table, lane_block(b), put)
        at = lane_block(a)
        scale = jnp.where(row < 3, 1.0, jnp.where(row < 6, 2.0 * KAPPA, KAPPA))
        head = table[0:8, at] * scale - shift_rows(shift_of(box, shift, k), (8, SEG))
        left = [head[i : i + 1, :] for i in range(8)] + [table[8:9, at] * KAPPA]
        rows = tile(left, lambda c, r: column[c, 8 * r : 8 * r + 8, :], acc, b)
        for c in range(3):
            left_acc[a, c : c + 1, :] += rows[c]
        return carry

    lax.fori_loop(first, count[0], pair, 0)
    fold(acc, near)
    for b in range(acc.shape[0]):
        near[4 * b : 4 * b + 3, :] += left_acc[b, 0:3, :]


def pair_kernel(recv, off, tan, bur, ret, near, table, columns, acc, ids_vmem, ids, sem):
    peers = recv.shape[0]
    for p in range(peers):
        ids_vmem[p : p + 1, :] = recv[p, META : META + 1, :].astype(jnp.int32)
    copy = pltpu.make_async_copy(ids_vmem, ids, sem)
    copy.start()
    fill_table(table, off, tan, bur, 1.0, 1.0)
    table[9:16, :] = jnp.zeros((7, table.shape[1]), f32)
    clear(acc)

    def block(b, carry):
        def put(c, value):
            columns[b, c] = value

        fill_columns(table, lane_block(b), put)
        return carry

    lax.fori_loop(0, acc.shape[0], block, 0)
    copy.wait()

    def peer(p, carry):
        for s in range(SEND):
            b = ids[p, s]
            left = [recv[p, 8 * s + i : 8 * s + i + 1, :] for i in range(8)]
            left.append(recv[p, 40 + s : 41 + s, :])
            rows = tile(left, lambda c, r: columns[b, c, 8 * r : 8 * r + 8, :], acc, b)
            for c in range(3):
                ret[p, 3 * s + c : 3 * s + c + 1, :] = rows[c]
        ret[p, 15:16, :] = jnp.zeros((1, SEG), f32)
        return carry

    lax.fori_loop(0, peers, peer, 0)
    fold(acc, near)


def fill_phi(phi, off):
    powers = []
    for i in range(3):
        x = off[i : i + 1, :]
        made = [None, x]
        for _ in range(5):
            made.append(made[-1] * x)
        powers.append(made)
    pairs_of = {}
    for k, (a, b, c) in enumerate(exponents()):
        if (a, b) not in pairs_of:
            got = [p for p in (powers[0][a], powers[1][b]) if p is not None]
            pairs_of[a, b] = got[0] * got[1] if len(got) == 2 else got[0] if got else None
        value = pairs_of[a, b]
        if c:
            value = powers[2][c] if value is None else value * powers[2][c]
        phi[k : k + 1, :] = jnp.ones_like(powers[0][1]) if value is None else value


def dot_nt(left, right, precision=None):
    return lax.dot_general(
        left, right, (((1,), (1,)), ((), ())), precision=precision, preferred_element_type=f32
    )


def moment_kernel(cell, off, tan, bur, out, phi, charged):
    fill_phi(phi, off)
    charge = jnp.sum(bur[...] * tan[...], axis=0, keepdims=True)
    row = iota((CS, SEG), 0)
    for b in range(cell.shape[0]):
        part = charge[:, b * SEG : (b + 1) * SEG]
        charged[:, b * SEG : (b + 1) * SEG] = jnp.where(row == cell[b], part, 0.0)
    part = dot_nt(charged[...], phi[...], HIGH)
    whole = jnp.concatenate([part, jnp.zeros((CS, SEG - NM), f32)], axis=1)
    for p in range(out.shape[0]):
        out[p] = whole


def far_kernel_body(cell, stress, operator, off, tan, bur, *rest):
    count = len(rest) - 5
    sources, (out, around, shifted, phi, pots) = rest[:count], rest[count:]
    cells = count * CS
    for q in range(count):
        around[q * CS : (q + 1) * CS, :] = sources[(count - q) % count][...]
    around[cells : cells + CS, :] = sources[0][...]
    shifted[:, 0:NM] = jnp.zeros((CS, NM), f32)
    for o in range(1, cells):
        shifted[:, o * NM : (o + 1) * NM] = around[cells - o : cells - o + CS, 0:NM]
    local_exp = dot_nt(shifted[...], operator[...], HIGH)
    fill_phi(phi, off)
    pots[...] = lax.dot_general(
        local_exp, phi[...], (((1,), (0,)), ((), ())), precision=HIGH, preferred_element_type=f32
    )
    b = [bur[i : i + 1, :] for i in range(3)]
    t = [tan[i : i + 1, :] for i in range(3)]
    sym = [[0.5 * (stress[i, j] + stress[j, i]) for j in range(3)] for i in range(3)]
    trac = [sym[i][0] * b[0] + sym[i][1] * b[1] + sym[i][2] * b[2] for i in range(3)]
    for i in range(3):
        j, k = (i + 1) % 3, (i + 2) % 3
        out[i : i + 1, :] = trac[j] * t[k] - trac[k] * t[j]
    row = iota((CS, SEG), 0)
    for block in range(cell.shape[0]):
        at = slice(block * SEG, (block + 1) * SEG)
        mine = jnp.where(row == cell[block], pots[:, at], 0.0)
        out[:, at] += jnp.sum(mine, axis=0, keepdims=True) * bur[:, at]


def final_kernel(pairs, back, near_own, near_pair, far, conn, out, left_acc, force, split):
    clear(left_acc)

    def peer(p, carry):
        for s in range(SEND):
            a = pairs[0, p * SEND + s]
            left_acc[a, 0:3, :] += back[p, 3 * s : 3 * s + 3, :]
        return carry

    lax.fori_loop(0, back.shape[0], peer, 0)
    for b in range(left_acc.shape[0]):
        at = slice(b * SEG, (b + 1) * SEG)
        near = near_own[4 * b : 4 * b + 3, :] + near_pair[4 * b : 4 * b + 3, :]
        force[0:3, at] = 0.5 * (far[:, at] + near + left_acc[b, 0:3, :])
    value = force[0:3, :]
    high = value.astype(jnp.bfloat16).astype(f32)
    split[0:3, :] = high
    split[3:6, :] = value - high
    chunk = 1024
    segs = conn.shape[1]
    groups = segs // SEG
    total = jnp.zeros((6 * groups, SEG), f32)
    low_row, high_row = iota((SEG, chunk), 0), iota((groups, chunk), 0)
    for end in range(2):
        for start in range(0, segs, chunk):
            at = slice(start, start + chunk)
            node = conn[end : end + 1, at]
            low = jnp.where(low_row == (node & (SEG - 1)), 1.0, 0.0).astype(jnp.bfloat16)
            mark = high_row == (node >> 7)
            parts = [
                jnp.where(mark, split[i : i + 1, at], 0.0).astype(jnp.bfloat16) for i in range(6)
            ]
            total = total + dot_nt(jnp.concatenate(parts, axis=0), low)
    for c in range(3):
        whole = total[c * groups : (c + 1) * groups] + total[(3 + c) * groups : (4 + c) * groups]
        for g in range(groups):
            out[c : c + 1, g * SEG : (g + 1) * SEG] = whole[g : g + 1, :]


def call(body, out_shape, in_specs, scratch, flops, size=48):
    return pl.pallas_call(
        body,
        out_shape=out_shape,
        in_specs=in_specs,
        out_specs=jax.tree.map(lambda _: VMEM, out_shape),
        scratch_shapes=scratch,
        compiler_params=pltpu.CompilerParams(vmem_limit_bytes=size << 20),
        cost_estimate=pl.CostEstimate(flops=flops, bytes_accessed=1 << 20, transcendentals=0),
    )


def local(
    seg_offset,
    tangent,
    burgers,
    box_matrix,
    applied_stress,
    far_kernel,
    block_cell,
    fetch_table,
    pair_list,
    image_shift,
    pair_count,
    node_conn,
):
    blocks = block_cell.shape[0]
    segs = seg_offset.shape[1]
    peers = lax.axis_size("bulk")
    slabs = lax.axis_size("slab")
    shape = lambda *dims: jax.ShapeDtypeStruct(dims, f32)
    table = pltpu.VMEM((16, segs), f32)
    acc = pltpu.VMEM((blocks, 3, SEG, SEG), f32)
    left_acc = pltpu.VMEM((blocks, 8, SEG), f32)

    send = call(
        pack_kernel, shape(peers, ROWS, SEG), [SMEM] * 4 + [VMEM] * 3, [table], 10**6, 16
    )(pair_list, image_shift, box_matrix, fetch_table, seg_offset, tangent, burgers)
    recv = lax.all_to_all(send, "bulk", 0, 0, tiled=True)

    moments_here = call(
        moment_kernel,
        shape(peers, CS, SEG),
        [SMEM] + [VMEM] * 3,
        [pltpu.VMEM((NM, segs), f32), pltpu.VMEM((CS, segs), f32)],
        10**9,
        16,
    )(block_cell, seg_offset, tangent, burgers)
    moments = jnp.sum(lax.all_to_all(moments_here, "bulk", 0, 0, tiled=True), axis=0)
    sources = [moments] + [
        lax.ppermute(moments, "slab", [(s, (s + k) % slabs) for s in range(slabs)])
        for k in range(1, slabs)
    ]

    near_own = call(
        own_kernel,
        shape(SEG, SEG),
        [SMEM] * 4 + [VMEM] * 3,
        [table, pltpu.VMEM((9, SEG, SEG), f32), acc, left_acc],
        10**9,
        24,
    )(pair_list, image_shift, box_matrix, pair_count, seg_offset, tangent, burgers)

    ret, near_pair = call(
        pair_kernel,
        (shape(peers, 16, SEG), shape(SEG, SEG)),
        [VMEM] * 4,
        [
            table,
            pltpu.VMEM((blocks, 9, SEG, SEG), f32),
            acc,
            pltpu.VMEM((peers, SEG), jnp.int32),
            pltpu.SMEM((peers, SEG), jnp.int32),
            pltpu.SemaphoreType.DMA,
        ],
        10**10,
        40,
    )(recv, seg_offset, tangent, burgers)
    back = lax.all_to_all(ret, "bulk", 0, 0, tiled=True)

    far = call(
        far_kernel_body,
        shape(3, segs),
        [SMEM] * 2 + [VMEM] * (4 + slabs),
        [
            pltpu.VMEM((slabs * CS + CS, SEG), f32),
            pltpu.VMEM((CS, slabs * CS * NM), f32),
            pltpu.VMEM((NM, segs), f32),
            pltpu.VMEM((CS, segs), f32),
        ],
        10**9,
        24,
    )(block_cell, applied_stress, far_kernel, seg_offset, tangent, burgers, *sources)

    return call(
        final_kernel,
        shape(3, segs),
        [SMEM] + [VMEM] * 5,
        [left_acc, pltpu.VMEM((8, segs), f32), pltpu.VMEM((8, segs), f32)],
        10**9,
        24,
    )(pair_list, back, near_own, near_pair, far, node_conn)


def solution(mesh):
    both = P(None, ("slab", "bulk"))
    in_specs = (
        both,
        both,
        both,
        P(),
        P(),
        P(),
        P(("slab", "bulk")),
        P(("slab", "bulk"), None),
        both,
        both,
        P(("slab", "bulk")),
        both,
    )
    return jax.shard_map(local, mesh=mesh, in_specs=in_specs, out_specs=both, check_vma=False)
```

time: 547 us -> 125 us (0.23)
  the two profiles are of different devices: /device:TPU:1 before, /device:TPU:105 now
where the time goes in v1:
time: 125 us; the launch traced here: 123 us
  Pallas kernels  59.5 us (48%)
  starting transfers between devices  38.4 us (31%)
  waiting for transfers between devices  13.5 us (11%)
  local copies, waits for them, and re-layouts  10.6 us (8%)
    pallas_call x1, Pallas kernels, local(): call(pair_kernel, (shape(peers, 16, SEG), shape(SEG, SEG)), [VMEM] * 4, [...  28.4 us
    pallas_call x1, Pallas kernels, local(): call(own_kernel, shape(SEG, SEG), [SMEM] * 4 + [VMEM] * 3, [table, pltpu....  15.4 us
    all_to_all x1, waiting for transfers between devices, local(): recv = lax.all_to_all(send, 'bulk', 0, 0, tiled=True)  13.5 us
    ppermute x7, starting transfers between devices, local(): lax.ppermute(moments, 'slab', [(s, (s + k) % slabs) for s in range(slabs)])  11.1 us
    unnamed x41, local copies, waits for them, and re-layouts  10.6 us
    all_to_all x1, starting transfers between devices, local(): recv = lax.all_to_all(send, 'bulk', 0, 0, tiled=True)  9.78 us
    all_to_all x1, starting transfers between devices, local(): back = lax.all_to_all(ret, 'bulk', 0, 0, tiled=True)  9.24 us
    all_to_all x1, starting transfers between devices, local(): lax.all_to_all(moments_here, 'bulk', 0, 0, tiled=True)  8.29 us
  transfers between devices with their start and end apart: 10, of which 1 were waited for; matrix products, arithmetic and copies ran while one was open for 0% of the time, Pallas kernels for 42%

profile of v1, /device:TPU:105, one launch (start us, length us, event | category | flops | bytes accessed | tf_op | source)
XLA Modules:
  0.0 123.0 jit_solution(8639155062068913484)
XLA Ops:
  0.0 0.8 copy.13.fetch
  0.8 0.8 copy-done.1
  1.6 0.8 copy-done.4
  2.5 0.8 copy-done.7
  3.3 0.7 copy-done.10
  5.3 4.2 %shard_map.118 = f32[32,48,128]{2,1,0:T(8,128)} custom-call(s32[2,192]{1,0:T(2,128)S(1)} %copy-done.15, s32[3,192]{1,0:T(4,128)S(1)} %copy-done.10, f32[3,3]{1,0:T(4,128)S(1)} %copy-done.12, s32[32,5]{1,0:T(8,128)S(1)} %copy.13.fetch, f32[3,4096]{1,0:T(4,128)S(1)} %copy-done.1, f32[3,4096]{1,0:T(4,128)S(1)} %copy-done.4, f32[3,4096]{1,0:T(4,128)S(1)} %copy-done.7), custom_call_target="tpu_custom_call" | custom-call | flops 1000000 | bytes 1048576 | tf_op jit(solution)/shard_map/pallas_call | solution.py:324
  9.6 9.8 %all-to-all-start = ((f32[32,48,128]{2,1,0:T(8,128)}), f32[32,48,128]{2,1,0:T(8,128)S(1)}, u32[]{:S(2)}, u32[]{:S(2)}) async-start(f32[32,48,128]{2,1,0:T(8,128)} %shard_map.118), calls=%async_computation | async-start | bytes 1572864 | tf_op jit(solution)/shard_map/all_to_all | solution.py:327
  19.4 0.8 copy-done.2
  20.2 0.8 copy-done.5
  21.1 0.8 copy-done.8
  22.5 2.7 %shard_map.121 = f32[32,16,128]{2,1,0:T(8,128)} custom-call(s32[32]{0:T(128)S(1)} %copy-done.17, f32[3,4096]{1,0:T(4,128)S(1)} %copy-done.2, f32[3,4096]{1,0:T(4,128)S(1)} %copy-done.5, f32[3,4096]{1,0:T(4,128)S(1)} %copy-done.8), custom_call_target="tpu_custom_call" | custom-call | flops 1000000000 | bytes 1048576 | tf_op jit(solution)/shard_map/pallas_call | solution.py:329
  25.2 13.5 %all-to-all-done.recv = f32[32,48,128]{2,1,0:T(8,128)S(1)} async-done(((f32[32,48,128]{2,1,0:T(8,128)}), f32[32,48,128]{2,1,0:T(8,128)S(1)}, u32[]{:S(2)}, u32[]{:S(2)}) %all-to-all-start) | async-done | bytes 786464 | tf_op jit(solution)/shard_map/all_to_all | solution.py:327
  38.7 8.3 %all-to-all-start.2 = ((f32[32,16,128]{2,1,0:T(8,128)}), f32[32,16,128]{2,1,0:T(8,128)S(1)}, u32[]{:S(2)}, u32[]{:S(2)}) async-start(f32[32,16,128]{2,1,0:T(8,128)} %shard_map.121), calls=%async_computation.2 | async-start | bytes 524288 | tf_op jit(solution)/shard_map/all_to_all | solution.py:337
  47.1 28.4 %shard_map.119 = (f32[32,16,128]{2,1,0:T(8,128)}, f32[128,128]{1,0:T(8,128)S(1)}) custom-call(f32[32,48,128]{2,1,0:T(8,128)S(1)} %all-to-all-done.recv, f32[3,4096]{1,0:T(4,128)S(1)} %copy-done.3, f32[3,4096]{1,0:T(4,128)S(1)} %copy-done.6, f32[3,4096]{1,0:T(4,128)S(1)} %copy-done.9), custom_call_target="tpu_custom_call" | custom-call | flops 10000000000 | bytes 1048576 | tf_op jit(solution)/shard_map/pallas_call | solution.py:352
  75.5 9.2 %all-to-all-start.1 = ((f32[32,16,128]{2,1,0:T(8,128)}), f32[32,16,128]{2,1,0:T(8,128)S(1)}, u32[]{:S(2)}, u32[]{:S(2)}) async-start(f32[32,16,128]{2,1,0:T(8,128)} %get-tuple-element.7), calls=%async_computation.1 | async-start | bytes 524288 | tf_op jit(solution)/shard_map/all_to_all | solution.py:367
  84.8 3.4 %collective-permute-start = (f32[16,128]{1,0:T(8,128)S(1)}, f32[16,128]{1,0:T(8,128)S(1)}, u32[]{:S(2)}, u32[]{:S(2)}) collective-permute-start(f32[16,128]{1,0:T(8,128)S(1)} %reduce_sum.9.rest_0_), channel_id=1, source_target_pairs={{0,32},{32,64},{64,96},{96,128},{128,160},{160,192},{192,224},{224... | collective-permute-start | bytes 24584 | tf_op jit(solution)/shard_map/ppermute | solution.py:339
  88.2 1.2 collective-permute-start.1
  90.0 1.7 %collective-permute-start.2 = (f32[16,128]{1,0:T(8,128)S(1)}, f32[16,128]{1,0:T(8,128)S(1)}, u32[]{:S(2)}, u32[]{:S(2)}) collective-permute-start(f32[16,128]{1,0:T(8,128)S(1)} %reduce_sum.9.rest_0_), channel_id=1, source_target_pairs={{0,96},{32,128},{64,160},{96,192},{128,224},{160,0},{192,32},{224,... | collective-permute-start | bytes 24584 | tf_op jit(solution)/shard_map/ppermute | solution.py:339
  92.2 1.9 %collective-permute-start.4 = (f32[16,128]{1,0:T(8,128)S(1)}, f32[16,128]{1,0:T(8,128)S(1)}, u32[]{:S(2)}, u32[]{:S(2)}) collective-permute-start(f32[16,128]{1,0:T(8,128)S(1)} %reduce_sum.9.rest_0_), channel_id=1, source_target_pairs={{0,160},{32,192},{64,224},{96,0},{128,32},{160,64},{192,96},{224,1... | collective-permute-start | bytes 24584 | tf_op jit(solution)/shard_map/ppermute | solution.py:339
  94.9 1.7 %collective-permute-start.6 = (f32[16,128]{1,0:T(8,128)S(1)}, f32[16,128]{1,0:T(8,128)S(1)}, u32[]{:S(2)}, u32[]{:S(2)}) collective-permute-start(f32[16,128]{1,0:T(8,128)S(1)} %reduce_sum.9.rest_0_), channel_id=1, source_target_pairs={{0,224},{32,0},{64,32},{96,64},{128,96},{160,128},{192,160},{224,1... | collective-permute-start | bytes 24584 | tf_op jit(solution)/shard_map/ppermute | solution.py:339
  96.5 15.4 %shard_map.120.near_own = f32[128,128]{1,0:T(8,128)S(1)} custom-call(s32[2,192]{1,0:T(2,128)S(1)} %copy-done.16, s32[3,192]{1,0:T(4,128)S(1)} %copy-done.11, f32[3,3]{1,0:T(4,128)S(1)} %copy-done.13, s32[1]{0:T(128)S(6)} %copy.14.count, f32[3,4096]{1,0:T(4,128)S(1)} %copy-done.3, f32[3,4096]{1,0:T(4,128)S(1)} %copy-done.6, f32[3,4096]{1,0:T(4,128)S(1)} %copy-done.9), custom_call_target="tpu_custom_call" | custom-call | flops 1000000000 | bytes 1048576 | tf_op jit(solution)/shard_map/pallas_call | solution.py:343
  112.0 2.1 %copy-done = f32[84,10752]{1,0:T(8,128)S(1)} copy-done((f32[84,10752]{1,0:T(8,128)S(1)}, f32[84,10752]{1,0:T(8,128)}, u32[]{:S(2)}) %copy-start) | copy-done | bytes 3612696
  114.1 5.6 %shard_map.122.far = f32[3,4096]{1,0:T(4,128)S(1)} custom-call(s32[32]{0:T(128)S(1)} %copy-done.18, f32[3,3]{1,0:T(4,128)S(1)} %copy-done.14, f32[84,10752]{1,0:T(8,128)S(1)} %copy-done, f32[3,4096]{1,0:T(4,128)S(1)} %copy-done.3, f32[3,4096]{1,0:T(4,128)S(1)} %copy-done.6, f32[3,4096]{1,0:T(4,128)S(1)} %copy-done.9, f32[16,128]{1,0:T(8,128)S(1)} %reduce_sum.9.rest_0_, ...), custom_call_target="tpu_custom_call" | custom-call | flops 1000000000 | bytes 1048576 | tf_op jit(solution)/shard_map/pallas_call | solution.py:369
  119.6 3.3 %shard_map.123 = f32[3,4096]{1,0:T(4,128)} custom-call(s32[2,192]{1,0:T(2,128)S(1)} %copy-done.16, f32[32,16,128]{2,1,0:T(8,128)S(1)} %all-to-all-done.1.back, f32[128,128]{1,0:T(8,128)S(1)} %shard_map.120.near_own, f32[128,128]{1,0:T(8,128)S(1)} %get-tuple-element.8.near_pair, f32[3,4096]{1,0:T(4,128)S(1)} %shard_map.122.far, s32[2,4096]{1,0:T(2,128)S(1)} %copy-done.19), custom_call_target="tpu_custom_call" | custom-call | flops 1000000000 | bytes 1048576 | tf_op jit(solution)/shard_map/pallas_call | solution.py:383
  (44 shorter events, 3.3 us)
Async XLA Ops:
  0.8 0.8 copy-start.1
  1.6 0.8 copy-start.4
  2.4 0.8 copy-start.7
  5.3 41.7 %copy-start.3 = (f32[3,4096]{1,0:T(4,128)S(1)}, f32[3,4096]{1,0:T(4,128)}, u32[]{:S(2)}) copy-start(f32[3,4096]{1,0:T(4,128)} %off.9) | copy-start | bytes 147460
  5.3 41.7 %copy-start.6 = (f32[3,4096]{1,0:T(4,128)S(1)}, f32[3,4096]{1,0:T(4,128)}, u32[]{:S(2)}) copy-start(f32[3,4096]{1,0:T(4,128)} %tan.9) | copy-start | bytes 147460
  5.3 41.7 %copy-start.9 = (f32[3,4096]{1,0:T(4,128)S(1)}, f32[3,4096]{1,0:T(4,128)}, u32[]{:S(2)}) copy-start(f32[3,4096]{1,0:T(4,128)} %bur.9) | copy-start | bytes 147460
  9.6 29.1 %all-to-all-start = ((f32[32,48,128]{2,1,0:T(8,128)}), f32[32,48,128]{2,1,0:T(8,128)S(1)}, u32[]{:S(2)}, u32[]{:S(2)}) async-start(f32[32,48,128]{2,1,0:T(8,128)} %shard_map.118), calls=%async_computation | async-start | bytes 1572864 | tf_op jit(solution)/shard_map/all_to_all | solution.py:327
  19.4 0.8 copy-start.2
  38.7 36.8 %all-to-all-start.2 = ((f32[32,16,128]{2,1,0:T(8,128)}), f32[32,16,128]{2,1,0:T(8,128)S(1)}, u32[]{:S(2)}, u32[]{:S(2)}) async-start(f32[32,16,128]{2,1,0:T(8,128)} %shard_map.121), calls=%async_computation.2 | async-start | bytes 524288 | tf_op jit(solution)/shard_map/all_to_all | solution.py:337
  47.0 49.5 %copy-start.11 = (s32[3,192]{1,0:T(4,128)S(1)}, s32[3,192]{1,0:T(4,128)}, u32[]{:S(2)}) copy-start(s32[3,192]{1,0:T(4,128)} %shift.3) | copy-start | bytes 6916
  47.0 49.5 %copy-start.13 = (f32[3,3]{1,0:T(4,128)S(1)}, f32[3,3]{1,0:T(4,128)}, u32[]{:S(2)}) copy-start(f32[3,3]{1,0:T(4,128)} %box.3) | copy-start | bytes 112
  47.0 49.5 %copy-start.16 = (s32[2,192]{1,0:T(2,128)S(1)}, s32[2,192]{1,0:T(2,128)}, u32[]{:S(2)}) copy-start(s32[2,192]{1,0:T(2,128)} %pairs.5) | copy-start | bytes 4612
  75.5 36.5 %copy-start.14 = (f32[3,3]{1,0:T(4,128)S(1)}, f32[3,3]{1,0:T(4,128)}, u32[]{:S(2)}) copy-start(f32[3,3]{1,0:T(4,128)} %stress.1) | copy-start | bytes 112
  75.5 36.5 %copy-start.18 = (s32[32]{0:T(128)S(1)}, s32[32]{0:T(128)}, u32[]{:S(2)}) copy-start(s32[32]{0:T(128)} %cell.3) | copy-start | bytes 388
  75.5 44.1 %all-to-all-start.1 = ((f32[32,16,128]{2,1,0:T(8,128)}), f32[32,16,128]{2,1,0:T(8,128)S(1)}, u32[]{:S(2)}, u32[]{:S(2)}) async-start(f32[32,16,128]{2,1,0:T(8,128)} %get-tuple-element.7), calls=%async_computation.1 | async-start | bytes 524288 | tf_op jit(solution)/shard_map/all_to_all | solution.py:367
  84.8 9.4 %collective-permute-start = (f32[16,128]{1,0:T(8,128)S(1)}, f32[16,128]{1,0:T(8,128)S(1)}, u32[]{:S(2)}, u32[]{:S(2)}) collective-permute-start(f32[16,128]{1,0:T(8,128)S(1)} %reduce_sum.9.rest_0_), channel_id=1, source_target_pairs={{0,32},{32,64},{64,96},{96,128},{128,160},{160,192},{192,224},{224... | collective-permute-start | bytes 24584 | tf_op jit(solution)/shard_map/ppermute | solution.py:339
  88.2 6.7 %collective-permute-start.1 = (f32[16,128]{1,0:T(8,128)S(1)}, f32[16,128]{1,0:T(8,128)S(1)}, u32[]{:S(2)}, u32[]{:S(2)}) collective-permute-start(f32[16,128]{1,0:T(8,128)S(1)} %reduce_sum.9.rest_0_), channel_id=1, source_target_pairs={{0,64},{32,96},{64,128},{96,160},{128,192},{160,224},{192,0},{224,... | collective-permute-start | bytes 24584 | tf_op jit(solution)/shard_map/ppermute | solution.py:339
  90.0 29.6 %copy-start.19 = (s32[2,4096]{1,0:T(2,128)S(1)}, s32[2,4096]{1,0:T(2,128)}, u32[]{:S(2)}) copy-start(s32[2,4096]{1,0:T(2,128)} %conn.1) | copy-start | bytes 98308
  90.0 21.9 %collective-permute-start.2 = (f32[16,128]{1,0:T(8,128)S(1)}, f32[16,128]{1,0:T(8,128)S(1)}, u32[]{:S(2)}, u32[]{:S(2)}) collective-permute-start(f32[16,128]{1,0:T(8,128)S(1)} %reduce_sum.9.rest_0_), channel_id=1, source_target_pairs={{0,96},{32,128},{64,160},{96,192},{128,224},{160,0},{192,32},{224,... | collective-permute-start | bytes 24584 | tf_op jit(solution)/shard_map/ppermute | solution.py:339
  91.7 20.2 %collective-permute-start.3 = (f32[16,128]{1,0:T(8,128)S(1)}, f32[16,128]{1,0:T(8,128)S(1)}, u32[]{:S(2)}, u32[]{:S(2)}) collective-permute-start(f32[16,128]{1,0:T(8,128)S(1)} %reduce_sum.9.rest_0_), channel_id=1, source_target_pairs={{0,128},{32,160},{64,192},{96,224},{128,0},{160,32},{192,64},{224,... | collective-permute-start | bytes 24584 | tf_op jit(solution)/shard_map/ppermute | solution.py:339
  92.2 19.7 %collective-permute-start.4 = (f32[16,128]{1,0:T(8,128)S(1)}, f32[16,128]{1,0:T(8,128)S(1)}, u32[]{:S(2)}, u32[]{:S(2)}) collective-permute-start(f32[16,128]{1,0:T(8,128)S(1)} %reduce_sum.9.rest_0_), channel_id=1, source_target_pairs={{0,160},{32,192},{64,224},{96,0},{128,32},{160,64},{192,96},{224,1... | collective-permute-start | bytes 24584 | tf_op jit(solution)/shard_map/ppermute | solution.py:339
  94.2 17.8 %collective-permute-start.5 = (f32[16,128]{1,0:T(8,128)S(1)}, f32[16,128]{1,0:T(8,128)S(1)}, u32[]{:S(2)}, u32[]{:S(2)}) collective-permute-start(f32[16,128]{1,0:T(8,128)S(1)} %reduce_sum.9.rest_0_), channel_id=1, source_target_pairs={{0,192},{32,224},{64,0},{96,32},{128,64},{160,96},{192,128},{224,1... | collective-permute-start | bytes 24584 | tf_op jit(solution)/shard_map/ppermute | solution.py:339
  94.9 17.1 %collective-permute-start.6 = (f32[16,128]{1,0:T(8,128)S(1)}, f32[16,128]{1,0:T(8,128)S(1)}, u32[]{:S(2)}, u32[]{:S(2)}) collective-permute-start(f32[16,128]{1,0:T(8,128)S(1)} %reduce_sum.9.rest_0_), channel_id=1, source_target_pairs={{0,224},{32,0},{64,32},{96,64},{128,96},{160,128},{192,160},{224,1... | collective-permute-start | bytes 24584 | tf_op jit(solution)/shard_map/ppermute | solution.py:339
  112.0 2.1 %copy-start = (f32[84,10752]{1,0:T(8,128)S(1)}, f32[84,10752]{1,0:T(8,128)}, u32[]{:S(2)}) copy-start(f32[84,10752]{1,0:T(8,128)} %operator.1) | copy-start | bytes 10838020
  (6 other events, 4.4 us)

commit v2 on v1

--- a/solution.py
+++ b/solution.py
@@ -12,8 +12,9 @@
 CS = 16
 NM = 84
 SEND = 5
-ROWS = 48
 META = 45
+MOMENTS = 48
+ROWS = MOMENTS + CS
 KAPPA = 0.2
 CORE_SQ = 0.25
 HIGH = lax.Precision.HIGHEST
@@ -54,20 +55,36 @@
     return jnp.where(row == 0, vec[0], jnp.where(row == 1, vec[1], jnp.where(row == 2, vec[2], 0.0)))
 
 
-def pack_kernel(pairs, shift, box, fetch, off, tan, bur, send, table):
+def fetch_all(sources, targets, sems):
+    copies = [
+        pltpu.make_async_copy(source, target, sems.at[i])
+        for i, (source, target) in enumerate(zip(sources, targets, strict=True))
+    ]
+    for copy in copies:
+        copy.start()
+    return copies
+
+
+def pack_kernel(*refs):
+    sources, send, scratch = refs[:8], refs[8], refs[9:]
+    pairs, shift, box, fetch, cell, off, tan, bur, sems, table, phi, charged = scratch
+    for copy in fetch_all(sources, scratch[:8], sems):
+        copy.wait()
     fill_table(table, off, tan, bur, 2.0 * KAPPA, KAPPA)
-    row, lane = iota((ROWS - META, SEG), 0), iota((ROWS - META, SEG), 1)
+    row, lane = iota((MOMENTS - META, SEG), 0), iota((MOMENTS - META, SEG), 1)
+    moments = cell_moments(cell, off, tan, bur, phi, charged)
 
     def peer(p, carry):
-        meta = jnp.zeros((ROWS - META, SEG), f32)
+        meta = jnp.zeros((MOMENTS - META, SEG), f32)
         for s in range(SEND):
             k = p * SEND + s
             at = lane_block(pairs[0, k])
             vec = shift_rows(shift_of(box, shift, k), (8, SEG))
             send[p, 8 * s : 8 * s + 8, :] = table[0:8, at] - vec
             send[p, 40 + s : 41 + s, :] = table[8:9, at]
-            meta = jnp.where((row == 0) & (lane == s), fetch[p, s].astype(f32), meta)
-        send[p, META:ROWS, :] = meta
+            meta = jnp.where((row == 0) & (lane == s), fetch[s, p].astype(f32), meta)
+        send[p, META:MOMENTS, :] = meta
+        send[p, MOMENTS:ROWS, :] = moments
         return carry
 
     lax.fori_loop(0, send.shape[0], peer, 0)
@@ -90,17 +107,6 @@
     return [jnp.sum(s, axis=0, keepdims=True) for s in sums]
 
 
-def fold(acc, near):
-    lane = iota((SEG, SEG), 1)
-
-    def block(b, total):
-        for c in range(3):
-            total = jnp.where(lane == 4 * b + c, jnp.sum(acc[b, c], axis=1, keepdims=True), total)
-        return total
-
-    near[...] = -lax.fori_loop(0, acc.shape[0], block, jnp.zeros((SEG, SEG), f32)).T
-
-
 def clear(acc):
     def block(b, carry):
         acc[b] = jnp.zeros(acc.shape[1:], f32)
@@ -109,60 +115,45 @@
     lax.fori_loop(0, acc.shape[0], block, 0)
 
 
-def fill_columns(table, at, col):
-    turned = table[0:16, at].T
-    for c in range(9):
-        col(c, jnp.broadcast_to(turned[:, c : c + 1], (SEG, SEG)))
-
-
-def own_kernel(pairs, shift, box, count, off, tan, bur, near, table, column, acc, left_acc):
+def own_kernel(pairs, shift, box, count, off, tan, bur, columns, acc, left_acc, table):
     fill_table(table, off, tan, bur, 1.0, 1.0)
-    table[9:16, :] = jnp.zeros((7, table.shape[1]), f32)
     clear(acc)
     clear(left_acc)
+    blocks = acc.shape[0]
+
+    def block(b, carry):
+        at = lane_block(b)
+        for c in range(9):
+            columns[b, c] = jnp.broadcast_to(table[c : c + 1, at], (SEG, SEG)).T
+        return carry
+
+    lax.fori_loop(0, blocks, block, 0)
     row = iota((8, SEG), 0)
-    first = pairs.shape[1] - acc.shape[0]
+    scale = jnp.where(row < 3, 1.0, jnp.where(row < 6, 2.0 * KAPPA, KAPPA))
 
     def pair(k, carry):
         a, b = pairs[0, k], pairs[1, k]
-
-        def put(c, value):
-            column[c] = value
-
-        fill_columns(table, lane_block(b), put)
         at = lane_block(a)
-        scale = jnp.where(row < 3, 1.0, jnp.where(row < 6, 2.0 * KAPPA, KAPPA))
         head = table[0:8, at] * scale - shift_rows(shift_of(box, shift, k), (8, SEG))
         left = [head[i : i + 1, :] for i in range(8)] + [table[8:9, at] * KAPPA]
-        rows = tile(left, lambda c, r: column[c, 8 * r : 8 * r + 8, :], acc, b)
+        rows = tile(left, lambda c, r: columns[b, c, 8 * r : 8 * r + 8, :], acc, b)
         for c in range(3):
             left_acc[a, c : c + 1, :] += rows[c]
         return carry
 
-    lax.fori_loop(first, count[0], pair, 0)
-    fold(acc, near)
-    for b in range(acc.shape[0]):
-        near[4 * b : 4 * b + 3, :] += left_acc[b, 0:3, :]
-
-
-def pair_kernel(recv, off, tan, bur, ret, near, table, columns, acc, ids_vmem, ids, sem):
+    lax.fori_loop(pairs.shape[1] - blocks, count[0], pair, 0)
+
+
+def pair_kernel(recv, columns, _, left_acc, ret, near, moments, acc, ids_vmem, ids, sem):
     peers = recv.shape[0]
     for p in range(peers):
         ids_vmem[p : p + 1, :] = recv[p, META : META + 1, :].astype(jnp.int32)
     copy = pltpu.make_async_copy(ids_vmem, ids, sem)
     copy.start()
-    fill_table(table, off, tan, bur, 1.0, 1.0)
-    table[9:16, :] = jnp.zeros((7, table.shape[1]), f32)
-    clear(acc)
-
-    def block(b, carry):
-        def put(c, value):
-            columns[b, c] = value
-
-        fill_columns(table, lane_block(b), put)
-        return carry
-
-    lax.fori_loop(0, acc.shape[0], block, 0)
+    total = recv[0, MOMENTS:ROWS, :]
+    for p in range(1, peers):
+        total = total + recv[p, MOMENTS:ROWS, :]
+    moments[...] = total
     copy.wait()
 
     def peer(p, carry):
@@ -177,7 +168,17 @@
         return carry
 
     lax.fori_loop(0, peers, peer, 0)
-    fold(acc, near)
+
+    def fold(half, carry):
+        rows = []
+        for b in (2 * half, 2 * half + 1):
+            for c in range(3):
+                rows.append(left_acc[b, c : c + 1, :] - jnp.sum(acc[b, c].T, axis=0, keepdims=True))
+            rows.append(jnp.zeros((1, SEG), f32))
+        near[pl.ds(pl.multiple_of(8 * half, 8), 8), :] = jnp.concatenate(rows, axis=0)
+        return carry
+
+    lax.fori_loop(0, acc.shape[0] // 2, fold, 0)
 
 
 def fill_phi(phi, off):
@@ -205,7 +206,7 @@
     )
 
 
-def moment_kernel(cell, off, tan, bur, out, phi, charged):
+def cell_moments(cell, off, tan, bur, phi, charged):
     fill_phi(phi, off)
     charge = jnp.sum(bur[...] * tan[...], axis=0, keepdims=True)
     row = iota((CS, SEG), 0)
@@ -213,9 +214,7 @@
         part = charge[:, b * SEG : (b + 1) * SEG]
         charged[:, b * SEG : (b + 1) * SEG] = jnp.where(row == cell[b], part, 0.0)
     part = dot_nt(charged[...], phi[...], HIGH)
-    whole = jnp.concatenate([part, jnp.zeros((CS, SEG - NM), f32)], axis=1)
-    for p in range(out.shape[0]):
-        out[p] = whole
+    return jnp.concatenate([part, jnp.zeros((CS, SEG - NM), f32)], axis=1)
 
 
 def far_kernel_body(cell, stress, operator, off, tan, bur, *rest):
@@ -247,7 +246,7 @@
         out[:, at] += jnp.sum(mine, axis=0, keepdims=True) * bur[:, at]
 
 
-def final_kernel(pairs, back, near_own, near_pair, far, conn, out, left_acc, force, split):
+def final_kernel(pairs, back, near_all, far, conn, out, left_acc, force, split):
     clear(left_acc)
 
     def peer(p, carry):
@@ -259,7 +258,7 @@
     lax.fori_loop(0, back.shape[0], peer, 0)
     for b in range(left_acc.shape[0]):
         at = slice(b * SEG, (b + 1) * SEG)
-        near = near_own[4 * b : 4 * b + 3, :] + near_pair[4 * b : 4 * b + 3, :]
+        near = near_all[4 * b : 4 * b + 3, :]
         force[0:3, at] = 0.5 * (far[:, at] + near + left_acc[b, 0:3, :])
     value = force[0:3, :]
     high = value.astype(jnp.bfloat16).astype(f32)
@@ -286,13 +285,14 @@
             out[c : c + 1, g * SEG : (g + 1) * SEG] = whole[g : g + 1, :]
 
 
-def call(body, out_shape, in_specs, scratch, flops, size=48):
+def call(body, out_shape, in_specs, scratch, flops, size, aliases=None):
     return pl.pallas_call(
         body,
         out_shape=out_shape,
         in_specs=in_specs,
         out_specs=jax.tree.map(lambda _: VMEM, out_shape),
         scratch_shapes=scratch,
+        input_output_aliases=aliases or {},
         compiler_params=pltpu.CompilerParams(vmem_limit_bytes=size << 20),
         cost_estimate=pl.CostEstimate(flops=flops, bytes_accessed=1 << 20, transcendentals=0),
     )
@@ -318,53 +318,49 @@
     slabs = lax.axis_size("slab")
     shape = lambda *dims: jax.ShapeDtypeStruct(dims, f32)
     table = pltpu.VMEM((16, segs), f32)
-    acc = pltpu.VMEM((blocks, 3, SEG, SEG), f32)
-    left_acc = pltpu.VMEM((blocks, 8, SEG), f32)
-
+
+    raw = [pair_list, image_shift, box_matrix, fetch_table.T, block_cell]
+    segments = [seg_offset, tangent, burgers]
     send = call(
-        pack_kernel, shape(peers, ROWS, SEG), [SMEM] * 4 + [VMEM] * 3, [table], 10**6, 16
-    )(pair_list, image_shift, box_matrix, fetch_table, seg_offset, tangent, burgers)
+        pack_kernel,
+        shape(peers, ROWS, SEG),
+        [pl.BlockSpec(memory_space=pltpu.HBM)] * 8,
+        [pltpu.SMEM(x.shape, x.dtype) for x in raw]
+        + [pltpu.VMEM(x.shape, x.dtype) for x in segments]
+        + [pltpu.SemaphoreType.DMA((8,))]
+        + [table, pltpu.VMEM((NM, segs), f32), pltpu.VMEM((CS, segs), f32)],
+        10**6,
+        60,
+    )(*raw, *segments)
     recv = lax.all_to_all(send, "bulk", 0, 0, tiled=True)
 
-    moments_here = call(
-        moment_kernel,
-        shape(peers, CS, SEG),
-        [SMEM] + [VMEM] * 3,
-        [pltpu.VMEM((NM, segs), f32), pltpu.VMEM((CS, segs), f32)],
+    columns, acc, left_acc = call(
+        own_kernel,
+        (shape(blocks, 9, SEG, SEG), shape(blocks, 3, SEG, SEG), shape(blocks, 8, SEG)),
+        [SMEM] * 4 + [VMEM] * 3,
+        [table],
         10**9,
-        16,
-    )(block_cell, seg_offset, tangent, burgers)
-    moments = jnp.sum(lax.all_to_all(moments_here, "bulk", 0, 0, tiled=True), axis=0)
-    sources = [moments] + [
-        lax.ppermute(moments, "slab", [(s, (s + k) % slabs) for s in range(slabs)])
-        for k in range(1, slabs)
-    ]
-
-    near_own = call(
-        own_kernel,
-        shape(SEG, SEG),
-        [SMEM] * 4 + [VMEM] * 3,
-        [table, pltpu.VMEM((9, SEG, SEG), f32), acc, left_acc],
-        10**9,
-        24,
-    )(pair_list, image_shift, box_matrix, pair_count, seg_offset, tangent, burgers)
-
-    ret, near_pair = call(
+        8,
+    )(pair_list, image_shift, box_matrix, pair_count, *segments)
+
+    ret, near, moments, _ = call(
         pair_kernel,
-        (shape(peers, 16, SEG), shape(SEG, SEG)),
+        (shape(peers, 16, SEG), shape(SEG, SEG), shape(CS, SEG), shape(blocks, 3, SEG, SEG)),
         [VMEM] * 4,
         [
-            table,
-            pltpu.VMEM((blocks, 9, SEG, SEG), f32),
-            acc,
             pltpu.VMEM((peers, SEG), jnp.int32),
             pltpu.SMEM((peers, SEG), jnp.int32),
             pltpu.SemaphoreType.DMA,
         ],
         10**10,
-        40,
-    )(recv, seg_offset, tangent, burgers)
+        8,
+        {2: 3},
+    )(recv, columns, acc, left_acc)
     back = lax.all_to_all(ret, "bulk", 0, 0, tiled=True)
+    sources = [moments] + [
+        lax.ppermute(moments, "slab", [(s, (s + k) % slabs) for s in range(slabs)])
+        for k in range(1, slabs)
+    ]
 
     far = call(
         far_kernel_body,
@@ -383,11 +379,11 @@
     return call(
         final_kernel,
         shape(3, segs),
-        [SMEM] + [VMEM] * 5,
-        [left_acc, pltpu.VMEM((8, segs), f32), pltpu.VMEM((8, segs), f32)],
+        [SMEM] + [VMEM] * 4,
+        [pltpu.VMEM((blocks, 8, SEG), f32), pltpu.VMEM((8, segs), f32), pltpu.VMEM((8, segs), f32)],
         10**9,
         24,
-    )(pair_list, back, near_own, near_pair, far, node_conn)
+    )(pair_list, back, near, far, node_conn)
 
 
 def solution(mesh):

time: 125 us -> 102 us (0.82)
  the two profiles are of different devices: /device:TPU:105 before, /device:TPU:1 now
where the time goes in v2:
time: 102 us
  Pallas kernels  40.3 us (40%)
  starting transfers between devices  31.1 us (30%)
  local copies, waits for them, and re-layouts  24.9 us (24%)
  waiting for transfers between devices  5.03 us (5%)
    unnamed x36, local copies, waits for them, and re-layouts  24.9 us
    pallas_call x1, Pallas kernels, local(): call(pair_kernel, (shape(peers, 16, SEG), shape(SEG, SEG), shape(CS, SEG)...  16.6 us
    all_to_all x1, starting transfers between devices, local(): recv = lax.all_to_all(send, 'bulk', 0, 0, tiled=True)  12 us
    ppermute x7, starting transfers between devices, local(): lax.ppermute(moments, 'slab', [(s, (s + k) % slabs) for s in range(slabs)])  10.2 us
    pallas_call x1, Pallas kernels, local(): call(own_kernel, (shape(blocks, 9, SEG, SEG), shape(blocks, 3, SEG, SEG),...  8.96 us
    all_to_all x1, starting transfers between devices, local(): back = lax.all_to_all(ret, 'bulk', 0, 0, tiled=True)  8.83 us
    pallas_call x1, Pallas kernels, local(): call(pack_kernel, shape(peers, ROWS, SEG), [pl.BlockSpec(memory_space=plt...  5.81 us
    pallas_call x1, Pallas kernels, local(): call(far_kernel_body, shape(3, segs), [SMEM] * 2 + [VMEM] * (4 + slabs),...  5.56 us
  transfers between devices with their start and end apart: 9, of which 3 were waited for; matrix products, arithmetic and copies ran while one was open for 0% of the time, Pallas kernels for 14%

profile of v2, /device:TPU:1, one launch (start us, length us, event | category | flops | bytes accessed | tf_op | source)
XLA Modules:
  0.0 102.1 jit_solution(1701137375358726017)
XLA Ops:
  0.0 5.8 %shard_map.118 = f32[32,64,128]{2,1,0:T(8,128)} custom-call(s32[2,192]{1,0:T(2,128)} %pairs.3, s32[3,192]{1,0:T(4,128)} %shift.1, f32[3,3]{1,0:T(4,128)} %box.1, s32[5,32]{1,0:T(8,128)} %bitcast.1, s32[32]{0:T(128)} %cell.1, f32[3,4096]{1,0:T(4,128)} %off.3, f32[3,4096]{1,0:T(4,128)} %tan.3, f32[3,4096]{1,0:T(4,128)} %bur.3), custom_call_target="tpu_custom_call" | custom-call | flops 1000000 | bytes 1048576 | tf_op jit(solution)/shard_map/pallas_call | solution.py:324
  5.8 12.0 %all-to-all-start = ((f32[32,64,128]{2,1,0:T(8,128)}), f32[32,64,128]{2,1,0:T(8,128)S(1)}, u32[]{:S(2)}, u32[]{:S(2)}) async-start(f32[32,64,128]{2,1,0:T(8,128)} %shard_map.118), calls=%async_computation | async-start | bytes 2097152 | tf_op jit(solution)/shard_map/all_to_all | solution.py:335
  18.5 0.8 copy-done.1
  19.4 0.8 copy-done.3
  20.2 0.8 copy-done.5
  21.0 0.7 copy-done.7
  22.4 0.7 copy-done.10
  23.1 9.0 %shard_map.119 = (f32[32,9,128,128]{3,2,1,0:T(8,128)S(1)}, f32[32,3,128,128]{3,2,1,0:T(8,128)S(1)}, f32[32,8,128]{2,1,0:T(8,128)S(1)}) custom-call(s32[2,192]{1,0:T(2,128)S(1)} %copy-done.10, s32[3,192]{1,0:T(4,128)S(1)} %copy-done.7, f32[3,3]{1,0:T(4,128)S(1)} %copy-done.8, s32[1]{0:T(128)S(6)} %copy.15.count, f32[3,4096]{1,0:T(4,128)S(1)} %copy-done.1, ...), custom_call_target="tpu_custom_call" | custom-call | flops 1000000000 | bytes 1048576 | tf_op jit(solution)/shard_map/pallas_call | solution.py:337
  32.1 6.4 %copy-done.14 = f32[32,9,128,128]{3,2,1,0:T(8,128)} copy-done((f32[32,9,128,128]{3,2,1,0:T(8,128)}, f32[32,9,128,128]{3,2,1,0:T(8,128)S(1)}, u32[]{:S(2)}) %copy-start.14) | copy-done | bytes 18874392
  38.5 2.6 %copy-done.16 = f32[32,3,128,128]{3,2,1,0:T(8,128)} copy-done((f32[32,3,128,128]{3,2,1,0:T(8,128)}, f32[32,3,128,128]{3,2,1,0:T(8,128)S(1)}, u32[]{:S(2)}) %copy-start.16) | copy-done | bytes 6291480
  41.1 1.4 %all-to-all-done.recv = f32[32,64,128]{2,1,0:T(8,128)S(1)} async-done(((f32[32,64,128]{2,1,0:T(8,128)}), f32[32,64,128]{2,1,0:T(8,128)S(1)}, u32[]{:S(2)}, u32[]{:S(2)}) %all-to-all-start) | async-done | bytes 1048608 | tf_op jit(solution)/shard_map/all_to_all | solution.py:335
  42.5 6.4 %copy-done.15 = f32[32,9,128,128]{3,2,1,0:T(8,128)S(1)} copy-done((f32[32,9,128,128]{3,2,1,0:T(8,128)S(1)}, f32[32,9,128,128]{3,2,1,0:T(8,128)}, u32[]{:S(2)}) %copy-start.15) | copy-done | bytes 18874392
  48.9 2.8 %copy-done.17 = f32[32,3,128,128]{3,2,1,0:T(8,128)S(1)} copy-done((f32[32,3,128,128]{3,2,1,0:T(8,128)S(1)}, f32[32,3,128,128]{3,2,1,0:T(8,128)}, u32[]{:S(2)}) %copy-start.17) | copy-done | bytes 6291480
  51.7 16.6 %shard_map.120 = (f32[32,16,128]{2,1,0:T(8,128)}, f32[128,128]{1,0:T(8,128)S(1)}, f32[16,128]{1,0:T(8,128)S(1)}, f32[32,3,128,128]{3,2,1,0:T(8,128)S(1)}) custom-call(f32[32,64,128]{2,1,0:T(8,128)S(1)} %all-to-all-done.recv, f32[32,9,128,128]{3,2,1,0:T(8,128)S(1)} %copy-done.15, f32[32,3,128,128]{3,2,1,0:T(8,128)S(1)} %copy-done.17, ...), custom_call_target="tpu_custom_call", output_to_operand_aliasing={{3}: (2, {})} | custom-call | flops 10000000000 | bytes 1048576 | tf_op jit(solution)/shard_map/pallas_call | solution.py:346
  68.3 8.8 %all-to-all-start.1 = ((f32[32,16,128]{2,1,0:T(8,128)}), f32[32,16,128]{2,1,0:T(8,128)S(1)}, u32[]{:S(2)}, u32[]{:S(2)}) async-start(f32[32,16,128]{2,1,0:T(8,128)} %get-tuple-element.14), calls=%async_computation.1 | async-start | bytes 524288 | tf_op jit(solution)/shard_map/all_to_all | solution.py:359
  77.2 2.4 %collective-permute-start.6 = (f32[16,128]{1,0:T(8,128)S(1)}, f32[16,128]{1,0:T(8,128)S(1)}, u32[]{:S(2)}, u32[]{:S(2)}) collective-permute-start(f32[16,128]{1,0:T(8,128)S(1)} %get-tuple-element.16.rest_0_), channel_id=1, source_target_pairs={{0,224},{32,0},{64,32},{96,64},{128,96},{160,128},{192,160},{224,1... | collective-permute-start | bytes 24584 | tf_op jit(solution)/shard_map/ppermute | solution.py:361
  79.6 2.0 %collective-permute-start.5 = (f32[16,128]{1,0:T(8,128)S(1)}, f32[16,128]{1,0:T(8,128)S(1)}, u32[]{:S(2)}, u32[]{:S(2)}) collective-permute-start(f32[16,128]{1,0:T(8,128)S(1)} %get-tuple-element.16.rest_0_), channel_id=1, source_target_pairs={{0,192},{32,224},{64,0},{96,32},{128,64},{160,96},{192,128},{224,1... | collective-permute-start | bytes 24584 | tf_op jit(solution)/shard_map/ppermute | solution.py:361
  81.8 3.6 %collective-permute-start.3 = (f32[16,128]{1,0:T(8,128)S(1)}, f32[16,128]{1,0:T(8,128)S(1)}, u32[]{:S(2)}, u32[]{:S(2)}) collective-permute-start(f32[16,128]{1,0:T(8,128)S(1)} %get-tuple-element.16.rest_0_), channel_id=1, source_target_pairs={{0,128},{32,160},{64,192},{96,224},{128,0},{160,32},{192,64},{224,... | collective-permute-start | bytes 24584 | tf_op jit(solution)/shard_map/ppermute | solution.py:361
  85.4 2.0 %collective-permute-start.2 = (f32[16,128]{1,0:T(8,128)S(1)}, f32[16,128]{1,0:T(8,128)S(1)}, u32[]{:S(2)}, u32[]{:S(2)}) collective-permute-start(f32[16,128]{1,0:T(8,128)S(1)} %get-tuple-element.16.rest_0_), channel_id=1, source_target_pairs={{0,96},{32,128},{64,160},{96,192},{128,224},{160,0},{192,32},{224,... | collective-permute-start | bytes 24584 | tf_op jit(solution)/shard_map/ppermute | solution.py:361
  87.4 2.5 %collective-permute-done.2.rest_3_ = f32[16,128]{1,0:T(8,128)S(1)} collective-permute-done((f32[16,128]{1,0:T(8,128)S(1)}, f32[16,128]{1,0:T(8,128)S(1)}, u32[]{:S(2)}, u32[]{:S(2)}) %collective-permute-start.2) | collective-permute-done | bytes 8224 | tf_op jit(solution)/shard_map/ppermute | solution.py:361
  89.9 1.1 %collective-permute-done.1.rest_2_ = f32[16,128]{1,0:T(8,128)S(1)} collective-permute-done((f32[16,128]{1,0:T(8,128)S(1)}, f32[16,128]{1,0:T(8,128)S(1)}, u32[]{:S(2)}, u32[]{:S(2)}) %collective-permute-start.1) | collective-permute-done | bytes 8224 | tf_op jit(solution)/shard_map/ppermute | solution.py:361
  91.1 2.1 %copy-done = f32[84,10752]{1,0:T(8,128)S(1)} copy-done((f32[84,10752]{1,0:T(8,128)S(1)}, f32[84,10752]{1,0:T(8,128)}, u32[]{:S(2)}) %copy-start) | copy-done | bytes 3612696
  93.2 5.6 %shard_map.121.far = f32[3,4096]{1,0:T(4,128)S(1)} custom-call(s32[32]{0:T(128)S(1)} %copy-done.12, f32[3,3]{1,0:T(4,128)S(1)} %copy-done.9, f32[84,10752]{1,0:T(8,128)S(1)} %copy-done, f32[3,4096]{1,0:T(4,128)S(1)} %copy-done.2, f32[3,4096]{1,0:T(4,128)S(1)} %copy-done.4, f32[3,4096]{1,0:T(4,128)S(1)} %copy-done.6, ...), custom_call_target="tpu_custom_call" | custom-call | flops 1000000000 | bytes 1048576 | tf_op jit(solution)/shard_map/pallas_call | solution.py:365
  98.8 3.3 %shard_map.122 = f32[3,4096]{1,0:T(4,128)} custom-call(s32[2,192]{1,0:T(2,128)S(1)} %copy-done.11, f32[32,16,128]{2,1,0:T(8,128)S(1)} %all-to-all-done.1.back, f32[128,128]{1,0:T(8,128)S(1)} %get-tuple-element.15.near_all, f32[3,4096]{1,0:T(4,128)S(1)} %shard_map.121.far, s32[2,4096]{1,0:T(2,128)S(1)} %copy-done.13), custom_call_target="tpu_custom_call" | custom-call | flops 1000000000 | bytes 1048576 | tf_op jit(solution)/shard_map/pallas_call | solution.py:379
  (35 shorter events, 0.9 us)
Async XLA Ops:
  5.8 36.7 %all-to-all-start = ((f32[32,64,128]{2,1,0:T(8,128)}), f32[32,64,128]{2,1,0:T(8,128)S(1)}, u32[]{:S(2)}, u32[]{:S(2)}) async-start(f32[32,64,128]{2,1,0:T(8,128)} %shard_map.118), calls=%async_computation | async-start | bytes 2097152 | tf_op jit(solution)/shard_map/all_to_all | solution.py:335
  18.5 0.8 copy-start.1
  19.4 0.8 copy-start.3
  20.2 0.8 copy-start.5
  32.1 6.4 %copy-start.14 = (f32[32,9,128,128]{3,2,1,0:T(8,128)}, f32[32,9,128,128]{3,2,1,0:T(8,128)S(1)}, u32[]{:S(2)}) copy-start(f32[32,9,128,128]{3,2,1,0:T(8,128)S(1)} %get-tuple-element.11.columns) | copy-start | bytes 56623108
  38.5 2.6 %copy-start.16 = (f32[32,3,128,128]{3,2,1,0:T(8,128)}, f32[32,3,128,128]{3,2,1,0:T(8,128)S(1)}, u32[]{:S(2)}) copy-start(f32[32,3,128,128]{3,2,1,0:T(8,128)S(1)} %get-tuple-element.12._) | copy-start | bytes 18874372
  42.5 6.4 %copy-start.15 = (f32[32,9,128,128]{3,2,1,0:T(8,128)S(1)}, f32[32,9,128,128]{3,2,1,0:T(8,128)}, u32[]{:S(2)}) copy-start(f32[32,9,128,128]{3,2,1,0:T(8,128)} %copy-done.14) | copy-start | bytes 56623108
  48.9 2.8 %copy-start.17 = (f32[32,3,128,128]{3,2,1,0:T(8,128)S(1)}, f32[32,3,128,128]{3,2,1,0:T(8,128)}, u32[]{:S(2)}) copy-start(f32[32,3,128,128]{3,2,1,0:T(8,128)} %copy-done.16) | copy-start | bytes 18874372
  51.6 39.4 %copy-start.2 = (f32[3,4096]{1,0:T(4,128)S(1)}, f32[3,4096]{1,0:T(4,128)}, u32[]{:S(2)}) copy-start(f32[3,4096]{1,0:T(4,128)} %off.3) | copy-start | bytes 147460
  51.7 39.4 %copy-start.4 = (f32[3,4096]{1,0:T(4,128)S(1)}, f32[3,4096]{1,0:T(4,128)}, u32[]{:S(2)}) copy-start(f32[3,4096]{1,0:T(4,128)} %tan.3) | copy-start | bytes 147460
  51.7 39.4 %copy-start.6 = (f32[3,4096]{1,0:T(4,128)S(1)}, f32[3,4096]{1,0:T(4,128)}, u32[]{:S(2)}) copy-start(f32[3,4096]{1,0:T(4,128)} %bur.3) | copy-start | bytes 147460
  51.7 39.5 %copy-start.9 = (f32[3,3]{1,0:T(4,128)S(1)}, f32[3,3]{1,0:T(4,128)}, u32[]{:S(2)}) copy-start(f32[3,3]{1,0:T(4,128)} %stress.1) | copy-start | bytes 112
  51.7 39.5 %copy-start.12 = (s32[32]{0:T(128)S(1)}, s32[32]{0:T(128)}, u32[]{:S(2)}) copy-start(s32[32]{0:T(128)} %cell.1) | copy-start | bytes 388
  51.7 47.1 %copy-start.11 = (s32[2,192]{1,0:T(2,128)S(1)}, s32[2,192]{1,0:T(2,128)}, u32[]{:S(2)}) copy-start(s32[2,192]{1,0:T(2,128)} %pairs.3) | copy-start | bytes 4612
  51.7 47.1 %copy-start.13 = (s32[2,4096]{1,0:T(2,128)S(1)}, s32[2,4096]{1,0:T(2,128)}, u32[]{:S(2)}) copy-start(s32[2,4096]{1,0:T(2,128)} %conn.1) | copy-start | bytes 98308
  68.3 30.4 %all-to-all-start.1 = ((f32[32,16,128]{2,1,0:T(8,128)}), f32[32,16,128]{2,1,0:T(8,128)S(1)}, u32[]{:S(2)}, u32[]{:S(2)}) async-start(f32[32,16,128]{2,1,0:T(8,128)} %get-tuple-element.14), calls=%async_computation.1 | async-start | bytes 524288 | tf_op jit(solution)/shard_map/all_to_all | solution.py:359
  77.2 10.2 %collective-permute-start.6 = (f32[16,128]{1,0:T(8,128)S(1)}, f32[16,128]{1,0:T(8,128)S(1)}, u32[]{:S(2)}, u32[]{:S(2)}) collective-permute-start(f32[16,128]{1,0:T(8,128)S(1)} %get-tuple-element.16.rest_0_), channel_id=1, source_target_pairs={{0,224},{32,0},{64,32},{96,64},{128,96},{160,128},{192,160},{224,1... | collective-permute-start | bytes 24584 | tf_op jit(solution)/shard_map/ppermute | solution.py:361
  79.6 7.8 %collective-permute-start.5 = (f32[16,128]{1,0:T(8,128)S(1)}, f32[16,128]{1,0:T(8,128)S(1)}, u32[]{:S(2)}, u32[]{:S(2)}) collective-permute-start(f32[16,128]{1,0:T(8,128)S(1)} %get-tuple-element.16.rest_0_), channel_id=1, source_target_pairs={{0,192},{32,224},{64,0},{96,32},{128,64},{160,96},{192,128},{224,1... | collective-permute-start | bytes 24584 | tf_op jit(solution)/shard_map/ppermute | solution.py:361
  81.6 5.8 %collective-permute-start.4 = (f32[16,128]{1,0:T(8,128)S(1)}, f32[16,128]{1,0:T(8,128)S(1)}, u32[]{:S(2)}, u32[]{:S(2)}) collective-permute-start(f32[16,128]{1,0:T(8,128)S(1)} %get-tuple-element.16.rest_0_), channel_id=1, source_target_pairs={{0,160},{32,192},{64,224},{96,0},{128,32},{160,64},{192,96},{224,1... | collective-permute-start | bytes 24584 | tf_op jit(solution)/shard_map/ppermute | solution.py:361
  81.8 5.6 %collective-permute-start.3 = (f32[16,128]{1,0:T(8,128)S(1)}, f32[16,128]{1,0:T(8,128)S(1)}, u32[]{:S(2)}, u32[]{:S(2)}) collective-permute-start(f32[16,128]{1,0:T(8,128)S(1)} %get-tuple-element.16.rest_0_), channel_id=1, source_target_pairs={{0,128},{32,160},{64,192},{96,224},{128,0},{160,32},{192,64},{224,... | collective-permute-start | bytes 24584 | tf_op jit(solution)/shard_map/ppermute | solution.py:361
  85.4 4.6 %collective-permute-start.2 = (f32[16,128]{1,0:T(8,128)S(1)}, f32[16,128]{1,0:T(8,128)S(1)}, u32[]{:S(2)}, u32[]{:S(2)}) collective-permute-start(f32[16,128]{1,0:T(8,128)S(1)} %get-tuple-element.16.rest_0_), channel_id=1, source_target_pairs={{0,96},{32,128},{64,160},{96,192},{128,224},{160,0},{192,32},{224,... | collective-permute-start | bytes 24584 | tf_op jit(solution)/shard_map/ppermute | solution.py:361
  87.4 3.7 %collective-permute-start.1 = (f32[16,128]{1,0:T(8,128)S(1)}, f32[16,128]{1,0:T(8,128)S(1)}, u32[]{:S(2)}, u32[]{:S(2)}) collective-permute-start(f32[16,128]{1,0:T(8,128)S(1)} %get-tuple-element.16.rest_0_), channel_id=1, source_target_pairs={{0,64},{32,96},{64,128},{96,160},{128,192},{160,224},{192,0},{224,... | collective-permute-start | bytes 24584 | tf_op jit(solution)/shard_map/ppermute | solution.py:361
  87.4 3.7 %collective-permute-start = (f32[16,128]{1,0:T(8,128)S(1)}, f32[16,128]{1,0:T(8,128)S(1)}, u32[]{:S(2)}, u32[]{:S(2)}) collective-permute-start(f32[16,128]{1,0:T(8,128)S(1)} %get-tuple-element.16.rest_0_), channel_id=1, source_target_pairs={{0,32},{32,64},{64,96},{96,128},{128,160},{160,192},{192,224},{224... | collective-permute-start | bytes 24584 | tf_op jit(solution)/shard_map/ppermute | solution.py:361
  91.1 2.1 %copy-start = (f32[84,10752]{1,0:T(8,128)S(1)}, f32[84,10752]{1,0:T(8,128)}, u32[]{:S(2)}) copy-start(f32[84,10752]{1,0:T(8,128)} %operator.1) | copy-start | bytes 10838020
  (3 other events, 2.0 us)

commit v3 on v2

--- a/solution.py
+++ b/solution.py
@@ -2,7 +2,6 @@
 
 import jax
 import jax.numpy as jnp
-import numpy as np
 from jax import lax
 from jax.experimental import pallas as pl
 from jax.experimental.pallas import tpu as pltpu
@@ -15,12 +14,15 @@
 META = 45
 MOMENTS = 48
 ROWS = MOMENTS + CS
+FEATURES = 48
 KAPPA = 0.2
 CORE_SQ = 0.25
 HIGH = lax.Precision.HIGHEST
 VMEM = pl.BlockSpec(memory_space=pltpu.VMEM)
+HBM = pl.BlockSpec(memory_space=pltpu.HBM)
 SMEM = pl.BlockSpec(memory_space=pltpu.SMEM)
 f32 = jnp.float32
+bf16 = jnp.bfloat16
 
 
 def exponents():
@@ -90,21 +92,85 @@
     lax.fori_loop(0, send.shape[0], peer, 0)
 
 
-def tile(left, col, acc, b):
+def split(value):
+    high = value.astype(bf16).astype(f32)
+    rest = value - high
+    mid = rest.astype(bf16).astype(f32)
+    return high, mid, (rest - mid).astype(bf16).astype(f32)
+
+
+def fill_features(table, features):
+    row = iota((8, SEG), 0)
+    first = row < 3
+
+    def block(b, carry):
+        at = lane_block(b)
+        high, mid, low = split(table[0:8, at])
+        last_high, last_mid, _ = split(table[8:9, at])
+        groups = [jnp.where(first, 1.0, high)] * 2
+        groups.append(
+            jnp.where(first, 1.0, jnp.where(row < 5, last_high, jnp.where(row == 5, last_mid, 0.0)))
+        )
+        groups.append(jnp.where(first, high, mid))
+        groups.append(jnp.concatenate([mid[0:3], low[0:3], jnp.zeros((2, SEG), f32)], axis=0))
+        groups.append(jnp.zeros((SEG - 40, SEG), f32))
+        turned = jnp.concatenate(groups, axis=0).T
+        features[b] = turned[:, 0:FEATURES].astype(bf16)
+        return carry
+
+    lax.fori_loop(0, features.shape[0], block, 0)
+
+
+def weights(head, last):
+    row = iota((8, SEG), 0)
+    high, mid, low = split(head)
+    last_high, last_mid, _ = split(last)
+    none = jnp.zeros((8, SEG), f32)
+    columns = []
+    for i in range(3):
+        own = row == i
+        parts = [jnp.where(own, part, 0.0) for part in (high, mid, low, -1.0)]
+        parts += [jnp.where(own | (row == i + 3), -1.0, 0.0), none]
+        columns.append(jnp.concatenate(parts, axis=0))
+    tail = row >= 3
+    high = jnp.where(tail, high, 0.0)
+    edge = jnp.where((row == 3) | (row == 5), last_high, jnp.where(row == 4, last_mid, 0.0))
+    columns.append(
+        jnp.concatenate([high, jnp.where(tail, mid, 0.0), edge, high, none, none], axis=0)
+    )
+    return jnp.concatenate(columns, axis=1).astype(bf16)
+
+
+def tile(head, last, features, acc, b):
+    both = weights(head, last)
     sums = [jnp.zeros((8, SEG), f32) for _ in range(3)]
-    for r in range(SEG // 8):
-        gap = [left[c] - col(c, r) for c in range(3)]
+    step = 32
+    for start in range(0, SEG, step):
+        at = slice(start, start + step)
+        made = jnp.dot(features[b, at, :], both, preferred_element_type=f32)
+        gap = [made[:, i * SEG : (i + 1) * SEG] for i in range(3)]
         dist = gap[0] * gap[0] + CORE_SQ + gap[1] * gap[1] + gap[2] * gap[2]
-        coupling = left[3] * col(3, r)
-        for c in range(4, 9):
-            coupling = coupling + left[c] * col(c, r)
         inv = lax.rsqrt(dist)
-        weight = coupling * (inv * inv * inv)
+        weight = made[:, 3 * SEG :] * (inv * inv * inv)
         for c in range(3):
             push = weight * gap[c]
-            acc[b, c, 8 * r : 8 * r + 8, :] += push
-            sums[c] = sums[c] + push
-    return [jnp.sum(s, axis=0, keepdims=True) for s in sums]
+            acc[b, c, at, :] += push
+            for r in range(0, step, 8):
+                sums[c] = sums[c] + push[r : r + 8]
+    return [jnp.sum(part, axis=0, keepdims=True) for part in sums]
+
+
+def fold(acc, near, others):
+    def pair(half, carry):
+        at = pl.ds(pl.multiple_of(8 * half, 8), 8)
+        rows = []
+        for b in (2 * half, 2 * half + 1):
+            rows += [jnp.sum(acc[b, c].T, axis=0, keepdims=True) for c in range(3)]
+            rows.append(jnp.zeros((1, SEG), f32))
+        near[at, :] = others[at, :] - jnp.concatenate(rows, axis=0)
+        return carry
+
+    lax.fori_loop(0, acc.shape[0] // 2, pair, 0)
 
 
 def clear(acc):
@@ -115,19 +181,17 @@
     lax.fori_loop(0, acc.shape[0], block, 0)
 
 
-def own_kernel(pairs, shift, box, count, off, tan, bur, columns, acc, left_acc, table):
+def own_kernel(*refs):
+    sources, (features, near), scratch = refs[:7], refs[7:9], refs[9:]
+    pairs, shift, box, count, off, tan, bur, sems, table, acc, left_acc = scratch
+    copies = fetch_all(sources, scratch[:7], sems)
+    clear(acc)
+    left_acc[...] = jnp.zeros_like(left_acc)
+    for copy in copies:
+        copy.wait()
     fill_table(table, off, tan, bur, 1.0, 1.0)
-    clear(acc)
-    clear(left_acc)
+    fill_features(table, features)
     blocks = acc.shape[0]
-
-    def block(b, carry):
-        at = lane_block(b)
-        for c in range(9):
-            columns[b, c] = jnp.broadcast_to(table[c : c + 1, at], (SEG, SEG)).T
-        return carry
-
-    lax.fori_loop(0, blocks, block, 0)
     row = iota((8, SEG), 0)
     scale = jnp.where(row < 3, 1.0, jnp.where(row < 6, 2.0 * KAPPA, KAPPA))
 
@@ -135,50 +199,37 @@
         a, b = pairs[0, k], pairs[1, k]
         at = lane_block(a)
         head = table[0:8, at] * scale - shift_rows(shift_of(box, shift, k), (8, SEG))
-        left = [head[i : i + 1, :] for i in range(8)] + [table[8:9, at] * KAPPA]
-        rows = tile(left, lambda c, r: columns[b, c, 8 * r : 8 * r + 8, :], acc, b)
+        rows = tile(head, table[8:9, at] * KAPPA, features, acc, b)
         for c in range(3):
             left_acc[a, c : c + 1, :] += rows[c]
         return carry
 
     lax.fori_loop(pairs.shape[1] - blocks, count[0], pair, 0)
-
-
-def pair_kernel(recv, columns, _, left_acc, ret, near, moments, acc, ids_vmem, ids, sem):
+    for b in range(blocks):
+        near[4 * b : 4 * b + 4, :] = left_acc[b, 0:4, :]
+    fold(acc, near, near)
+
+
+def pair_kernel(recv, features, near_own, ret, near, acc, ids_vmem, ids, sem):
     peers = recv.shape[0]
     for p in range(peers):
         ids_vmem[p : p + 1, :] = recv[p, META : META + 1, :].astype(jnp.int32)
     copy = pltpu.make_async_copy(ids_vmem, ids, sem)
     copy.start()
-    total = recv[0, MOMENTS:ROWS, :]
-    for p in range(1, peers):
-        total = total + recv[p, MOMENTS:ROWS, :]
-    moments[...] = total
+    clear(acc)
     copy.wait()
 
     def peer(p, carry):
         for s in range(SEND):
-            b = ids[p, s]
-            left = [recv[p, 8 * s + i : 8 * s + i + 1, :] for i in range(8)]
-            left.append(recv[p, 40 + s : 41 + s, :])
-            rows = tile(left, lambda c, r: columns[b, c, 8 * r : 8 * r + 8, :], acc, b)
+            head, last = recv[p, 8 * s : 8 * s + 8, :], recv[p, 40 + s : 41 + s, :]
+            rows = tile(head, last, features, acc, ids[p, s])
             for c in range(3):
                 ret[p, 3 * s + c : 3 * s + c + 1, :] = rows[c]
         ret[p, 15:16, :] = jnp.zeros((1, SEG), f32)
         return carry
 
     lax.fori_loop(0, peers, peer, 0)
-
-    def fold(half, carry):
-        rows = []
-        for b in (2 * half, 2 * half + 1):
-            for c in range(3):
-                rows.append(left_acc[b, c : c + 1, :] - jnp.sum(acc[b, c].T, axis=0, keepdims=True))
-            rows.append(jnp.zeros((1, SEG), f32))
-        near[pl.ds(pl.multiple_of(8 * half, 8), 8), :] = jnp.concatenate(rows, axis=0)
-        return carry
-
-    lax.fori_loop(0, acc.shape[0] // 2, fold, 0)
+    fold(acc, near, near_own)
 
 
 def fill_phi(phi, off):
@@ -217,9 +268,10 @@
     return jnp.concatenate([part, jnp.zeros((CS, SEG - NM), f32)], axis=1)
 
 
-def far_kernel_body(cell, stress, operator, off, tan, bur, *rest):
-    count = len(rest) - 5
-    sources, (out, around, shifted, phi, pots) = rest[:count], rest[count:]
+def far_kernel_body(count, *refs):
+    raw, sources, out, scratch = refs[:6], refs[6 : 6 + count], refs[6 + count], refs[7 + count :]
+    cell, stress, off, tan, bur, operator, sems, around, shifted, phi, pots = scratch
+    copies = fetch_all(raw, scratch[:6], sems)
     cells = count * CS
     for q in range(count):
         around[q * CS : (q + 1) * CS, :] = sources[(count - q) % count][...]
@@ -227,8 +279,11 @@
     shifted[:, 0:NM] = jnp.zeros((CS, NM), f32)
     for o in range(1, cells):
         shifted[:, o * NM : (o + 1) * NM] = around[cells - o : cells - o + CS, 0:NM]
+    for copy in copies[:5]:
+        copy.wait()
+    fill_phi(phi, off)
+    copies[5].wait()
     local_exp = dot_nt(shifted[...], operator[...], HIGH)
-    fill_phi(phi, off)
     pots[...] = lax.dot_general(
         local_exp, phi[...], (((1,), (0,)), ((), ())), precision=HIGH, preferred_element_type=f32
     )
@@ -246,7 +301,7 @@
         out[:, at] += jnp.sum(mine, axis=0, keepdims=True) * bur[:, at]
 
 
-def final_kernel(pairs, back, near_all, far, conn, out, left_acc, force, split):
+def final_kernel(pairs, back, near_all, far, conn, out, left_acc, force, halves):
     clear(left_acc)
 
     def peer(p, carry):
@@ -261,9 +316,9 @@
         near = near_all[4 * b : 4 * b + 3, :]
         force[0:3, at] = 0.5 * (far[:, at] + near + left_acc[b, 0:3, :])
     value = force[0:3, :]
-    high = value.astype(jnp.bfloat16).astype(f32)
-    split[0:3, :] = high
-    split[3:6, :] = value - high
+    high = value.astype(bf16).astype(f32)
+    halves[0:3, :] = high
+    halves[3:6, :] = value - high
     chunk = 1024
     segs = conn.shape[1]
     groups = segs // SEG
@@ -273,10 +328,10 @@
         for start in range(0, segs, chunk):
             at = slice(start, start + chunk)
             node = conn[end : end + 1, at]
-            low = jnp.where(low_row == (node & (SEG - 1)), 1.0, 0.0).astype(jnp.bfloat16)
+            low = jnp.where(low_row == (node & (SEG - 1)), 1.0, 0.0).astype(bf16)
             mark = high_row == (node >> 7)
             parts = [
-                jnp.where(mark, split[i : i + 1, at], 0.0).astype(jnp.bfloat16) for i in range(6)
+                jnp.where(mark, halves[i : i + 1, at], 0.0).astype(bf16) for i in range(6)
             ]
             total = total + dot_nt(jnp.concatenate(parts, axis=0), low)
     for c in range(3):
@@ -285,14 +340,13 @@
             out[c : c + 1, g * SEG : (g + 1) * SEG] = whole[g : g + 1, :]
 
 
-def call(body, out_shape, in_specs, scratch, flops, size, aliases=None):
+def call(body, out_shape, in_specs, scratch, flops, size):
     return pl.pallas_call(
         body,
         out_shape=out_shape,
         in_specs=in_specs,
         out_specs=jax.tree.map(lambda _: VMEM, out_shape),
         scratch_shapes=scratch,
-        input_output_aliases=aliases or {},
         compiler_params=pltpu.CompilerParams(vmem_limit_bytes=size << 20),
         cost_estimate=pl.CostEstimate(flops=flops, bytes_accessed=1 << 20, transcendentals=0),
     )
@@ -324,7 +378,7 @@
     send = call(
         pack_kernel,
         shape(peers, ROWS, SEG),
-        [pl.BlockSpec(memory_space=pltpu.HBM)] * 8,
+        [HBM] * 8,
         [pltpu.SMEM(x.shape, x.dtype) for x in raw]
         + [pltpu.VMEM(x.shape, x.dtype) for x in segments]
         + [pltpu.SemaphoreType.DMA((8,))]
@@ -334,47 +388,56 @@
     )(*raw, *segments)
     recv = lax.all_to_all(send, "bulk", 0, 0, tiled=True)
 
-    columns, acc, left_acc = call(
+    raw = [pair_list, image_shift, box_matrix, pair_count]
+    features, near_own = call(
         own_kernel,
-        (shape(blocks, 9, SEG, SEG), shape(blocks, 3, SEG, SEG), shape(blocks, 8, SEG)),
-        [SMEM] * 4 + [VMEM] * 3,
-        [table],
+        (jax.ShapeDtypeStruct((blocks, SEG, FEATURES), bf16), shape(SEG, SEG)),
+        [HBM] * 7,
+        [pltpu.SMEM(x.shape, x.dtype) for x in raw]
+        + [pltpu.VMEM(x.shape, x.dtype) for x in segments]
+        + [pltpu.SemaphoreType.DMA((7,)), table]
+        + [pltpu.VMEM((blocks, 3, SEG, SEG), f32), pltpu.VMEM((blocks, 8, SEG), f32)],
         10**9,
-        8,
-    )(pair_list, image_shift, box_matrix, pair_count, *segments)
-
-    ret, near, moments, _ = call(
+        60,
+    )(*raw, *segments)
+
+    moments = jnp.sum(recv[:, MOMENTS:, :], axis=0)
+    sources = [moments] + [
+        lax.ppermute(moments, "slab", [(s, (s + k) % slabs) for s in range(slabs)])
+        for k in range(1, slabs)
+    ]
+
+    ret, near = call(
         pair_kernel,
-        (shape(peers, 16, SEG), shape(SEG, SEG), shape(CS, SEG), shape(blocks, 3, SEG, SEG)),
-        [VMEM] * 4,
+        (shape(peers, 16, SEG), shape(SEG, SEG)),
+        [VMEM] * 3,
         [
+            pltpu.VMEM((blocks, 3, SEG, SEG), f32),
             pltpu.VMEM((peers, SEG), jnp.int32),
             pltpu.SMEM((peers, SEG), jnp.int32),
             pltpu.SemaphoreType.DMA,
         ],
         10**10,
-        8,
-        {2: 3},
-    )(recv, columns, acc, left_acc)
+        16,
+    )(recv, features, near_own)
     back = lax.all_to_all(ret, "bulk", 0, 0, tiled=True)
-    sources = [moments] + [
-        lax.ppermute(moments, "slab", [(s, (s + k) % slabs) for s in range(slabs)])
-        for k in range(1, slabs)
-    ]
-
+    raw = [block_cell, applied_stress]
     far = call(
-        far_kernel_body,
+        functools.partial(far_kernel_body, slabs),
         shape(3, segs),
-        [SMEM] * 2 + [VMEM] * (4 + slabs),
-        [
+        [HBM] * 6 + [VMEM] * slabs,
+        [pltpu.SMEM(x.shape, x.dtype) for x in raw]
+        + [pltpu.VMEM(x.shape, x.dtype) for x in segments + [far_kernel]]
+        + [
+            pltpu.SemaphoreType.DMA((6,)),
             pltpu.VMEM((slabs * CS + CS, SEG), f32),
             pltpu.VMEM((CS, slabs * CS * NM), f32),
             pltpu.VMEM((NM, segs), f32),
             pltpu.VMEM((CS, segs), f32),
         ],
         10**9,
-        24,
-    )(block_cell, applied_stress, far_kernel, seg_offset, tangent, burgers, *sources)
+        61,
+    )(*raw, *segments, far_kernel, *sources)
 
     return call(
         final_kernel,

time: 102 us -> 96.4 us (0.945)
  local copies, waits for them, and re-layouts: 24.9 us -> 3.53 us
  waiting for transfers between devices: 5.03 us -> 17.6 us
  Pallas kernels: 40.3 us -> 43 us
    unnamed x36 -> x26, local copies, waits for them, and re-layouts: 24.9 us -> 3.53 us
    all_to_all x1, waiting for transfers between devices: 1.35 us -> 15.7 us  [local(): recv = lax.all_to_all(send, 'bulk', 0, 0, tiled=True)]
    pallas_call x4, Pallas kernels: 37 us -> 39.7 us  [the longest x1 16.9 us: local(): call(pair_kernel, (shape(peers, 16, SEG), shape(SEG, SEG)), [VMEM] * 3, [...]
    ppermute x7, waiting for transfers between devices: 3.67 us -> 1.88 us  [local(): lax.ppermute(moments, 'slab', [(s, (s + k) % slabs) for s in range(slabs)])]
  transfers between devices with their start and end apart: 9 -> 9, of which waited for: 3 -> 3; matrix products, arithmetic and copies ran while one was open for 0% -> 0% of each run, Pallas kernels for 14% -> 18%
where the time goes in v3:
time: 96.4 us; the launch traced here: 95.8 us
  Pallas kernels  43 us (45%)
  starting transfers between devices  30.8 us (32%)
  waiting for transfers between devices  17.6 us (18%)
  local copies, waits for them, and re-layouts  3.53 us (4%)
    pallas_call x1, Pallas kernels, local(): call(pair_kernel, (shape(peers, 16, SEG), shape(SEG, SEG)), [VMEM] * 3, [...  16.9 us
    all_to_all x1, waiting for transfers between devices, local(): recv = lax.all_to_all(send, 'bulk', 0, 0, tiled=True)  15.7 us
    all_to_all x1, starting transfers between devices, local(): recv = lax.all_to_all(send, 'bulk', 0, 0, tiled=True)  12 us
    ppermute x7, starting transfers between devices, local(): lax.ppermute(moments, 'slab', [(s, (s + k) % slabs) for s in range(slabs)])  10.2 us
    pallas_call x1, Pallas kernels, local(): call(functools.partial(far_kernel_body, slabs), shape(3, segs), [HBM] * 6...  8.77 us
    all_to_all x1, starting transfers between devices, local(): back = lax.all_to_all(ret, 'bulk', 0, 0, tiled=True)  8.59 us
    pallas_call x1, Pallas kernels, local(): call(own_kernel, (jax.ShapeDtypeStruct((blocks, SEG, FEATURES), bf16), sh...  8.28 us
    pallas_call x1, Pallas kernels, local(): call(pack_kernel, shape(peers, ROWS, SEG), [HBM] * 8, [pltpu.SMEM(x.shape...  5.75 us
  transfers between devices with their start and end apart: 9, of which 3 were waited for; matrix products, arithmetic and copies ran while one was open for 0% of the time, Pallas kernels for 18%

profile of v3, /device:TPU:1, one launch (start us, length us, event | category | flops | bytes accessed | tf_op | source)
XLA Modules:
  0.0 95.8 jit_solution(17371352810989649802)
XLA Ops:
  0.0 5.8 %shard_map.118 = f32[32,64,128]{2,1,0:T(8,128)} custom-call(s32[2,192]{1,0:T(2,128)} %pairs.1, s32[3,192]{1,0:T(4,128)} %refs_1_.4, f32[3,3]{1,0:T(4,128)} %refs_2_.4, s32[5,32]{1,0:T(8,128)} %bitcast.1, s32[32]{0:T(128)} %refs_0_.5, f32[3,4096]{1,0:T(4,128)} %refs_2_.5, f32[3,4096]{1,0:T(4,128)} %refs_3_.2, f32[3,4096]{1,0:T(4,128)} %refs_4_.5), custom_call_target="tpu_custom_call" | custom-call | flops 1000000 | bytes 1048576 | tf_op jit(solution)/shard_map/pallas_call | solution.py:378
  5.8 12.0 %all-to-all-start = ((f32[32,64,128]{2,1,0:T(8,128)}), f32[32,64,128]{2,1,0:T(8,128)S(1)}, u32[]{:S(2)}, u32[]{:S(2)}) async-start(f32[32,64,128]{2,1,0:T(8,128)} %shard_map.118), calls=%async_computation | async-start | bytes 2097152 | tf_op jit(solution)/shard_map/all_to_all | solution.py:389
  18.5 8.3 %shard_map.119 = (bf16[32,128,48]{2,1,0:T(8,128)(2,1)}, f32[128,128]{1,0:T(8,128)}) custom-call(s32[2,192]{1,0:T(2,128)} %pairs.1, s32[3,192]{1,0:T(4,128)} %refs_1_.4, f32[3,3]{1,0:T(4,128)} %refs_2_.4, s32[1]{0:T(128)S(6)} %copy.13.refs_3_, f32[3,4096]{1,0:T(4,128)} %refs_2_.5, f32[3,4096]{1,0:T(4,128)} %refs_3_.2, f32[3,4096]{1,0:T(4,128)} %refs_4_.5), custom_call_target="tpu_custom_call" | custom-call | flops 1000000000 | bytes 1048576 | tf_op jit(solution)/shard_map/pallas_call | solution.py:392
  26.7 15.7 %all-to-all-done.recv = f32[32,64,128]{2,1,0:T(8,128)S(1)} async-done(((f32[32,64,128]{2,1,0:T(8,128)}), f32[32,64,128]{2,1,0:T(8,128)S(1)}, u32[]{:S(2)}, u32[]{:S(2)}) %all-to-all-start) | async-done | bytes 1048608 | tf_op jit(solution)/shard_map/all_to_all | solution.py:389
  42.4 1.2 %copy-done.3 = bf16[32,128,48]{2,1,0:T(8,128)(2,1)S(1)} copy-done((bf16[32,128,48]{2,1,0:T(8,128)(2,1)S(1)}, bf16[32,128,48]{2,1,0:T(8,128)(2,1)}, u32[]{:S(2)}) %copy-start.3) | copy-done | bytes 393240
  43.7 0.8 copy-done.4
  44.5 16.9 %shard_map.120 = (f32[32,16,128]{2,1,0:T(8,128)}, f32[128,128]{1,0:T(8,128)S(1)}) custom-call(f32[32,64,128]{2,1,0:T(8,128)S(1)} %all-to-all-done.recv, bf16[32,128,48]{2,1,0:T(8,128)(2,1)S(1)} %copy-done.3, f32[128,128]{1,0:T(8,128)S(1)} %copy-done.4), custom_call_target="tpu_custom_call" | custom-call | flops 10000000000 | bytes 1048576 | tf_op jit(solution)/shard_map/pallas_call | solution.py:410
  61.4 0.0 copy-start.1
  61.4 0.0 copy-start.2
  61.4 8.6 %all-to-all-start.1 = ((f32[32,16,128]{2,1,0:T(8,128)}), f32[32,16,128]{2,1,0:T(8,128)S(1)}, u32[]{:S(2)}, u32[]{:S(2)}) async-start(f32[32,16,128]{2,1,0:T(8,128)} %get-tuple-element.11), calls=%async_computation.1 | async-start | bytes 524288 | tf_op jit(solution)/shard_map/all_to_all | solution.py:423
  70.1 2.6 %collective-permute-start = (f32[16,128]{1,0:T(8,128)S(1)}, f32[16,128]{1,0:T(8,128)S(1)}, u32[]{:S(2)}, u32[]{:S(2)}) collective-permute-start(f32[16,128]{1,0:T(8,128)S(1)} %slice_reduce_fusion.refs_6_), channel_id=1, source_target_pairs={{0,32},{32,64},{64,96},{96,128},{128,160},{160,192},{192,224},{224... | collective-permute-start | bytes 24584 | tf_op jit(solution)/shard_map/ppermute | solution.py:406
  72.7 1.2 %collective-permute-start.1 = (f32[16,128]{1,0:T(8,128)S(1)}, f32[16,128]{1,0:T(8,128)S(1)}, u32[]{:S(2)}, u32[]{:S(2)}) collective-permute-start(f32[16,128]{1,0:T(8,128)S(1)} %slice_reduce_fusion.refs_6_), channel_id=1, source_target_pairs={{0,64},{32,96},{64,128},{96,160},{128,192},{160,224},{192,0},{224,... | collective-permute-start | bytes 24584 | tf_op jit(solution)/shard_map/ppermute | solution.py:406
  73.9 1.6 %collective-permute-start.2 = (f32[16,128]{1,0:T(8,128)S(1)}, f32[16,128]{1,0:T(8,128)S(1)}, u32[]{:S(2)}, u32[]{:S(2)}) collective-permute-start(f32[16,128]{1,0:T(8,128)S(1)} %slice_reduce_fusion.refs_6_), channel_id=1, source_target_pairs={{0,96},{32,128},{64,160},{96,192},{128,224},{160,0},{192,32},{224,... | collective-permute-start | bytes 24584 | tf_op jit(solution)/shard_map/ppermute | solution.py:406
  75.5 0.5 collective-permute-start.3
  76.0 1.9 %collective-permute-start.4 = (f32[16,128]{1,0:T(8,128)S(1)}, f32[16,128]{1,0:T(8,128)S(1)}, u32[]{:S(2)}, u32[]{:S(2)}) collective-permute-start(f32[16,128]{1,0:T(8,128)S(1)} %slice_reduce_fusion.refs_6_), channel_id=1, source_target_pairs={{0,160},{32,192},{64,224},{96,0},{128,32},{160,64},{192,96},{224,1... | collective-permute-start | bytes 24584 | tf_op jit(solution)/shard_map/ppermute | solution.py:406
  77.9 0.7 collective-permute-start.5
  78.6 1.7 %collective-permute-start.6 = (f32[16,128]{1,0:T(8,128)S(1)}, f32[16,128]{1,0:T(8,128)S(1)}, u32[]{:S(2)}, u32[]{:S(2)}) collective-permute-start(f32[16,128]{1,0:T(8,128)S(1)} %slice_reduce_fusion.refs_6_), channel_id=1, source_target_pairs={{0,224},{32,0},{64,32},{96,64},{128,96},{160,128},{192,160},{224,1... | collective-permute-start | bytes 24584 | tf_op jit(solution)/shard_map/ppermute | solution.py:406
  80.3 0.6 collective-permute-done.4.refs_11_
  80.9 1.3 %collective-permute-done.6.refs_13_ = f32[16,128]{1,0:T(8,128)S(1)} collective-permute-done((f32[16,128]{1,0:T(8,128)S(1)}, f32[16,128]{1,0:T(8,128)S(1)}, u32[]{:S(2)}, u32[]{:S(2)}) %collective-permute-start.6) | collective-permute-done | bytes 8224 | tf_op jit(solution)/shard_map/ppermute | solution.py:406
  82.3 0.6 copy-done.12
  82.8 8.8 %shard_map.121.far = f32[3,4096]{1,0:T(4,128)} custom-call(s32[32]{0:T(128)} %refs_0_.5, f32[3,3]{1,0:T(4,128)} %refs_1_.5, f32[3,4096]{1,0:T(4,128)} %refs_2_.5, f32[3,4096]{1,0:T(4,128)} %refs_3_.2, f32[3,4096]{1,0:T(4,128)} %refs_4_.5, f32[84,10752]{1,0:T(8,128)} %refs_5_.5, f32[16,128]{1,0:T(8,128)} %copy-done.5, f32[16,128]{1,0:T(8,128)} %copy-done.6, ...), custom_call_target="tpu_custom_call" | custom-call | flops 1000000000 | bytes 1048576 | tf_op jit(solution)/shard_map/pallas_call | solution.py:425
  91.6 0.0 copy-start
  91.7 0.8 copy-done
  92.5 3.3 %shard_map.122 = f32[3,4096]{1,0:T(4,128)} custom-call(s32[2,192]{1,0:T(2,128)S(1)} %copy-done.1, f32[32,16,128]{2,1,0:T(8,128)S(1)} %all-to-all-done.1.back, f32[128,128]{1,0:T(8,128)S(1)} %get-tuple-element.12.near_all, f32[3,4096]{1,0:T(4,128)S(1)} %copy-done, s32[2,4096]{1,0:T(2,128)S(1)} %copy-done.2), custom_call_target="tpu_custom_call" | custom-call | flops 1000000000 | bytes 1048576 | tf_op jit(solution)/shard_map/pallas_call | solution.py:442
  (26 shorter events, 0.1 us)
Async XLA Ops:
  5.8 36.7 %all-to-all-start = ((f32[32,64,128]{2,1,0:T(8,128)}), f32[32,64,128]{2,1,0:T(8,128)S(1)}, u32[]{:S(2)}, u32[]{:S(2)}) async-start(f32[32,64,128]{2,1,0:T(8,128)} %shard_map.118), calls=%async_computation | async-start | bytes 2097152 | tf_op jit(solution)/shard_map/all_to_all | solution.py:389
  42.4 1.2 %copy-start.3 = (bf16[32,128,48]{2,1,0:T(8,128)(2,1)S(1)}, bf16[32,128,48]{2,1,0:T(8,128)(2,1)}, u32[]{:S(2)}) copy-start(bf16[32,128,48]{2,1,0:T(8,128)(2,1)} %get-tuple-element.9.features) | copy-start | bytes 1179652
  43.7 0.8 copy-start.4
  61.4 30.2 %copy-start.1 = (s32[2,192]{1,0:T(2,128)S(1)}, s32[2,192]{1,0:T(2,128)}, u32[]{:S(2)}) copy-start(s32[2,192]{1,0:T(2,128)} %pairs.1) | copy-start | bytes 4612
  61.4 30.2 %copy-start.2 = (s32[2,4096]{1,0:T(2,128)S(1)}, s32[2,4096]{1,0:T(2,128)}, u32[]{:S(2)}) copy-start(s32[2,4096]{1,0:T(2,128)} %conn.1) | copy-start | bytes 98308
  61.4 30.2 %all-to-all-start.1 = ((f32[32,16,128]{2,1,0:T(8,128)}), f32[32,16,128]{2,1,0:T(8,128)S(1)}, u32[]{:S(2)}, u32[]{:S(2)}) async-start(f32[32,16,128]{2,1,0:T(8,128)} %get-tuple-element.11), calls=%async_computation.1 | async-start | bytes 524288 | tf_op jit(solution)/shard_map/all_to_all | solution.py:423
  70.1 12.1 %copy-start.5 = (f32[16,128]{1,0:T(8,128)}, f32[16,128]{1,0:T(8,128)S(1)}, u32[]{:S(2)}) copy-start(f32[16,128]{1,0:T(8,128)S(1)} %slice_reduce_fusion.refs_6_) | copy-start | bytes 24580
  70.1 7.9 %collective-permute-start = (f32[16,128]{1,0:T(8,128)S(1)}, f32[16,128]{1,0:T(8,128)S(1)}, u32[]{:S(2)}, u32[]{:S(2)}) collective-permute-start(f32[16,128]{1,0:T(8,128)S(1)} %slice_reduce_fusion.refs_6_), channel_id=1, source_target_pairs={{0,32},{32,64},{64,96},{96,128},{128,160},{160,192},{192,224},{224... | collective-permute-start | bytes 24584 | tf_op jit(solution)/shard_map/ppermute | solution.py:406
  72.7 5.9 %collective-permute-start.1 = (f32[16,128]{1,0:T(8,128)S(1)}, f32[16,128]{1,0:T(8,128)S(1)}, u32[]{:S(2)}, u32[]{:S(2)}) collective-permute-start(f32[16,128]{1,0:T(8,128)S(1)} %slice_reduce_fusion.refs_6_), channel_id=1, source_target_pairs={{0,64},{32,96},{64,128},{96,160},{128,192},{160,224},{192,0},{224,... | collective-permute-start | bytes 24584 | tf_op jit(solution)/shard_map/ppermute | solution.py:406
  73.9 6.4 %collective-permute-start.2 = (f32[16,128]{1,0:T(8,128)S(1)}, f32[16,128]{1,0:T(8,128)S(1)}, u32[]{:S(2)}, u32[]{:S(2)}) collective-permute-start(f32[16,128]{1,0:T(8,128)S(1)} %slice_reduce_fusion.refs_6_), channel_id=1, source_target_pairs={{0,96},{32,128},{64,160},{96,192},{128,224},{160,0},{192,32},{224,... | collective-permute-start | bytes 24584 | tf_op jit(solution)/shard_map/ppermute | solution.py:406
  75.5 4.8 %collective-permute-start.3 = (f32[16,128]{1,0:T(8,128)S(1)}, f32[16,128]{1,0:T(8,128)S(1)}, u32[]{:S(2)}, u32[]{:S(2)}) collective-permute-start(f32[16,128]{1,0:T(8,128)S(1)} %slice_reduce_fusion.refs_6_), channel_id=1, source_target_pairs={{0,128},{32,160},{64,192},{96,224},{128,0},{160,32},{192,64},{224,... | collective-permute-start | bytes 24584 | tf_op jit(solution)/shard_map/ppermute | solution.py:406
  76.0 4.9 %collective-permute-start.4 = (f32[16,128]{1,0:T(8,128)S(1)}, f32[16,128]{1,0:T(8,128)S(1)}, u32[]{:S(2)}, u32[]{:S(2)}) collective-permute-start(f32[16,128]{1,0:T(8,128)S(1)} %slice_reduce_fusion.refs_6_), channel_id=1, source_target_pairs={{0,160},{32,192},{64,224},{96,0},{128,32},{160,64},{192,96},{224,1... | collective-permute-start | bytes 24584 | tf_op jit(solution)/shard_map/ppermute | solution.py:406
  77.9 4.3 %copy-start.6 = (f32[16,128]{1,0:T(8,128)}, f32[16,128]{1,0:T(8,128)S(1)}, u32[]{:S(2)}) copy-start(f32[16,128]{1,0:T(8,128)S(1)} %collective-permute-done.refs_7_) | copy-start | bytes 24580
  77.9 2.9 %collective-permute-start.5 = (f32[16,128]{1,0:T(8,128)S(1)}, f32[16,128]{1,0:T(8,128)S(1)}, u32[]{:S(2)}, u32[]{:S(2)}) collective-permute-start(f32[16,128]{1,0:T(8,128)S(1)} %slice_reduce_fusion.refs_6_), channel_id=1, source_target_pairs={{0,192},{32,224},{64,0},{96,32},{128,64},{160,96},{192,128},{224,1... | collective-permute-start | bytes 24584 | tf_op jit(solution)/shard_map/ppermute | solution.py:406
  78.6 3.6 %copy-start.7 = (f32[16,128]{1,0:T(8,128)}, f32[16,128]{1,0:T(8,128)S(1)}, u32[]{:S(2)}) copy-start(f32[16,128]{1,0:T(8,128)S(1)} %collective-permute-done.1.refs_8_) | copy-start | bytes 24580
  78.6 3.6 %collective-permute-start.6 = (f32[16,128]{1,0:T(8,128)S(1)}, f32[16,128]{1,0:T(8,128)S(1)}, u32[]{:S(2)}, u32[]{:S(2)}) collective-permute-start(f32[16,128]{1,0:T(8,128)S(1)} %slice_reduce_fusion.refs_6_), channel_id=1, source_target_pairs={{0,224},{32,0},{64,32},{96,64},{128,96},{160,128},{192,160},{224,1... | collective-permute-start | bytes 24584 | tf_op jit(solution)/shard_map/ppermute | solution.py:406
  80.3 1.9 %copy-start.8 = (f32[16,128]{1,0:T(8,128)}, f32[16,128]{1,0:T(8,128)S(1)}, u32[]{:S(2)}) copy-start(f32[16,128]{1,0:T(8,128)S(1)} %collective-permute-done.2.refs_9_) | copy-start | bytes 24580
  80.3 1.9 %copy-start.9 = (f32[16,128]{1,0:T(8,128)}, f32[16,128]{1,0:T(8,128)S(1)}, u32[]{:S(2)}) copy-start(f32[16,128]{1,0:T(8,128)S(1)} %collective-permute-done.3.refs_10_) | copy-start | bytes 24580
  80.9 1.3 %copy-start.10 = (f32[16,128]{1,0:T(8,128)}, f32[16,128]{1,0:T(8,128)S(1)}, u32[]{:S(2)}) copy-start(f32[16,128]{1,0:T(8,128)S(1)} %collective-permute-done.4.refs_11_) | copy-start | bytes 24580
  80.9 1.4 %copy-start.11 = (f32[16,128]{1,0:T(8,128)}, f32[16,128]{1,0:T(8,128)S(1)}, u32[]{:S(2)}) copy-start(f32[16,128]{1,0:T(8,128)S(1)} %collective-permute-done.5.refs_12_) | copy-start | bytes 24580
  82.2 0.6 copy-start.12
  91.6 0.8 copy-start

commit v4 on v3

--- a/solution.py
+++ b/solution.py
@@ -1,5 +1,3 @@
-import functools
-
 import jax
 import jax.numpy as jnp
 from jax import lax
@@ -11,9 +9,11 @@
 CS = 16
 NM = 84
 SEND = 5
-META = 45
-MOMENTS = 48
-ROWS = MOMENTS + CS
+LAST = 40
+MOMENTS = 45
+ROWS = 56
+GROUP = 11
+META = 112
 FEATURES = 48
 KAPPA = 0.2
 CORE_SQ = 0.25
@@ -73,20 +73,20 @@
     for copy in fetch_all(sources, scratch[:8], sems):
         copy.wait()
     fill_table(table, off, tan, bur, 2.0 * KAPPA, KAPPA)
-    row, lane = iota((MOMENTS - META, SEG), 0), iota((MOMENTS - META, SEG), 1)
-    moments = cell_moments(cell, off, tan, bur, phi, charged)
+    packed = cell_moments(cell, off, tan, bur, phi, charged)
+    row, lane = iota((ROWS - LAST, SEG), 0), iota((ROWS - LAST, SEG), 1)
 
     def peer(p, carry):
-        meta = jnp.zeros((MOMENTS - META, SEG), f32)
+        rest = packed
         for s in range(SEND):
             k = p * SEND + s
             at = lane_block(pairs[0, k])
             vec = shift_rows(shift_of(box, shift, k), (8, SEG))
             send[p, 8 * s : 8 * s + 8, :] = table[0:8, at] - vec
-            send[p, 40 + s : 41 + s, :] = table[8:9, at]
-            meta = jnp.where((row == 0) & (lane == s), fetch[s, p].astype(f32), meta)
-        send[p, META:MOMENTS, :] = meta
-        send[p, MOMENTS:ROWS, :] = moments
+            rest = jnp.where(row == s, table[8:9, at], rest)
+            mine = (row == ROWS - LAST - 1) & (lane == META + s)
+            rest = jnp.where(mine, fetch[s, p].astype(f32), rest)
+        send[p, LAST:ROWS, :] = rest
         return carry
 
     lax.fori_loop(0, send.shape[0], peer, 0)
@@ -181,14 +181,9 @@
     lax.fori_loop(0, acc.shape[0], block, 0)
 
 
-def own_kernel(*refs):
-    sources, (features, near), scratch = refs[:7], refs[7:9], refs[9:]
-    pairs, shift, box, count, off, tan, bur, sems, table, acc, left_acc = scratch
-    copies = fetch_all(sources, scratch[:7], sems)
+def own_kernel(pairs, shift, box, count, off, tan, bur, features, near, table, acc, left_acc):
     clear(acc)
     left_acc[...] = jnp.zeros_like(left_acc)
-    for copy in copies:
-        copy.wait()
     fill_table(table, off, tan, bur, 1.0, 1.0)
     fill_features(table, features)
     blocks = acc.shape[0]
@@ -213,7 +208,7 @@
 def pair_kernel(recv, features, near_own, ret, near, acc, ids_vmem, ids, sem):
     peers = recv.shape[0]
     for p in range(peers):
-        ids_vmem[p : p + 1, :] = recv[p, META : META + 1, :].astype(jnp.int32)
+        ids_vmem[p : p + 1, :] = recv[p, ROWS - 1 : ROWS, :].astype(jnp.int32)
     copy = pltpu.make_async_copy(ids_vmem, ids, sem)
     copy.start()
     clear(acc)
@@ -221,8 +216,8 @@
 
     def peer(p, carry):
         for s in range(SEND):
-            head, last = recv[p, 8 * s : 8 * s + 8, :], recv[p, 40 + s : 41 + s, :]
-            rows = tile(head, last, features, acc, ids[p, s])
+            head, last = recv[p, 8 * s : 8 * s + 8, :], recv[p, LAST + s : LAST + s + 1, :]
+            rows = tile(head, last, features, acc, ids[p, META + s])
             for c in range(3):
                 ret[p, 3 * s + c : 3 * s + c + 1, :] = rows[c]
         ret[p, 15:16, :] = jnp.zeros((1, SEG), f32)
@@ -264,18 +259,28 @@
     for b in range(cell.shape[0]):
         part = charge[:, b * SEG : (b + 1) * SEG]
         charged[:, b * SEG : (b + 1) * SEG] = jnp.where(row == cell[b], part, 0.0)
-    part = dot_nt(charged[...], phi[...], HIGH)
-    return jnp.concatenate([part, jnp.zeros((CS, SEG - NM), f32)], axis=1)
-
-
-def far_kernel_body(count, *refs):
-    raw, sources, out, scratch = refs[:6], refs[6 : 6 + count], refs[6 + count], refs[7 + count :]
+    part = dot_nt(phi[...], charged[...], HIGH)
+    part = jnp.concatenate([part, jnp.zeros((8 * GROUP - NM, CS), f32)], axis=0)
+    groups = [part[GROUP * g : GROUP * (g + 1), :] for g in range(8)]
+    return jnp.concatenate([jnp.zeros((MOMENTS - LAST, SEG), f32), jnp.concatenate(groups, axis=1)], axis=0)
+
+
+def far_kernel_body(*refs):
+    raw, sources, out, scratch = refs[:6], refs[6:10], refs[10], refs[11:]
     cell, stress, off, tan, bur, operator, sems, around, shifted, phi, pots = scratch
     copies = fetch_all(raw, scratch[:6], sems)
+    half = len(sources)
+    count = 2 * half
     cells = count * CS
+    turned = jnp.concatenate([source[...] for source in sources], axis=0).T
+    first = MOMENTS - LAST
     for q in range(count):
-        around[q * CS : (q + 1) * CS, :] = sources[(count - q) % count][...]
-    around[cells : cells + CS, :] = sources[0][...]
+        back = (count - q) % count
+        at = CS * (2 * (back % half) + back // half) + first
+        for g in range(8):
+            piece = turned[CS * g : CS * (g + 1), at : at + GROUP]
+            around[q * CS : (q + 1) * CS, GROUP * g : GROUP * (g + 1)] = piece
+    around[cells : cells + CS, :] = around[0:CS, :]
     shifted[:, 0:NM] = jnp.zeros((CS, NM), f32)
     for o in range(1, cells):
         shifted[:, o * NM : (o + 1) * NM] = around[cells - o : cells - o + CS, 0:NM]
@@ -388,24 +393,25 @@
     )(*raw, *segments)
     recv = lax.all_to_all(send, "bulk", 0, 0, tiled=True)
 
-    raw = [pair_list, image_shift, box_matrix, pair_count]
     features, near_own = call(
         own_kernel,
         (jax.ShapeDtypeStruct((blocks, SEG, FEATURES), bf16), shape(SEG, SEG)),
-        [HBM] * 7,
-        [pltpu.SMEM(x.shape, x.dtype) for x in raw]
-        + [pltpu.VMEM(x.shape, x.dtype) for x in segments]
-        + [pltpu.SemaphoreType.DMA((7,)), table]
-        + [pltpu.VMEM((blocks, 3, SEG, SEG), f32), pltpu.VMEM((blocks, 8, SEG), f32)],
+        [SMEM] * 4 + [VMEM] * 3,
+        [
+            table,
+            pltpu.VMEM((blocks, 3, SEG, SEG), f32),
+            pltpu.VMEM((blocks, 8, SEG), f32),
+        ],
         10**9,
-        60,
-    )(*raw, *segments)
-
-    moments = jnp.sum(recv[:, MOMENTS:, :], axis=0)
-    sources = [moments] + [
-        lax.ppermute(moments, "slab", [(s, (s + k) % slabs) for s in range(slabs)])
-        for k in range(1, slabs)
-    ]
+        12,
+    )(pair_list, image_shift, box_matrix, pair_count, *segments)
+
+    def from_slab(value, back):
+        return lax.ppermute(value, "slab", [(s, (s + back) % slabs) for s in range(slabs)])
+
+    half = slabs // 2
+    moments = jnp.sum(recv[:, LAST:, :], axis=0)
+    other = from_slab(moments, half)
 
     ret, near = call(
         pair_kernel,
@@ -420,12 +426,15 @@
         10**10,
         16,
     )(recv, features, near_own)
+    ret, other = lax.optimization_barrier((ret, other))
     back = lax.all_to_all(ret, "bulk", 0, 0, tiled=True)
+    two = jnp.concatenate([moments, other], axis=0)
+    sources = [two] + [from_slab(two, k) for k in range(1, half)]
     raw = [block_cell, applied_stress]
     far = call(
-        functools.partial(far_kernel_body, slabs),
+        far_kernel_body,
         shape(3, segs),
-        [HBM] * 6 + [VMEM] * slabs,
+        [HBM] * 6 + [VMEM] * half,
         [pltpu.SMEM(x.shape, x.dtype) for x in raw]
         + [pltpu.VMEM(x.shape, x.dtype) for x in segments + [far_kernel]]
         + [
@@ -436,7 +445,7 @@
             pltpu.VMEM((CS, segs), f32),
         ],
         10**9,
-        61,
+        52,
     )(*raw, *segments, far_kernel, *sources)
 
     return call(

time: 96.4 us -> 86.5 us (0.90)
  waiting for transfers between devices: 17.6 us -> 10.2 us
  starting transfers between devices: 30.8 us -> 27.4 us
  local copies, waits for them, and re-layouts: 3.53 us -> 4.59 us
    all_to_all x1, waiting for transfers between devices: 15.7 us -> 7.63 us  [local(): recv = lax.all_to_all(send, 'bulk', 0, 0, tiled=True)]
    ppermute x7 -> x4, starting transfers between devices: 10.2 us -> 6.87 us  [from_slab(): lax.ppermute(value, 'slab', [(s, (s + back) % slabs) for s in range(slabs)])]
    unnamed x26, local copies, waits for them, and re-layouts: 3.53 us -> 4.59 us
    pallas_call x1, Pallas kernels: 8.77 us -> 7.76 us  [local(): call(far_kernel_body, shape(3, segs), [HBM] * 6 + [VMEM] * half, [pltpu.S...]
    ppermute x7 -> x4, waiting for transfers between devices: 1.88 us -> 2.6 us  [from_slab(): lax.ppermute(value, 'slab', [(s, (s + back) % slabs) for s in range(slabs)])]
  transfers between devices with their start and end apart: 9 -> 6, of which waited for: 3 -> 3; matrix products, arithmetic and copies ran while one was open for 0% -> 0% of each run, Pallas kernels for 18% -> 39%
where the time goes in v4:
time: 86.5 us; the launch traced here: 85.9 us
  Pallas kernels  42.9 us (50%)
  starting transfers between devices  27.4 us (32%)
  waiting for transfers between devices  10.2 us (12%)
  local copies, waits for them, and re-layouts  4.59 us (5%)
    pallas_call x1, Pallas kernels, local(): call(pair_kernel, (shape(peers, 16, SEG), shape(SEG, SEG)), [VMEM] * 3, [...  16.9 us
    all_to_all x1, starting transfers between devices, local(): recv = lax.all_to_all(send, 'bulk', 0, 0, tiled=True)  12 us
    pallas_call x1, Pallas kernels, local(): call(own_kernel, (jax.ShapeDtypeStruct((blocks, SEG, FEATURES), bf16), sh...  9.08 us
    all_to_all x1, starting transfers between devices, local(): back = lax.all_to_all(ret, 'bulk', 0, 0, tiled=True)  8.47 us
    pallas_call x1, Pallas kernels, local(): call(far_kernel_body, shape(3, segs), [HBM] * 6 + [VMEM] * half, [pltpu.S...  7.76 us
    all_to_all x1, waiting for transfers between devices, local(): recv = lax.all_to_all(send, 'bulk', 0, 0, tiled=True)  7.63 us
    ppermute x4, starting transfers between devices, from_slab(): lax.ppermute(value, 'slab', [(s, (s + back) % slabs) for s in range(slabs)])  6.87 us
    pallas_call x1, Pallas kernels, local(): call(pack_kernel, shape(peers, ROWS, SEG), [HBM] * 8, [pltpu.SMEM(x.shape...  5.85 us
  transfers between devices with their start and end apart: 6, of which 3 were waited for; matrix products, arithmetic and copies ran while one was open for 0% of the time, Pallas kernels for 39%

profile of v4, /device:TPU:1, one launch (start us, length us, event | category | flops | bytes accessed | tf_op | source)
XLA Modules:
  0.0 85.9 jit_solution(15189843730576513358)
XLA Ops:
  0.0 5.9 %shard_map.118 = f32[32,56,128]{2,1,0:T(8,128)} custom-call(s32[2,192]{1,0:T(2,128)} %pairs.3, s32[3,192]{1,0:T(4,128)} %shift.1, f32[3,3]{1,0:T(4,128)} %box.1, s32[5,32]{1,0:T(8,128)} %bitcast.1, s32[32]{0:T(128)} %refs_0_.3, f32[3,4096]{1,0:T(4,128)} %refs_2_.3, f32[3,4096]{1,0:T(4,128)} %refs_3_.1, f32[3,4096]{1,0:T(4,128)} %refs_4_.3), custom_call_target="tpu_custom_call" | custom-call | flops 1000000 | bytes 1048576 | tf_op jit(solution)/shard_map/pallas_call | solution.py:383
  5.9 12.0 %all-to-all-start = ((f32[32,56,128]{2,1,0:T(8,128)}), f32[32,56,128]{2,1,0:T(8,128)S(1)}, u32[]{:S(2)}, u32[]{:S(2)}) async-start(f32[32,56,128]{2,1,0:T(8,128)} %shard_map.118), calls=%async_computation | async-start | bytes 1835008 | tf_op jit(solution)/shard_map/all_to_all | solution.py:394
  18.6 0.0 copy-start
  18.6 0.8 copy-done
  19.4 0.8 copy-done.2
  20.2 0.8 copy-done.4
  21.1 0.7 copy-done.6
  21.8 0.7 copy-done.7
  22.5 0.7 copy-done.9
  23.1 9.1 %shard_map.119 = (bf16[32,128,48]{2,1,0:T(8,128)(2,1)S(1)}, f32[128,128]{1,0:T(8,128)S(1)}) custom-call(s32[2,192]{1,0:T(2,128)S(1)} %copy-done.9, s32[3,192]{1,0:T(4,128)S(1)} %copy-done.6, f32[3,3]{1,0:T(4,128)S(1)} %copy-done.7, s32[1]{0:T(128)S(6)} %copy.13.count, f32[3,4096]{1,0:T(4,128)S(1)} %copy-done, f32[3,4096]{1,0:T(4,128)S(1)} %copy-done.2, ...), custom_call_target="tpu_custom_call" | custom-call | flops 1000000000 | bytes 1048576 | tf_op jit(solution)/shard_map/pallas_call | solution.py:396
  32.2 7.6 %all-to-all-done.recv = f32[32,56,128]{2,1,0:T(8,128)S(1)} async-done(((f32[32,56,128]{2,1,0:T(8,128)}), f32[32,56,128]{2,1,0:T(8,128)S(1)}, u32[]{:S(2)}, u32[]{:S(2)}) %all-to-all-start) | async-done | bytes 917536 | tf_op jit(solution)/shard_map/all_to_all | solution.py:394
  39.9 2.8 %collective-permute-start = (f32[16,128]{1,0:T(8,128)S(1)}, f32[16,128]{1,0:T(8,128)S(1)}, u32[]{:S(2)}, u32[]{:S(2)}) collective-permute-start(f32[16,128]{1,0:T(8,128)S(1)} %slice_reduce_fusion), channel_id=1, source_target_pairs={{0,128},{32,160},{64,192},{96,224},{128,0},{160,32},{192,64},{224,... | collective-permute-start | bytes 24584 | tf_op jit(solution)/shard_map/ppermute | solution.py:410
  42.7 0.0 copy-start.11
  42.8 16.9 %shard_map.120 = (f32[32,16,128]{2,1,0:T(8,128)}, f32[128,128]{1,0:T(8,128)S(1)}) custom-call(f32[32,56,128]{2,1,0:T(8,128)S(1)} %all-to-all-done.recv, bf16[32,128,48]{2,1,0:T(8,128)(2,1)S(1)} %get-tuple-element.11.features, f32[128,128]{1,0:T(8,128)S(1)} %get-tuple-element.12.near_own), custom_call_target="tpu_custom_call" | custom-call | flops 10000000000 | bytes 1048576 | tf_op jit(solution)/shard_map/pallas_call | solution.py:416
  59.6 0.0 copy-start.10
  59.6 0.0 copy-start.12
  59.7 8.5 %all-to-all-start.1 = ((f32[32,16,128]{2,1,0:T(8,128)}), f32[32,16,128]{2,1,0:T(8,128)S(1)}, u32[]{:S(2)}, u32[]{:S(2)}) async-start(f32[32,16,128]{2,1,0:T(8,128)} %get-tuple-element.14), calls=%async_computation.1 | async-start | bytes 524288 | tf_op jit(solution)/shard_map/all_to_all | solution.py:430
  68.2 1.9 %collective-permute-start.1 = (f32[32,128]{1,0:T(8,128)S(1)}, f32[32,128]{1,0:T(8,128)S(1)}, u32[]{:S(2)}, u32[]{:S(2)}) collective-permute-start(f32[32,128]{1,0:T(8,128)S(1)} %pad_maximum_fusion.refs_6_), channel_id=1, source_target_pairs={{0,32},{32,64},{64,96},{96,128},{128,160},{160,192},{192,224},{224... | collective-permute-start | bytes 49160 | tf_op jit(solution)/shard_map/ppermute | solution.py:410
  70.1 0.0 collective-permute-start.2
  70.1 2.1 %collective-permute-start.3 = (f32[32,128]{1,0:T(8,128)S(1)}, f32[32,128]{1,0:T(8,128)S(1)}, u32[]{:S(2)}, u32[]{:S(2)}) collective-permute-start(f32[32,128]{1,0:T(8,128)S(1)} %pad_maximum_fusion.refs_6_), channel_id=1, source_target_pairs={{0,96},{32,128},{64,160},{96,192},{128,224},{160,0},{192,32},{224,... | collective-permute-start | bytes 49160 | tf_op jit(solution)/shard_map/ppermute | solution.py:410
  72.2 1.7 %collective-permute-done.2.refs_8_ = f32[32,128]{1,0:T(8,128)S(1)} collective-permute-done((f32[32,128]{1,0:T(8,128)S(1)}, f32[32,128]{1,0:T(8,128)S(1)}, u32[]{:S(2)}, u32[]{:S(2)}) %collective-permute-start.2) | collective-permute-done | bytes 16416 | tf_op jit(solution)/shard_map/ppermute | solution.py:410
  73.9 0.9 %collective-permute-done.3.refs_9_ = f32[32,128]{1,0:T(8,128)S(1)} collective-permute-done((f32[32,128]{1,0:T(8,128)S(1)}, f32[32,128]{1,0:T(8,128)S(1)}, u32[]{:S(2)}, u32[]{:S(2)}) %collective-permute-start.3) | collective-permute-done | bytes 16416 | tf_op jit(solution)/shard_map/ppermute | solution.py:410
  74.8 7.8 %shard_map.121.far = f32[3,4096]{1,0:T(4,128)S(1)} custom-call(s32[32]{0:T(128)S(1)} %copy-done.11, f32[3,3]{1,0:T(4,128)S(1)} %copy-done.8, f32[3,4096]{1,0:T(4,128)S(1)} %copy-done.1, f32[3,4096]{1,0:T(4,128)S(1)} %copy-done.3, f32[3,4096]{1,0:T(4,128)S(1)} %copy-done.5, f32[84,10752]{1,0:T(8,128)} %refs_5_.3, f32[32,128]{1,0:T(8,128)S(1)} %pad_maximum_fusion.refs_6_, ...), custom_call_target="tpu_custom_call" | custom-call | flops 1000000000 | bytes 1048576 | tf_op jit(solution)/shard_map/pallas_call | solution.py:434
  82.6 3.3 %shard_map.122 = f32[3,4096]{1,0:T(4,128)} custom-call(s32[2,192]{1,0:T(2,128)S(1)} %copy-done.10, f32[32,16,128]{2,1,0:T(8,128)S(1)} %all-to-all-done.1.back, f32[128,128]{1,0:T(8,128)S(1)} %get-tuple-element.15.near_all, f32[3,4096]{1,0:T(4,128)S(1)} %shard_map.121.far, s32[2,4096]{1,0:T(2,128)S(1)} %copy-done.12), custom_call_target="tpu_custom_call" | custom-call | flops 1000000000 | bytes 1048576 | tf_op jit(solution)/shard_map/pallas_call | solution.py:451
  (21 shorter events, 0.1 us)
Async XLA Ops:
  5.9 34.0 %all-to-all-start = ((f32[32,56,128]{2,1,0:T(8,128)}), f32[32,56,128]{2,1,0:T(8,128)S(1)}, u32[]{:S(2)}, u32[]{:S(2)}) async-start(f32[32,56,128]{2,1,0:T(8,128)} %shard_map.118), calls=%async_computation | async-start | bytes 1835008 | tf_op jit(solution)/shard_map/all_to_all | solution.py:394
  18.6 0.8 copy-start
  19.4 0.8 copy-start.2
  20.2 0.8 copy-start.4
  21.1 0.7 copy-start.6
  21.8 0.7 copy-start.7
  22.5 0.7 copy-start.9
  39.9 19.8 %collective-permute-start = (f32[16,128]{1,0:T(8,128)S(1)}, f32[16,128]{1,0:T(8,128)S(1)}, u32[]{:S(2)}, u32[]{:S(2)}) collective-permute-start(f32[16,128]{1,0:T(8,128)S(1)} %slice_reduce_fusion), channel_id=1, source_target_pairs={{0,128},{32,160},{64,192},{96,224},{128,0},{160,32},{192,64},{224,... | collective-permute-start | bytes 24584 | tf_op jit(solution)/shard_map/ppermute | solution.py:410
  42.7 32.1 %copy-start.1 = (f32[3,4096]{1,0:T(4,128)S(1)}, f32[3,4096]{1,0:T(4,128)}, u32[]{:S(2)}) copy-start(f32[3,4096]{1,0:T(4,128)} %refs_2_.3) | copy-start | bytes 147460
  42.7 32.1 %copy-start.3 = (f32[3,4096]{1,0:T(4,128)S(1)}, f32[3,4096]{1,0:T(4,128)}, u32[]{:S(2)}) copy-start(f32[3,4096]{1,0:T(4,128)} %refs_3_.1) | copy-start | bytes 147460
  42.7 32.1 %copy-start.5 = (f32[3,4096]{1,0:T(4,128)S(1)}, f32[3,4096]{1,0:T(4,128)}, u32[]{:S(2)}) copy-start(f32[3,4096]{1,0:T(4,128)} %refs_4_.3) | copy-start | bytes 147460
  42.7 32.1 %copy-start.8 = (f32[3,3]{1,0:T(4,128)S(1)}, f32[3,3]{1,0:T(4,128)}, u32[]{:S(2)}) copy-start(f32[3,3]{1,0:T(4,128)} %refs_1_.3) | copy-start | bytes 112
  42.7 32.1 %copy-start.11 = (s32[32]{0:T(128)S(1)}, s32[32]{0:T(128)}, u32[]{:S(2)}) copy-start(s32[32]{0:T(128)} %refs_0_.3) | copy-start | bytes 388
  59.6 23.0 %copy-start.10 = (s32[2,192]{1,0:T(2,128)S(1)}, s32[2,192]{1,0:T(2,128)}, u32[]{:S(2)}) copy-start(s32[2,192]{1,0:T(2,128)} %pairs.3) | copy-start | bytes 4612
  59.6 23.0 %copy-start.12 = (s32[2,4096]{1,0:T(2,128)S(1)}, s32[2,4096]{1,0:T(2,128)}, u32[]{:S(2)}) copy-start(s32[2,4096]{1,0:T(2,128)} %conn.1) | copy-start | bytes 98308
  59.7 22.9 %all-to-all-start.1 = ((f32[32,16,128]{2,1,0:T(8,128)}), f32[32,16,128]{2,1,0:T(8,128)S(1)}, u32[]{:S(2)}, u32[]{:S(2)}) async-start(f32[32,16,128]{2,1,0:T(8,128)} %get-tuple-element.14), calls=%async_computation.1 | async-start | bytes 524288 | tf_op jit(solution)/shard_map/all_to_all | solution.py:430
  68.2 4.0 %collective-permute-start.1 = (f32[32,128]{1,0:T(8,128)S(1)}, f32[32,128]{1,0:T(8,128)S(1)}, u32[]{:S(2)}, u32[]{:S(2)}) collective-permute-start(f32[32,128]{1,0:T(8,128)S(1)} %pad_maximum_fusion.refs_6_), channel_id=1, source_target_pairs={{0,32},{32,64},{64,96},{96,128},{128,160},{160,192},{192,224},{224... | collective-permute-start | bytes 49160 | tf_op jit(solution)/shard_map/ppermute | solution.py:410
  70.1 3.8 %collective-permute-start.2 = (f32[32,128]{1,0:T(8,128)S(1)}, f32[32,128]{1,0:T(8,128)S(1)}, u32[]{:S(2)}, u32[]{:S(2)}) collective-permute-start(f32[32,128]{1,0:T(8,128)S(1)} %pad_maximum_fusion.refs_6_), channel_id=1, source_target_pairs={{0,64},{32,96},{64,128},{96,160},{128,192},{160,224},{192,0},{224,... | collective-permute-start | bytes 49160 | tf_op jit(solution)/shard_map/ppermute | solution.py:410
  70.1 4.7 %collective-permute-start.3 = (f32[32,128]{1,0:T(8,128)S(1)}, f32[32,128]{1,0:T(8,128)S(1)}, u32[]{:S(2)}, u32[]{:S(2)}) collective-permute-start(f32[32,128]{1,0:T(8,128)S(1)} %pad_maximum_fusion.refs_6_), channel_id=1, source_target_pairs={{0,96},{32,128},{64,160},{96,192},{128,224},{160,0},{192,32},{224,... | collective-permute-start | bytes 49160 | tf_op jit(solution)/shard_map/ppermute | solution.py:410

commit v5 on v4

--- a/solution.py
+++ b/solution.py
@@ -14,10 +14,9 @@
 ROWS = 56
 GROUP = 11
 META = 112
-FEATURES = 48
+FEATURES = 64
 KAPPA = 0.2
 CORE_SQ = 0.25
-HIGH = lax.Precision.HIGHEST
 VMEM = pl.BlockSpec(memory_space=pltpu.VMEM)
 HBM = pl.BlockSpec(memory_space=pltpu.HBM)
 SMEM = pl.BlockSpec(memory_space=pltpu.SMEM)
@@ -67,29 +66,37 @@
     return copies
 
 
+def shift_table(box, shift):
+    steps = [shift[i : i + 1, :].astype(f32) for i in range(3)]
+    rows = [box[c, 0] * steps[0] + box[c, 1] * steps[1] + box[c, 2] * steps[2] for c in range(3)]
+    return jnp.concatenate(rows + [jnp.zeros((5, shift.shape[1]), f32)], axis=0)
+
+
 def pack_kernel(*refs):
     sources, send, scratch = refs[:8], refs[8], refs[9:]
-    pairs, shift, box, fetch, cell, off, tan, bur, sems, table, phi, charged = scratch
+    pairs, box, cell, shift, fetch, off, tan, bur, sems, table, phi, charged = scratch
     for copy in fetch_all(sources, scratch[:8], sems):
         copy.wait()
     fill_table(table, off, tan, bur, 2.0 * KAPPA, KAPPA)
     packed = cell_moments(cell, off, tan, bur, phi, charged)
+    vectors = shift_table(box, shift)
+    peers = send.shape[0]
+    wide = jnp.concatenate([fetch[...].astype(f32), jnp.zeros((SEND, SEG - peers), f32)], axis=1)
+    tall = jnp.concatenate([wide, jnp.zeros((8 - SEND, SEG), f32)], axis=0).T
+    meta = jnp.concatenate(
+        [jnp.zeros((SEG, META), f32), tall, jnp.zeros((SEG, SEG - META - 8), f32)], axis=1
+    )
     row, lane = iota((ROWS - LAST, SEG), 0), iota((ROWS - LAST, SEG), 1)
-
-    def peer(p, carry):
-        rest = packed
+    mark = (row == ROWS - LAST - 1) & (lane >= META)
+    for p in range(peers):
+        rest = jnp.where(mark, meta[p : p + 1, :], packed)
         for s in range(SEND):
             k = p * SEND + s
             at = lane_block(pairs[0, k])
-            vec = shift_rows(shift_of(box, shift, k), (8, SEG))
+            vec = jnp.broadcast_to(vectors[:, k : k + 1], (8, SEG))
             send[p, 8 * s : 8 * s + 8, :] = table[0:8, at] - vec
             rest = jnp.where(row == s, table[8:9, at], rest)
-            mine = (row == ROWS - LAST - 1) & (lane == META + s)
-            rest = jnp.where(mine, fetch[s, p].astype(f32), rest)
         send[p, LAST:ROWS, :] = rest
-        return carry
-
-    lax.fori_loop(0, send.shape[0], peer, 0)
 
 
 def split(value):
@@ -100,60 +107,70 @@
 
 
 def fill_features(table, features):
-    row = iota((8, SEG), 0)
-    first = row < 3
+    first = iota((8, SEG), 0) < 3
+    one, none = jnp.ones((3, SEG), f32), jnp.zeros((1, SEG), f32)
 
     def block(b, carry):
         at = lane_block(b)
-        high, mid, low = split(table[0:8, at])
+        head = table[0:8, at]
+        high, mid, low = split(head)
         last_high, last_mid, _ = split(table[8:9, at])
+        square = split(jnp.sum(jnp.where(first, head * head, 0.0), axis=0, keepdims=True))
         groups = [jnp.where(first, 1.0, high)] * 2
         groups.append(
-            jnp.where(first, 1.0, jnp.where(row < 5, last_high, jnp.where(row == 5, last_mid, 0.0)))
+            jnp.concatenate([one, last_high, last_high, last_mid, square[0], square[1]], axis=0)
         )
         groups.append(jnp.where(first, high, mid))
-        groups.append(jnp.concatenate([mid[0:3], low[0:3], jnp.zeros((2, SEG), f32)], axis=0))
-        groups.append(jnp.zeros((SEG - 40, SEG), f32))
+        groups.append(jnp.concatenate([mid[0:3], low[0:3], square[2], none], axis=0))
+        groups.append(jnp.concatenate([high[0:3], high[0:3], none, none], axis=0))
+        groups.append(jnp.concatenate([mid[0:3], one, none, none], axis=0))
+        groups.append(jnp.zeros((SEG - 56, SEG), f32))
         turned = jnp.concatenate(groups, axis=0).T
         features[b] = turned[:, 0:FEATURES].astype(bf16)
         return carry
 
-    lax.fori_loop(0, features.shape[0], block, 0)
+    lax.fori_loop(0, features.shape[0], block, 0, unroll=4)
 
 
 def weights(head, last):
     row = iota((8, SEG), 0)
+    first, second = row < 3, (row >= 3) & (row < 6)
     high, mid, low = split(head)
     last_high, last_mid, _ = split(last)
+    square = split(jnp.sum(jnp.where(first, head * head, 0.0), axis=0, keepdims=True) + CORE_SQ)
     none = jnp.zeros((8, SEG), f32)
     columns = []
     for i in range(3):
         own = row == i
         parts = [jnp.where(own, part, 0.0) for part in (high, mid, low, -1.0)]
-        parts += [jnp.where(own | (row == i + 3), -1.0, 0.0), none]
+        parts += [jnp.where(own | (row == i + 3), -1.0, 0.0), none, none, none]
         columns.append(jnp.concatenate(parts, axis=0))
-    tail = row >= 3
-    high = jnp.where(tail, high, 0.0)
+    tail = jnp.where(first, 0.0, high)
     edge = jnp.where((row == 3) | (row == 5), last_high, jnp.where(row == 4, last_mid, 0.0))
-    columns.append(
-        jnp.concatenate([high, jnp.where(tail, mid, 0.0), edge, high, none, none], axis=0)
-    )
+    parts = [tail, jnp.where(first, 0.0, mid), edge, tail, none, none, none, none]
+    columns.append(jnp.concatenate(parts, axis=0))
+    twice = [-2.0 * part for part in (high, mid, low)]
+    below = [jnp.concatenate([part[0:3], part[0:3], part[0:2]], axis=0) for part in twice]
+    norm = jnp.where(row == 3, square[0], jnp.where(row == 4, square[1], square[2]))
+    parts = [none, none, jnp.where(row >= 6, 1.0, 0.0), jnp.where(first, twice[0], 0.0)]
+    parts.append(jnp.where(row < 6, below[0], jnp.where(row == 6, 1.0, 0.0)))
+    parts.append(jnp.where(first, twice[1], jnp.where(second, below[2], 0.0)))
+    parts += [jnp.where(first, twice[1], jnp.where(second, norm, 0.0)), none]
+    columns.append(jnp.concatenate(parts, axis=0))
     return jnp.concatenate(columns, axis=1).astype(bf16)
 
 
 def tile(head, last, features, acc, b):
     both = weights(head, last)
     sums = [jnp.zeros((8, SEG), f32) for _ in range(3)]
-    step = 32
+    step = 64
     for start in range(0, SEG, step):
         at = slice(start, start + step)
         made = jnp.dot(features[b, at, :], both, preferred_element_type=f32)
-        gap = [made[:, i * SEG : (i + 1) * SEG] for i in range(3)]
-        dist = gap[0] * gap[0] + CORE_SQ + gap[1] * gap[1] + gap[2] * gap[2]
-        inv = lax.rsqrt(dist)
-        weight = made[:, 3 * SEG :] * (inv * inv * inv)
+        inv = lax.rsqrt(made[:, 4 * SEG :])
+        weight = made[:, 3 * SEG : 4 * SEG] * (inv * inv * inv)
         for c in range(3):
-            push = weight * gap[c]
+            push = weight * made[:, c * SEG : (c + 1) * SEG]
             acc[b, c, at, :] += push
             for r in range(0, step, 8):
                 sums[c] = sums[c] + push[r : r + 8]
@@ -170,7 +187,7 @@
         near[at, :] = others[at, :] - jnp.concatenate(rows, axis=0)
         return carry
 
-    lax.fori_loop(0, acc.shape[0] // 2, pair, 0)
+    lax.fori_loop(0, acc.shape[0] // 2, pair, 0, unroll=True)
 
 
 def clear(acc):
@@ -178,7 +195,7 @@
         acc[b] = jnp.zeros(acc.shape[1:], f32)
         return carry
 
-    lax.fori_loop(0, acc.shape[0], block, 0)
+    lax.fori_loop(0, acc.shape[0], block, 0, unroll=4)
 
 
 def own_kernel(pairs, shift, box, count, off, tan, bur, features, near, table, acc, left_acc):
@@ -223,7 +240,7 @@
         ret[p, 15:16, :] = jnp.zeros((1, SEG), f32)
         return carry
 
-    lax.fori_loop(0, peers, peer, 0)
+    lax.fori_loop(0, peers, peer, 0, unroll=8)
     fold(acc, near, near_own)
 
 
@@ -246,10 +263,26 @@
         phi[k : k + 1, :] = jnp.ones_like(powers[0][1]) if value is None else value
 
 
-def dot_nt(left, right, precision=None):
+def dot_nt(left, right):
     return lax.dot_general(
-        left, right, (((1,), (1,)), ((), ())), precision=precision, preferred_element_type=f32
+        left, right, (((1,), (1,)), ((), ())), preferred_element_type=f32
     )
+
+
+def halves_of(value):
+    high = value.astype(bf16)
+    return high, (value - high.astype(f32)).astype(bf16)
+
+
+def dot_halves(left, right, axis):
+    left_high, left_low = halves_of(left)
+    right_high, right_low = halves_of(right)
+    dims = (((1,), (axis,)), ((), ()))
+    count = right.shape[1 - axis]
+    both = jnp.concatenate([right_high, right_low], axis=1 - axis)
+    made = lax.dot_general(left_high, both, dims, preferred_element_type=f32)
+    made = made[:, :count] + made[:, count:]
+    return made + lax.dot_general(left_low, right_high, dims, preferred_element_type=f32)
 
 
 def cell_moments(cell, off, tan, bur, phi, charged):
@@ -259,7 +292,7 @@
     for b in range(cell.shape[0]):
         part = charge[:, b * SEG : (b + 1) * SEG]
         charged[:, b * SEG : (b + 1) * SEG] = jnp.where(row == cell[b], part, 0.0)
-    part = dot_nt(phi[...], charged[...], HIGH)
+    part = dot_halves(phi[...], charged[...], 1)
     part = jnp.concatenate([part, jnp.zeros((8 * GROUP - NM, CS), f32)], axis=0)
     groups = [part[GROUP * g : GROUP * (g + 1), :] for g in range(8)]
     return jnp.concatenate([jnp.zeros((MOMENTS - LAST, SEG), f32), jnp.concatenate(groups, axis=1)], axis=0)
@@ -269,6 +302,9 @@
     raw, sources, out, scratch = refs[:6], refs[6:10], refs[10], refs[11:]
     cell, stress, off, tan, bur, operator, sems, around, shifted, phi, pots = scratch
     copies = fetch_all(raw, scratch[:6], sems)
+    for copy in copies[:5]:
+        copy.wait()
+    fill_phi(phi, off)
     half = len(sources)
     count = 2 * half
     cells = count * CS
@@ -284,14 +320,13 @@
     shifted[:, 0:NM] = jnp.zeros((CS, NM), f32)
     for o in range(1, cells):
         shifted[:, o * NM : (o + 1) * NM] = around[cells - o : cells - o + CS, 0:NM]
-    for copy in copies[:5]:
-        copy.wait()
-    fill_phi(phi, off)
     copies[5].wait()
-    local_exp = dot_nt(shifted[...], operator[...], HIGH)
-    pots[...] = lax.dot_general(
-        local_exp, phi[...], (((1,), (0,)), ((), ())), precision=HIGH, preferred_element_type=f32
-    )
+    local_exp = dot_halves(operator[...], shifted[...], 1).T
+    high, low = halves_of(local_exp)
+    phi_high, phi_low = halves_of(phi[...])
+    made = jnp.dot(jnp.concatenate([high, low], axis=0), phi_high, preferred_element_type=f32)
+    made = made[0:CS] + made[CS:]
+    pots[...] = made + jnp.dot(high, phi_low, preferred_element_type=f32)
     b = [bur[i : i + 1, :] for i in range(3)]
     t = [tan[i : i + 1, :] for i in range(3)]
     sym = [[0.5 * (stress[i, j] + stress[j, i]) for j in range(3)] for i in range(3)]
@@ -378,19 +413,20 @@
     shape = lambda *dims: jax.ShapeDtypeStruct(dims, f32)
     table = pltpu.VMEM((16, segs), f32)
 
-    raw = [pair_list, image_shift, box_matrix, fetch_table.T, block_cell]
+    raw = [pair_list, box_matrix, block_cell]
     segments = [seg_offset, tangent, burgers]
+    vectors = [image_shift, fetch_table.T, *segments]
     send = call(
         pack_kernel,
         shape(peers, ROWS, SEG),
         [HBM] * 8,
         [pltpu.SMEM(x.shape, x.dtype) for x in raw]
-        + [pltpu.VMEM(x.shape, x.dtype) for x in segments]
+        + [pltpu.VMEM(x.shape, x.dtype) for x in vectors]
         + [pltpu.SemaphoreType.DMA((8,))]
         + [table, pltpu.VMEM((NM, segs), f32), pltpu.VMEM((CS, segs), f32)],
         10**6,
         60,
-    )(*raw, *segments)
+    )(*raw, *vectors)
     recv = lax.all_to_all(send, "bulk", 0, 0, tiled=True)
 
     features, near_own = call(

time: 86.5 us -> 74.2 us (0.86)
  Pallas kernels: 42.9 us -> 24.6 us
  waiting for transfers between devices: 10.2 us -> 15.3 us
    pallas_call x1, Pallas kernels: 16.9 us -> 10.5 us  [local(): call(pair_kernel, (shape(peers, 16, SEG), shape(SEG, SEG)), [VMEM] * 3, [...]
    all_to_all x1, waiting for transfers between devices: 7.63 us -> 12.7 us  [local(): recv = lax.all_to_all(send, 'bulk', 0, 0, tiled=True)]
    pallas_call x1, Pallas kernels: 9.08 us -> 3.98 us  [local(): call(own_kernel, (jax.ShapeDtypeStruct((blocks, SEG, FEATURES), bf16), sh...]
    pallas_call x1, Pallas kernels: 7.76 us -> 4.09 us  [local(): call(far_kernel_body, shape(3, segs), [HBM] * 6 + [VMEM] * half, [pltpu.S...]
    pallas_call x1, Pallas kernels: 5.85 us -> 2.84 us  [local(): call(pack_kernel, shape(peers, ROWS, SEG), [HBM] * 8, [pltpu.SMEM(x.shape...]
  transfers between devices with their start and end apart: 6 -> 6, of which waited for: 3 -> 3; matrix products, arithmetic and copies ran while one was open for 0% -> 0% of each run, Pallas kernels for 39% -> 26%
where the time goes in v5:
time: 74.2 us; the launch traced here: 72.8 us
  starting transfers between devices  27.4 us (37%)
  Pallas kernels  24.6 us (33%)
  waiting for transfers between devices  15.3 us (21%)
  local copies, waits for them, and re-layouts  4.59 us (6%)
  between operations  0.8 us (1%)
    all_to_all x1, waiting for transfers between devices, local(): recv = lax.all_to_all(send, 'bulk', 0, 0, tiled=True)  12.7 us
    all_to_all x1, starting transfers between devices, local(): recv = lax.all_to_all(send, 'bulk', 0, 0, tiled=True)  12 us
    pallas_call x1, Pallas kernels, local(): call(pair_kernel, (shape(peers, 16, SEG), shape(SEG, SEG)), [VMEM] * 3, [...  10.5 us
    all_to_all x1, starting transfers between devices, local(): back = lax.all_to_all(ret, 'bulk', 0, 0, tiled=True)  8.49 us
    ppermute x4, starting transfers between devices, from_slab(): lax.ppermute(value, 'slab', [(s, (s + back) % slabs) for s in range(slabs)])  6.86 us
    unnamed x26, local copies, waits for them, and re-layouts  4.59 us
    pallas_call x1, Pallas kernels, local(): call(far_kernel_body, shape(3, segs), [HBM] * 6 + [VMEM] * half, [pltpu.S...  4.09 us
    pallas_call x1, Pallas kernels, local(): call(own_kernel, (jax.ShapeDtypeStruct((blocks, SEG, FEATURES), bf16), sh...  3.98 us
  transfers between devices with their start and end apart: 6, of which 3 were waited for; matrix products, arithmetic and copies ran while one was open for 0% of the time, Pallas kernels for 26%

profile of v5, /device:TPU:1, one launch (start us, length us, event | category | flops | bytes accessed | tf_op | source)
XLA Modules:
  0.0 72.8 jit_solution(9344226871715976026)
XLA Ops:
  0.0 2.8 %shard_map.118 = f32[32,56,128]{2,1,0:T(8,128)} custom-call(s32[2,192]{1,0:T(2,128)} %pairs.3, f32[3,3]{1,0:T(4,128)} %box.1, s32[32]{0:T(128)} %refs_0_.3, s32[3,192]{1,0:T(4,128)} %shift.1, s32[5,32]{1,0:T(8,128)} %bitcast.1, f32[3,4096]{1,0:T(4,128)} %refs_2_.3, f32[3,4096]{1,0:T(4,128)} %refs_3_.3, f32[3,4096]{1,0:T(4,128)} %refs_4_.1), custom_call_target="tpu_custom_call" | custom-call | flops 1000000 | bytes 1048576 | tf_op jit(solution)/shard_map/pallas_call | solution.py:419
  2.8 12.0 %all-to-all-start = ((f32[32,56,128]{2,1,0:T(8,128)}), f32[32,56,128]{2,1,0:T(8,128)S(1)}, u32[]{:S(2)}, u32[]{:S(2)}) async-start(f32[32,56,128]{2,1,0:T(8,128)} %shard_map.118), calls=%async_computation | async-start | bytes 1835008 | tf_op jit(solution)/shard_map/all_to_all | solution.py:430
  15.5 0.0 copy-start
  15.6 0.8 %copy-done = f32[3,4096]{1,0:T(4,128)S(1)} copy-done((f32[3,4096]{1,0:T(4,128)S(1)}, f32[3,4096]{1,0:T(4,128)}, u32[]{:S(2)}) %copy-start) | copy-done | bytes 49176
  16.4 0.8 %copy-done.2 = f32[3,4096]{1,0:T(4,128)S(1)} copy-done((f32[3,4096]{1,0:T(4,128)S(1)}, f32[3,4096]{1,0:T(4,128)}, u32[]{:S(2)}) %copy-start.2) | copy-done | bytes 49176
  17.2 0.8 %copy-done.4 = f32[3,4096]{1,0:T(4,128)S(1)} copy-done((f32[3,4096]{1,0:T(4,128)S(1)}, f32[3,4096]{1,0:T(4,128)}, u32[]{:S(2)}) %copy-start.4) | copy-done | bytes 49176
  18.1 0.7 copy-done.6
  18.8 0.7 copy-done.7
  19.4 0.7 copy-done.9
  20.1 4.0 %shard_map.119 = (bf16[32,128,64]{2,1,0:T(8,128)(2,1)S(1)}, f32[128,128]{1,0:T(8,128)S(1)}) custom-call(s32[2,192]{1,0:T(2,128)S(1)} %copy-done.9, s32[3,192]{1,0:T(4,128)S(1)} %copy-done.6, f32[3,3]{1,0:T(4,128)S(1)} %copy-done.7, s32[1]{0:T(128)S(6)} %copy.13.count, f32[3,4096]{1,0:T(4,128)S(1)} %copy-done, f32[3,4096]{1,0:T(4,128)S(1)} %copy-done.2, ...), custom_call_target="tpu_custom_call" | custom-call | flops 1000000000 | bytes 1048576 | tf_op jit(solution)/shard_map/pallas_call | solution.py:432
  24.1 12.7 %all-to-all-done.recv = f32[32,56,128]{2,1,0:T(8,128)S(1)} async-done(((f32[32,56,128]{2,1,0:T(8,128)}), f32[32,56,128]{2,1,0:T(8,128)S(1)}, u32[]{:S(2)}, u32[]{:S(2)}) %all-to-all-start) | async-done | bytes 917536 | tf_op jit(solution)/shard_map/all_to_all | solution.py:430
  36.9 2.8 %collective-permute-start = (f32[16,128]{1,0:T(8,128)S(1)}, f32[16,128]{1,0:T(8,128)S(1)}, u32[]{:S(2)}, u32[]{:S(2)}) collective-permute-start(f32[16,128]{1,0:T(8,128)S(1)} %slice_reduce_fusion), channel_id=1, source_target_pairs={{0,128},{32,160},{64,192},{96,224},{128,0},{160,32},{192,64},{224,... | collective-permute-start | bytes 24584 | tf_op jit(solution)/shard_map/ppermute | solution.py:446
  39.7 0.0 copy-start.11
  39.7 10.5 %shard_map.120 = (f32[32,16,128]{2,1,0:T(8,128)}, f32[128,128]{1,0:T(8,128)S(1)}) custom-call(f32[32,56,128]{2,1,0:T(8,128)S(1)} %all-to-all-done.recv, bf16[32,128,64]{2,1,0:T(8,128)(2,1)S(1)} %get-tuple-element.11.features, f32[128,128]{1,0:T(8,128)S(1)} %get-tuple-element.12.near_own), custom_call_target="tpu_custom_call" | custom-call | flops 10000000000 | bytes 1048576 | tf_op jit(solution)/shard_map/pallas_call | solution.py:452
  50.3 0.0 copy-start.10
  50.3 0.0 copy-start.12
  50.3 0.0 collective-permute-done
  50.3 8.5 %all-to-all-start.1 = ((f32[32,16,128]{2,1,0:T(8,128)}), f32[32,16,128]{2,1,0:T(8,128)S(1)}, u32[]{:S(2)}, u32[]{:S(2)}) async-start(f32[32,16,128]{2,1,0:T(8,128)} %get-tuple-element.14), calls=%async_computation.1 | async-start | bytes 524288 | tf_op jit(solution)/shard_map/all_to_all | solution.py:466
  58.8 1.9 %collective-permute-start.1 = (f32[32,128]{1,0:T(8,128)S(1)}, f32[32,128]{1,0:T(8,128)S(1)}, u32[]{:S(2)}, u32[]{:S(2)}) collective-permute-start(f32[32,128]{1,0:T(8,128)S(1)} %pad_maximum_fusion.refs_6_), channel_id=1, source_target_pairs={{0,32},{32,64},{64,96},{96,128},{128,160},{160,192},{192,224},{224... | collective-permute-start | bytes 49160 | tf_op jit(solution)/shard_map/ppermute | solution.py:446
  60.7 2.1 %collective-permute-start.3 = (f32[32,128]{1,0:T(8,128)S(1)}, f32[32,128]{1,0:T(8,128)S(1)}, u32[]{:S(2)}, u32[]{:S(2)}) collective-permute-start(f32[32,128]{1,0:T(8,128)S(1)} %pad_maximum_fusion.refs_6_), channel_id=1, source_target_pairs={{0,96},{32,128},{64,160},{96,192},{128,224},{160,0},{192,32},{224,... | collective-permute-start | bytes 49160 | tf_op jit(solution)/shard_map/ppermute | solution.py:446
  62.9 1.7 %collective-permute-done.2.refs_8_ = f32[32,128]{1,0:T(8,128)S(1)} collective-permute-done((f32[32,128]{1,0:T(8,128)S(1)}, f32[32,128]{1,0:T(8,128)S(1)}, u32[]{:S(2)}, u32[]{:S(2)}) %collective-permute-start.2) | collective-permute-done | bytes 16416 | tf_op jit(solution)/shard_map/ppermute | solution.py:446
  64.5 0.9 %collective-permute-done.3.refs_9_ = f32[32,128]{1,0:T(8,128)S(1)} collective-permute-done((f32[32,128]{1,0:T(8,128)S(1)}, f32[32,128]{1,0:T(8,128)S(1)}, u32[]{:S(2)}, u32[]{:S(2)}) %collective-permute-start.3) | collective-permute-done | bytes 16416 | tf_op jit(solution)/shard_map/ppermute | solution.py:446
  65.5 4.1 %shard_map.121.far = f32[3,4096]{1,0:T(4,128)S(1)} custom-call(s32[32]{0:T(128)S(1)} %copy-done.11, f32[3,3]{1,0:T(4,128)S(1)} %copy-done.8, f32[3,4096]{1,0:T(4,128)S(1)} %copy-done.1, f32[3,4096]{1,0:T(4,128)S(1)} %copy-done.3, f32[3,4096]{1,0:T(4,128)S(1)} %copy-done.5, f32[84,10752]{1,0:T(8,128)} %refs_5_.3, f32[32,128]{1,0:T(8,128)S(1)} %pad_maximum_fusion.refs_6_, ...), custom_call_target="tpu_custom_call" | custom-call | flops 1000000000 | bytes 1048576 | tf_op jit(solution)/shard_map/pallas_call | solution.py:470
  69.6 3.2 %shard_map.122 = f32[3,4096]{1,0:T(4,128)} custom-call(s32[2,192]{1,0:T(2,128)S(1)} %copy-done.10, f32[32,16,128]{2,1,0:T(8,128)S(1)} %all-to-all-done.1.back, f32[128,128]{1,0:T(8,128)S(1)} %get-tuple-element.15.near_all, f32[3,4096]{1,0:T(4,128)S(1)} %shard_map.121.far, s32[2,4096]{1,0:T(2,128)S(1)} %copy-done.12), custom_call_target="tpu_custom_call" | custom-call | flops 1000000000 | bytes 1048576 | tf_op jit(solution)/shard_map/pallas_call | solution.py:487
  (21 shorter events, 0.1 us)
Async XLA Ops:
  2.8 34.0 %all-to-all-start = ((f32[32,56,128]{2,1,0:T(8,128)}), f32[32,56,128]{2,1,0:T(8,128)S(1)}, u32[]{:S(2)}, u32[]{:S(2)}) async-start(f32[32,56,128]{2,1,0:T(8,128)} %shard_map.118), calls=%async_computation | async-start | bytes 1835008 | tf_op jit(solution)/shard_map/all_to_all | solution.py:430
  15.5 0.8 %copy-start = (f32[3,4096]{1,0:T(4,128)S(1)}, f32[3,4096]{1,0:T(4,128)}, u32[]{:S(2)}) copy-start(f32[3,4096]{1,0:T(4,128)} %refs_2_.3) | copy-start | bytes 147460
  16.4 0.8 %copy-start.2 = (f32[3,4096]{1,0:T(4,128)S(1)}, f32[3,4096]{1,0:T(4,128)}, u32[]{:S(2)}) copy-start(f32[3,4096]{1,0:T(4,128)} %refs_3_.3) | copy-start | bytes 147460
  17.2 0.8 %copy-start.4 = (f32[3,4096]{1,0:T(4,128)S(1)}, f32[3,4096]{1,0:T(4,128)}, u32[]{:S(2)}) copy-start(f32[3,4096]{1,0:T(4,128)} %refs_4_.1) | copy-start | bytes 147460
  18.1 0.7 copy-start.6
  18.8 0.7 copy-start.7
  19.4 0.7 copy-start.9
  36.9 13.4 %collective-permute-start = (f32[16,128]{1,0:T(8,128)S(1)}, f32[16,128]{1,0:T(8,128)S(1)}, u32[]{:S(2)}, u32[]{:S(2)}) collective-permute-start(f32[16,128]{1,0:T(8,128)S(1)} %slice_reduce_fusion), channel_id=1, source_target_pairs={{0,128},{32,160},{64,192},{96,224},{128,0},{160,32},{192,64},{224,... | collective-permute-start | bytes 24584 | tf_op jit(solution)/shard_map/ppermute | solution.py:446
  39.7 25.7 %copy-start.1 = (f32[3,4096]{1,0:T(4,128)S(1)}, f32[3,4096]{1,0:T(4,128)}, u32[]{:S(2)}) copy-start(f32[3,4096]{1,0:T(4,128)} %refs_2_.3) | copy-start | bytes 147460
  39.7 25.7 %copy-start.3 = (f32[3,4096]{1,0:T(4,128)S(1)}, f32[3,4096]{1,0:T(4,128)}, u32[]{:S(2)}) copy-start(f32[3,4096]{1,0:T(4,128)} %refs_3_.3) | copy-start | bytes 147460
  39.7 25.7 %copy-start.5 = (f32[3,4096]{1,0:T(4,128)S(1)}, f32[3,4096]{1,0:T(4,128)}, u32[]{:S(2)}) copy-start(f32[3,4096]{1,0:T(4,128)} %refs_4_.1) | copy-start | bytes 147460
  39.7 25.7 %copy-start.8 = (f32[3,3]{1,0:T(4,128)S(1)}, f32[3,3]{1,0:T(4,128)}, u32[]{:S(2)}) copy-start(f32[3,3]{1,0:T(4,128)} %refs_1_.3) | copy-start | bytes 112
  39.7 25.7 %copy-start.11 = (s32[32]{0:T(128)S(1)}, s32[32]{0:T(128)}, u32[]{:S(2)}) copy-start(s32[32]{0:T(128)} %refs_0_.3) | copy-start | bytes 388
  50.3 19.3 %copy-start.10 = (s32[2,192]{1,0:T(2,128)S(1)}, s32[2,192]{1,0:T(2,128)}, u32[]{:S(2)}) copy-start(s32[2,192]{1,0:T(2,128)} %pairs.3) | copy-start | bytes 4612
  50.3 19.3 %copy-start.12 = (s32[2,4096]{1,0:T(2,128)S(1)}, s32[2,4096]{1,0:T(2,128)}, u32[]{:S(2)}) copy-start(s32[2,4096]{1,0:T(2,128)} %conn.1) | copy-start | bytes 98308
  50.3 19.3 %all-to-all-start.1 = ((f32[32,16,128]{2,1,0:T(8,128)}), f32[32,16,128]{2,1,0:T(8,128)S(1)}, u32[]{:S(2)}, u32[]{:S(2)}) async-start(f32[32,16,128]{2,1,0:T(8,128)} %get-tuple-element.14), calls=%async_computation.1 | async-start | bytes 524288 | tf_op jit(solution)/shard_map/all_to_all | solution.py:466
  58.8 4.0 %collective-permute-start.1 = (f32[32,128]{1,0:T(8,128)S(1)}, f32[32,128]{1,0:T(8,128)S(1)}, u32[]{:S(2)}, u32[]{:S(2)}) collective-permute-start(f32[32,128]{1,0:T(8,128)S(1)} %pad_maximum_fusion.refs_6_), channel_id=1, source_target_pairs={{0,32},{32,64},{64,96},{96,128},{128,160},{160,192},{192,224},{224... | collective-permute-start | bytes 49160 | tf_op jit(solution)/shard_map/ppermute | solution.py:446
  60.7 3.8 %collective-permute-start.2 = (f32[32,128]{1,0:T(8,128)S(1)}, f32[32,128]{1,0:T(8,128)S(1)}, u32[]{:S(2)}, u32[]{:S(2)}) collective-permute-start(f32[32,128]{1,0:T(8,128)S(1)} %pad_maximum_fusion.refs_6_), channel_id=1, source_target_pairs={{0,64},{32,96},{64,128},{96,160},{128,192},{160,224},{192,0},{224,... | collective-permute-start | bytes 49160 | tf_op jit(solution)/shard_map/ppermute | solution.py:446
  60.7 4.7 %collective-permute-start.3 = (f32[32,128]{1,0:T(8,128)S(1)}, f32[32,128]{1,0:T(8,128)S(1)}, u32[]{:S(2)}, u32[]{:S(2)}) collective-permute-start(f32[32,128]{1,0:T(8,128)S(1)} %pad_maximum_fusion.refs_6_), channel_id=1, source_target_pairs={{0,96},{32,128},{64,160},{96,192},{128,224},{160,0},{192,32},{224,... | collective-permute-start | bytes 49160 | tf_op jit(solution)/shard_map/ppermute | solution.py:446

commit v6 on v5

--- a/solution.py
+++ b/solution.py
@@ -198,7 +198,25 @@
     lax.fori_loop(0, acc.shape[0], block, 0, unroll=4)
 
 
-def own_kernel(pairs, shift, box, count, off, tan, bur, features, near, table, acc, left_acc):
+def left_rows(blocks, out_shape):
+    slots = blocks.shape[1]
+    slot, lane = iota((slots, out_shape[1]), 0), iota((slots, out_shape[1]), 1)
+    peer, rest = lane >> 4, lane & 15
+    third = (rest >= 3).astype(jnp.int32) + (rest >= 6) + (rest >= 9) + (rest >= 12)
+    pick = (slot == SEND * peer + third) & (rest < 15)
+    tall = jnp.broadcast_to(blocks.astype(f32), (16, slots)).astype(bf16)
+    found = jnp.dot(tall, jnp.where(pick, 1.0, 0.0).astype(bf16), preferred_element_type=f32)
+    lane = iota(out_shape, 1)
+    rest = lane & 15
+    third = (rest >= 3).astype(jnp.int32) + (rest >= 6) + (rest >= 9) + (rest >= 12)
+    row = 4 * found[0 : out_shape[0]].astype(jnp.int32) + rest - 3 * third
+    return jnp.where(rest < 15, row, -1)
+
+
+def own_kernel(
+    pairs, shift, box, count, off, tan, bur, pairs_row, features, near, left, table, acc, left_acc
+):
+    left[...] = left_rows(pairs_row[0:1, :], left.shape)
     clear(acc)
     left_acc[...] = jnp.zeros_like(left_acc)
     fill_table(table, off, tan, bur, 1.0, 1.0)
@@ -341,27 +359,22 @@
         out[:, at] += jnp.sum(mine, axis=0, keepdims=True) * bur[:, at]
 
 
-def final_kernel(pairs, back, near_all, far, conn, out, left_acc, force, halves):
-    clear(left_acc)
-
-    def peer(p, carry):
-        for s in range(SEND):
-            a = pairs[0, p * SEND + s]
-            left_acc[a, 0:3, :] += back[p, 3 * s : 3 * s + 3, :]
-        return carry
-
-    lax.fori_loop(0, back.shape[0], peer, 0)
-    for b in range(left_acc.shape[0]):
+def final_kernel(back, near_all, far, conn, left, out, force, halves):
+    groups = conn.shape[1] // SEG
+    returned = back[...].reshape(back.shape[0] * 16, SEG)
+    spread = jnp.where(iota((SEG, returned.shape[0]), 0) == left[0:1, :], 1.0, 0.0).astype(bf16)
+    high, low = halves_of(returned)
+    near = near_all[...] + jnp.dot(spread, high, preferred_element_type=f32)
+    near = near + jnp.dot(spread, low, preferred_element_type=f32)
+    for b in range(groups):
         at = slice(b * SEG, (b + 1) * SEG)
-        near = near_all[4 * b : 4 * b + 3, :]
-        force[0:3, at] = 0.5 * (far[:, at] + near + left_acc[b, 0:3, :])
+        force[0:3, at] = 0.5 * (far[:, at] + near[4 * b : 4 * b + 3, :])
     value = force[0:3, :]
     high = value.astype(bf16).astype(f32)
     halves[0:3, :] = high
     halves[3:6, :] = value - high
     chunk = 1024
     segs = conn.shape[1]
-    groups = segs // SEG
     total = jnp.zeros((6 * groups, SEG), f32)
     low_row, high_row = iota((SEG, chunk), 0), iota((groups, chunk), 0)
     for end in range(2):
@@ -429,10 +442,14 @@
     )(*raw, *vectors)
     recv = lax.all_to_all(send, "bulk", 0, 0, tiled=True)
 
-    features, near_own = call(
+    features, near_own, left = call(
         own_kernel,
-        (jax.ShapeDtypeStruct((blocks, SEG, FEATURES), bf16), shape(SEG, SEG)),
-        [SMEM] * 4 + [VMEM] * 3,
+        (
+            jax.ShapeDtypeStruct((blocks, SEG, FEATURES), bf16),
+            shape(SEG, SEG),
+            jax.ShapeDtypeStruct((8, peers * 16), jnp.int32),
+        ),
+        [SMEM] * 4 + [VMEM] * 4,
         [
             table,
             pltpu.VMEM((blocks, 3, SEG, SEG), f32),
@@ -440,7 +457,7 @@
         ],
         10**9,
         12,
-    )(pair_list, image_shift, box_matrix, pair_count, *segments)
+    )(pair_list, image_shift, box_matrix, pair_count, *segments, pair_list)
 
     def from_slab(value, back):
         return lax.ppermute(value, "slab", [(s, (s + back) % slabs) for s in range(slabs)])
@@ -487,11 +504,11 @@
     return call(
         final_kernel,
         shape(3, segs),
-        [SMEM] + [VMEM] * 4,
-        [pltpu.VMEM((blocks, 8, SEG), f32), pltpu.VMEM((8, segs), f32), pltpu.VMEM((8, segs), f32)],
+        [VMEM] * 5,
+        [pltpu.VMEM((8, segs), f32), pltpu.VMEM((8, segs), f32)],
         10**9,
         24,
-    )(pair_list, back, near, far, node_conn)
+    )(back, near, far, node_conn, left)
 
 
 def solution(mesh):

time: 74.2 us -> 72.7 us (0.980)
  waiting for transfers between devices: 15.3 us -> 9.05 us
  Pallas kernels: 24.6 us -> 29.4 us
    all_to_all x1, waiting for transfers between devices: 12.7 us -> 6.44 us  [local(): recv = lax.all_to_all(send, 'bulk', 0, 0, tiled=True)]
    pallas_call x1, Pallas kernels: 3.98 us -> 10.3 us  [local(): call(own_kernel, (jax.ShapeDtypeStruct((blocks, SEG, FEATURES), bf16), sh...]
    pallas_call x1, Pallas kernels: 3.16 us -> 1.83 us  [local(): call(final_kernel, shape(3, segs), [VMEM] * 5, [pltpu.VMEM((8, segs), f32...]
    unnamed x26 -> x24, local copies, waits for them, and re-layouts: 4.59 us -> 4.59 us
  transfers between devices with their start and end apart: 6 -> 6, of which waited for: 3 -> 3; matrix products, arithmetic and copies ran while one was open for 0% -> 0% of each run, Pallas kernels for 26% -> 35%
where the time goes in v6:
time: 72.7 us; the launch traced here: 71.3 us
  Pallas kernels  29.4 us (40%)
  starting transfers between devices  27.4 us (38%)
  waiting for transfers between devices  9.05 us (12%)
  local copies, waits for them, and re-layouts  4.59 us (6%)
  between operations  0.79 us (1%)
    all_to_all x1, starting transfers between devices, local(): recv = lax.all_to_all(send, 'bulk', 0, 0, tiled=True)  12 us
    pallas_call x1, Pallas kernels, local(): call(pair_kernel, (shape(peers, 16, SEG), shape(SEG, SEG)), [VMEM] * 3, [...  10.4 us
    pallas_call x1, Pallas kernels, local(): call(own_kernel, (jax.ShapeDtypeStruct((blocks, SEG, FEATURES), bf16), sh...  10.3 us
    all_to_all x1, starting transfers between devices, local(): back = lax.all_to_all(ret, 'bulk', 0, 0, tiled=True)  8.47 us
    ppermute x4, starting transfers between devices, from_slab(): lax.ppermute(value, 'slab', [(s, (s + back) % slabs) for s in range(slabs)])  6.88 us
    all_to_all x1, waiting for transfers between devices, local(): recv = lax.all_to_all(send, 'bulk', 0, 0, tiled=True)  6.44 us
    unnamed x24, local copies, waits for them, and re-layouts  4.59 us
    pallas_call x1, Pallas kernels, local(): call(far_kernel_body, shape(3, segs), [HBM] * 6 + [VMEM] * half, [pltpu.S...  4.09 us
  transfers between devices with their start and end apart: 6, of which 3 were waited for; matrix products, arithmetic and copies ran while one was open for 0% of the time, Pallas kernels for 35%

profile of v6, /device:TPU:1, one launch (start us, length us, event | category | flops | bytes accessed | tf_op | source)
XLA Modules:
  0.0 71.3 jit_solution(3379904551132411425)
XLA Ops:
  0.0 2.8 %shard_map.118 = f32[32,56,128]{2,1,0:T(8,128)} custom-call(s32[2,192]{1,0:T(2,128)} %pairs_row.1, f32[3,3]{1,0:T(4,128)} %box.1, s32[32]{0:T(128)} %refs_0_.3, s32[3,192]{1,0:T(4,128)} %shift.1, s32[5,32]{1,0:T(8,128)} %bitcast.1, f32[3,4096]{1,0:T(4,128)} %refs_2_.3, f32[3,4096]{1,0:T(4,128)} %refs_3_.3, f32[3,4096]{1,0:T(4,128)} %refs_4_.1), custom_call_target="tpu_custom_call" | custom-call | flops 1000000 | bytes 1048576 | tf_op jit(solution)/shard_map/pallas_call | solution.py:432
  2.8 12.0 %all-to-all-start = ((f32[32,56,128]{2,1,0:T(8,128)}), f32[32,56,128]{2,1,0:T(8,128)S(1)}, u32[]{:S(2)}, u32[]{:S(2)}) async-start(f32[32,56,128]{2,1,0:T(8,128)} %shard_map.118), calls=%async_computation | async-start | bytes 1835008 | tf_op jit(solution)/shard_map/all_to_all | solution.py:443
  15.5 0.0 copy-start
  15.6 0.8 %copy-done = f32[3,4096]{1,0:T(4,128)S(1)} copy-done((f32[3,4096]{1,0:T(4,128)S(1)}, f32[3,4096]{1,0:T(4,128)}, u32[]{:S(2)}) %copy-start) | copy-done | bytes 49176
  16.4 0.8 %copy-done.2 = f32[3,4096]{1,0:T(4,128)S(1)} copy-done((f32[3,4096]{1,0:T(4,128)S(1)}, f32[3,4096]{1,0:T(4,128)}, u32[]{:S(2)}) %copy-start.2) | copy-done | bytes 49176
  17.2 0.8 %copy-done.4 = f32[3,4096]{1,0:T(4,128)S(1)} copy-done((f32[3,4096]{1,0:T(4,128)S(1)}, f32[3,4096]{1,0:T(4,128)}, u32[]{:S(2)}) %copy-start.4) | copy-done | bytes 49176
  18.1 0.7 copy-done.6
  18.8 0.7 copy-done.7
  19.4 0.7 copy-done.8
  20.1 10.3 %shard_map.119 = (bf16[32,128,64]{2,1,0:T(8,128)(2,1)S(1)}, f32[128,128]{1,0:T(8,128)S(1)}, s32[8,512]{1,0:T(8,128)S(1)}) custom-call(s32[2,192]{1,0:T(2,128)S(1)} %copy-done.7, s32[3,192]{1,0:T(4,128)S(1)} %copy-done.6, f32[3,3]{1,0:T(4,128)S(1)} %copy-done.8, s32[1]{0:T(128)S(6)} %copy.13.count, f32[3,4096]{1,0:T(4,128)S(1)} %copy-done, ...), custom_call_target="tpu_custom_call" | custom-call | flops 1000000000 | bytes 1048576 | tf_op jit(solution)/shard_map/pallas_call | solution.py:445
  30.4 6.4 %all-to-all-done.recv = f32[32,56,128]{2,1,0:T(8,128)S(1)} async-done(((f32[32,56,128]{2,1,0:T(8,128)}), f32[32,56,128]{2,1,0:T(8,128)S(1)}, u32[]{:S(2)}, u32[]{:S(2)}) %all-to-all-start) | async-done | bytes 917536 | tf_op jit(solution)/shard_map/all_to_all | solution.py:443
  36.9 2.8 %collective-permute-start = (f32[16,128]{1,0:T(8,128)S(1)}, f32[16,128]{1,0:T(8,128)S(1)}, u32[]{:S(2)}, u32[]{:S(2)}) collective-permute-start(f32[16,128]{1,0:T(8,128)S(1)} %slice_reduce_fusion), channel_id=1, source_target_pairs={{0,128},{32,160},{64,192},{96,224},{128,0},{160,32},{192,64},{224,... | collective-permute-start | bytes 24584 | tf_op jit(solution)/shard_map/ppermute | solution.py:463
  39.7 0.0 copy-start.10
  39.7 10.4 %shard_map.120 = (f32[32,16,128]{2,1,0:T(8,128)}, f32[128,128]{1,0:T(8,128)S(1)}) custom-call(f32[32,56,128]{2,1,0:T(8,128)S(1)} %all-to-all-done.recv, bf16[32,128,64]{2,1,0:T(8,128)(2,1)S(1)} %get-tuple-element.12.features, f32[128,128]{1,0:T(8,128)S(1)} %get-tuple-element.13.near_own), custom_call_target="tpu_custom_call" | custom-call | flops 10000000000 | bytes 1048576 | tf_op jit(solution)/shard_map/pallas_call | solution.py:469
  50.1 0.0 copy-start.11
  50.1 0.0 collective-permute-done
  50.2 8.5 %all-to-all-start.1 = ((f32[32,16,128]{2,1,0:T(8,128)}), f32[32,16,128]{2,1,0:T(8,128)S(1)}, u32[]{:S(2)}, u32[]{:S(2)}) async-start(f32[32,16,128]{2,1,0:T(8,128)} %get-tuple-element.15), calls=%async_computation.1 | async-start | bytes 524288 | tf_op jit(solution)/shard_map/all_to_all | solution.py:483
  58.6 1.9 %collective-permute-start.1 = (f32[32,128]{1,0:T(8,128)S(1)}, f32[32,128]{1,0:T(8,128)S(1)}, u32[]{:S(2)}, u32[]{:S(2)}) collective-permute-start(f32[32,128]{1,0:T(8,128)S(1)} %pad_maximum_fusion.refs_6_), channel_id=1, source_target_pairs={{0,32},{32,64},{64,96},{96,128},{128,160},{160,192},{192,224},{224... | collective-permute-start | bytes 49160 | tf_op jit(solution)/shard_map/ppermute | solution.py:463
  60.6 0.0 collective-permute-start.2
  60.6 2.1 %collective-permute-start.3 = (f32[32,128]{1,0:T(8,128)S(1)}, f32[32,128]{1,0:T(8,128)S(1)}, u32[]{:S(2)}, u32[]{:S(2)}) collective-permute-start(f32[32,128]{1,0:T(8,128)S(1)} %pad_maximum_fusion.refs_6_), channel_id=1, source_target_pairs={{0,96},{32,128},{64,160},{96,192},{128,224},{160,0},{192,32},{224,... | collective-permute-start | bytes 49160 | tf_op jit(solution)/shard_map/ppermute | solution.py:463
  62.7 1.7 %collective-permute-done.2.refs_8_ = f32[32,128]{1,0:T(8,128)S(1)} collective-permute-done((f32[32,128]{1,0:T(8,128)S(1)}, f32[32,128]{1,0:T(8,128)S(1)}, u32[]{:S(2)}, u32[]{:S(2)}) %collective-permute-start.2) | collective-permute-done | bytes 16416 | tf_op jit(solution)/shard_map/ppermute | solution.py:463
  64.4 0.9 %collective-permute-done.3.refs_9_ = f32[32,128]{1,0:T(8,128)S(1)} collective-permute-done((f32[32,128]{1,0:T(8,128)S(1)}, f32[32,128]{1,0:T(8,128)S(1)}, u32[]{:S(2)}, u32[]{:S(2)}) %collective-permute-start.3) | collective-permute-done | bytes 16416 | tf_op jit(solution)/shard_map/ppermute | solution.py:463
  65.3 4.1 %shard_map.121.far = f32[3,4096]{1,0:T(4,128)S(1)} custom-call(s32[32]{0:T(128)S(1)} %copy-done.10, f32[3,3]{1,0:T(4,128)S(1)} %copy-done.9, f32[3,4096]{1,0:T(4,128)S(1)} %copy-done.1, f32[3,4096]{1,0:T(4,128)S(1)} %copy-done.3, f32[3,4096]{1,0:T(4,128)S(1)} %copy-done.5, f32[84,10752]{1,0:T(8,128)} %refs_5_.3, f32[32,128]{1,0:T(8,128)S(1)} %pad_maximum_fusion.refs_6_, ...), custom_call_target="tpu_custom_call" | custom-call | flops 1000000000 | bytes 1048576 | tf_op jit(solution)/shard_map/pallas_call | solution.py:487
  69.5 1.8 %shard_map.122 = f32[3,4096]{1,0:T(4,128)} custom-call(f32[32,16,128]{2,1,0:T(8,128)S(1)} %all-to-all-done.1.back, f32[128,128]{1,0:T(8,128)S(1)} %get-tuple-element.16.near_all, f32[3,4096]{1,0:T(4,128)S(1)} %shard_map.121.far, s32[2,4096]{1,0:T(2,128)S(1)} %copy-done.11, s32[8,512]{1,0:T(8,128)S(1)} %get-tuple-element.18.left), custom_call_target="tpu_custom_call" | custom-call | flops 1000000000 | bytes 1048576 | tf_op jit(solution)/shard_map/pallas_call | solution.py:504
  (19 shorter events, 0.1 us)
Async XLA Ops:
  2.8 34.0 %all-to-all-start = ((f32[32,56,128]{2,1,0:T(8,128)}), f32[32,56,128]{2,1,0:T(8,128)S(1)}, u32[]{:S(2)}, u32[]{:S(2)}) async-start(f32[32,56,128]{2,1,0:T(8,128)} %shard_map.118), calls=%async_computation | async-start | bytes 1835008 | tf_op jit(solution)/shard_map/all_to_all | solution.py:443
  15.5 0.8 %copy-start = (f32[3,4096]{1,0:T(4,128)S(1)}, f32[3,4096]{1,0:T(4,128)}, u32[]{:S(2)}) copy-start(f32[3,4096]{1,0:T(4,128)} %refs_2_.3) | copy-start | bytes 147460
  16.4 0.8 %copy-start.2 = (f32[3,4096]{1,0:T(4,128)S(1)}, f32[3,4096]{1,0:T(4,128)}, u32[]{:S(2)}) copy-start(f32[3,4096]{1,0:T(4,128)} %refs_3_.3) | copy-start | bytes 147460
  17.2 0.8 %copy-start.4 = (f32[3,4096]{1,0:T(4,128)S(1)}, f32[3,4096]{1,0:T(4,128)}, u32[]{:S(2)}) copy-start(f32[3,4096]{1,0:T(4,128)} %refs_4_.1) | copy-start | bytes 147460
  18.1 0.7 copy-start.6
  18.8 0.7 copy-start.7
  19.4 0.7 copy-start.8
  36.9 13.3 %collective-permute-start = (f32[16,128]{1,0:T(8,128)S(1)}, f32[16,128]{1,0:T(8,128)S(1)}, u32[]{:S(2)}, u32[]{:S(2)}) collective-permute-start(f32[16,128]{1,0:T(8,128)S(1)} %slice_reduce_fusion), channel_id=1, source_target_pairs={{0,128},{32,160},{64,192},{96,224},{128,0},{160,32},{192,64},{224,... | collective-permute-start | bytes 24584 | tf_op jit(solution)/shard_map/ppermute | solution.py:463
  39.7 25.6 %copy-start.1 = (f32[3,4096]{1,0:T(4,128)S(1)}, f32[3,4096]{1,0:T(4,128)}, u32[]{:S(2)}) copy-start(f32[3,4096]{1,0:T(4,128)} %refs_2_.3) | copy-start | bytes 147460
  39.7 25.6 %copy-start.3 = (f32[3,4096]{1,0:T(4,128)S(1)}, f32[3,4096]{1,0:T(4,128)}, u32[]{:S(2)}) copy-start(f32[3,4096]{1,0:T(4,128)} %refs_3_.3) | copy-start | bytes 147460
  39.7 25.6 %copy-start.5 = (f32[3,4096]{1,0:T(4,128)S(1)}, f32[3,4096]{1,0:T(4,128)}, u32[]{:S(2)}) copy-start(f32[3,4096]{1,0:T(4,128)} %refs_4_.1) | copy-start | bytes 147460
  39.7 25.6 %copy-start.9 = (f32[3,3]{1,0:T(4,128)S(1)}, f32[3,3]{1,0:T(4,128)}, u32[]{:S(2)}) copy-start(f32[3,3]{1,0:T(4,128)} %refs_1_.3) | copy-start | bytes 112
  39.7 25.6 %copy-start.10 = (s32[32]{0:T(128)S(1)}, s32[32]{0:T(128)}, u32[]{:S(2)}) copy-start(s32[32]{0:T(128)} %refs_0_.3) | copy-start | bytes 388
  50.1 19.3 %copy-start.11 = (s32[2,4096]{1,0:T(2,128)S(1)}, s32[2,4096]{1,0:T(2,128)}, u32[]{:S(2)}) copy-start(s32[2,4096]{1,0:T(2,128)} %conn.1) | copy-start | bytes 98308
  50.2 19.3 %all-to-all-start.1 = ((f32[32,16,128]{2,1,0:T(8,128)}), f32[32,16,128]{2,1,0:T(8,128)S(1)}, u32[]{:S(2)}, u32[]{:S(2)}) async-start(f32[32,16,128]{2,1,0:T(8,128)} %get-tuple-element.15), calls=%async_computation.1 | async-start | bytes 524288 | tf_op jit(solution)/shard_map/all_to_all | solution.py:483
  58.6 4.1 %collective-permute-start.1 = (f32[32,128]{1,0:T(8,128)S(1)}, f32[32,128]{1,0:T(8,128)S(1)}, u32[]{:S(2)}, u32[]{:S(2)}) collective-permute-start(f32[32,128]{1,0:T(8,128)S(1)} %pad_maximum_fusion.refs_6_), channel_id=1, source_target_pairs={{0,32},{32,64},{64,96},{96,128},{128,160},{160,192},{192,224},{224... | collective-permute-start | bytes 49160 | tf_op jit(solution)/shard_map/ppermute | solution.py:463
  60.6 3.8 %collective-permute-start.2 = (f32[32,128]{1,0:T(8,128)S(1)}, f32[32,128]{1,0:T(8,128)S(1)}, u32[]{:S(2)}, u32[]{:S(2)}) collective-permute-start(f32[32,128]{1,0:T(8,128)S(1)} %pad_maximum_fusion.refs_6_), channel_id=1, source_target_pairs={{0,64},{32,96},{64,128},{96,160},{128,192},{160,224},{192,0},{224,... | collective-permute-start | bytes 49160 | tf_op jit(solution)/shard_map/ppermute | solution.py:463
  60.6 4.7 %collective-permute-start.3 = (f32[32,128]{1,0:T(8,128)S(1)}, f32[32,128]{1,0:T(8,128)S(1)}, u32[]{:S(2)}, u32[]{:S(2)}) collective-permute-start(f32[32,128]{1,0:T(8,128)S(1)} %pad_maximum_fusion.refs_6_), channel_id=1, source_target_pairs={{0,96},{32,128},{64,160},{96,192},{128,224},{160,0},{192,32},{224,... | collective-permute-start | bytes 49160 | tf_op jit(solution)/shard_map/ppermute | solution.py:463

commit v7 on v6

--- a/solution.py
+++ b/solution.py
@@ -10,10 +10,8 @@
 NM = 84
 SEND = 5
 LAST = 40
-MOMENTS = 45
-ROWS = 56
-GROUP = 11
-META = 112
+META = 45
+ROWS = 48
 FEATURES = 64
 KAPPA = 0.2
 CORE_SQ = 0.25
@@ -73,23 +71,19 @@
 
 
 def pack_kernel(*refs):
-    sources, send, scratch = refs[:8], refs[8], refs[9:]
-    pairs, box, cell, shift, fetch, off, tan, bur, sems, table, phi, charged = scratch
-    for copy in fetch_all(sources, scratch[:8], sems):
+    sources, send, scratch = refs[:7], refs[7], refs[8:]
+    pairs, box, shift, fetch, off, tan, bur, sems, table = scratch
+    for copy in fetch_all(sources, scratch[:7], sems):
         copy.wait()
     fill_table(table, off, tan, bur, 2.0 * KAPPA, KAPPA)
-    packed = cell_moments(cell, off, tan, bur, phi, charged)
     vectors = shift_table(box, shift)
     peers = send.shape[0]
     wide = jnp.concatenate([fetch[...].astype(f32), jnp.zeros((SEND, SEG - peers), f32)], axis=1)
-    tall = jnp.concatenate([wide, jnp.zeros((8 - SEND, SEG), f32)], axis=0).T
-    meta = jnp.concatenate(
-        [jnp.zeros((SEG, META), f32), tall, jnp.zeros((SEG, SEG - META - 8), f32)], axis=1
-    )
-    row, lane = iota((ROWS - LAST, SEG), 0), iota((ROWS - LAST, SEG), 1)
-    mark = (row == ROWS - LAST - 1) & (lane >= META)
+    meta = jnp.concatenate([wide, jnp.zeros((8 - SEND, SEG), f32)], axis=0).T
+    meta = jnp.concatenate([meta, jnp.zeros((SEG, SEG - 8), f32)], axis=1)
+    row = iota((ROWS - LAST, SEG), 0)
     for p in range(peers):
-        rest = jnp.where(mark, meta[p : p + 1, :], packed)
+        rest = jnp.where(row == META - LAST, meta[p : p + 1, :], 0.0)
         for s in range(SEND):
             k = p * SEND + s
             at = lane_block(pairs[0, k])
@@ -243,7 +237,7 @@
 def pair_kernel(recv, features, near_own, ret, near, acc, ids_vmem, ids, sem):
     peers = recv.shape[0]
     for p in range(peers):
-        ids_vmem[p : p + 1, :] = recv[p, ROWS - 1 : ROWS, :].astype(jnp.int32)
+        ids_vmem[p : p + 1, :] = recv[p, META : META + 1, :].astype(jnp.int32)
     copy = pltpu.make_async_copy(ids_vmem, ids, sem)
     copy.start()
     clear(acc)
@@ -252,7 +246,7 @@
     def peer(p, carry):
         for s in range(SEND):
             head, last = recv[p, 8 * s : 8 * s + 8, :], recv[p, LAST + s : LAST + s + 1, :]
-            rows = tile(head, last, features, acc, ids[p, META + s])
+            rows = tile(head, last, features, acc, ids[p, s])
             for c in range(3):
                 ret[p, 3 * s + c : 3 * s + c + 1, :] = rows[c]
         ret[p, 15:16, :] = jnp.zeros((1, SEG), f32)
@@ -303,17 +297,15 @@
     return made + lax.dot_general(left_low, right_high, dims, preferred_element_type=f32)
 
 
-def cell_moments(cell, off, tan, bur, phi, charged):
+def moment_kernel(cell, off, tan, bur, out, phi, charged):
     fill_phi(phi, off)
     charge = jnp.sum(bur[...] * tan[...], axis=0, keepdims=True)
     row = iota((CS, SEG), 0)
     for b in range(cell.shape[0]):
         part = charge[:, b * SEG : (b + 1) * SEG]
         charged[:, b * SEG : (b + 1) * SEG] = jnp.where(row == cell[b], part, 0.0)
-    part = dot_halves(phi[...], charged[...], 1)
-    part = jnp.concatenate([part, jnp.zeros((8 * GROUP - NM, CS), f32)], axis=0)
-    groups = [part[GROUP * g : GROUP * (g + 1), :] for g in range(8)]
-    return jnp.concatenate([jnp.zeros((MOMENTS - LAST, SEG), f32), jnp.concatenate(groups, axis=1)], axis=0)
+    part = dot_halves(phi[...], charged[...], 1).T
+    out[...] = jnp.concatenate([part, jnp.zeros((CS, SEG - NM), f32)], axis=1)
 
 
 def far_kernel_body(*refs):
@@ -326,14 +318,10 @@
     half = len(sources)
     count = 2 * half
     cells = count * CS
-    turned = jnp.concatenate([source[...] for source in sources], axis=0).T
-    first = MOMENTS - LAST
     for q in range(count):
         back = (count - q) % count
-        at = CS * (2 * (back % half) + back // half) + first
-        for g in range(8):
-            piece = turned[CS * g : CS * (g + 1), at : at + GROUP]
-            around[q * CS : (q + 1) * CS, GROUP * g : GROUP * (g + 1)] = piece
+        at = CS * (back // half)
+        around[q * CS : (q + 1) * CS, :] = sources[back % half][at : at + CS, :]
     around[cells : cells + CS, :] = around[0:CS, :]
     shifted[:, 0:NM] = jnp.zeros((CS, NM), f32)
     for o in range(1, cells):
@@ -426,21 +414,39 @@
     shape = lambda *dims: jax.ShapeDtypeStruct(dims, f32)
     table = pltpu.VMEM((16, segs), f32)
 
-    raw = [pair_list, box_matrix, block_cell]
+    raw = [pair_list, box_matrix]
     segments = [seg_offset, tangent, burgers]
     vectors = [image_shift, fetch_table.T, *segments]
     send = call(
         pack_kernel,
         shape(peers, ROWS, SEG),
-        [HBM] * 8,
+        [HBM] * 7,
         [pltpu.SMEM(x.shape, x.dtype) for x in raw]
         + [pltpu.VMEM(x.shape, x.dtype) for x in vectors]
-        + [pltpu.SemaphoreType.DMA((8,))]
-        + [table, pltpu.VMEM((NM, segs), f32), pltpu.VMEM((CS, segs), f32)],
+        + [pltpu.SemaphoreType.DMA((7,)), table],
         10**6,
         60,
     )(*raw, *vectors)
     recv = lax.all_to_all(send, "bulk", 0, 0, tiled=True)
+
+    moments = call(
+        moment_kernel,
+        shape(CS, SEG),
+        [SMEM] + [VMEM] * 3,
+        [pltpu.VMEM((NM, segs), f32), pltpu.VMEM((CS, segs), f32)],
+        10**9,
+        12,
+    )(block_cell, *segments)
+    inner = 8
+    outer = peers // inner
+
+    def from_bulk(value, up, along):
+        to = lambda j: (j // inner + up) % outer * inner + (j % inner + along) % inner
+        return lax.ppermute(value, "bulk", [(j, to(j)) for j in range(peers)])
+
+    moments = moments + sum(from_bulk(moments, k, 0) for k in range(1, outer))
+    moments = moments + from_bulk(moments, 0, inner // 2)
+    moments = moments + sum(from_bulk(moments, 0, k) for k in range(1, inner // 2))
 
     features, near_own, left = call(
         own_kernel,
@@ -463,7 +469,6 @@
         return lax.ppermute(value, "slab", [(s, (s + back) % slabs) for s in range(slabs)])
 
     half = slabs // 2
-    moments = jnp.sum(recv[:, LAST:, :], axis=0)
     other = from_slab(moments, half)
 
     ret, near = call(

time: 72.7 us -> 85.7 us (1.18); the launches traced: 71.3 us -> 85.3 us
  starting transfers between devices: 27.4 us -> 42.9 us
  Pallas kernels: 29.4 us -> 27.4 us
  waiting for transfers between devices: 9.05 us -> 10.9 us
  local copies, waits for them, and re-layouts: 4.59 us -> 3.21 us
    ppermute x0 -> x7, starting transfers between devices: none -> 14.1 us  [from_bulk(): return lax.ppermute(value, 'bulk', [(j, to(j)) for j in range(peers)])]
    ppermute x0 -> x7, waiting for transfers between devices: none -> 6.77 us  [from_bulk(): return lax.ppermute(value, 'bulk', [(j, to(j)) for j in range(peers)])]
    all_to_all x1, waiting for transfers between devices: 6.44 us -> 0.01 us  [local(): recv = lax.all_to_all(send, 'bulk', 0, 0, tiled=True)]
    pallas_call x1, Pallas kernels: 10.3 us -> 7 us  [local(): call(own_kernel, (jax.ShapeDtypeStruct((blocks, SEG, FEATURES), bf16), sh...]
    all_to_all x1, starting transfers between devices: 8.47 us -> 11.3 us  [local(): back = lax.all_to_all(ret, 'bulk', 0, 0, tiled=True)]
    ppermute x4, waiting for transfers between devices: 2.6 us -> 4.14 us  [from_slab(): lax.ppermute(value, 'slab', [(s, (s + back) % slabs) for s in range(slabs)])]
    ppermute x4, starting transfers between devices: 6.88 us -> 5.46 us  [from_slab(): lax.ppermute(value, 'slab', [(s, (s + back) % slabs) for s in range(slabs)])]
    unnamed x24 -> x26, local copies, waits for them, and re-layouts: 4.59 us -> 3.21 us
  transfers between devices with their start and end apart: 6 -> 13, of which waited for: 3 -> 6; matrix products, arithmetic and copies ran while one was open for 0% -> 0% of each run, Pallas kernels for 35% -> 27%
where the time goes in v7:
time: 85.7 us; the launch traced here: 85.3 us
  starting transfers between devices  42.9 us (50%)
  Pallas kernels  27.4 us (32%)
  waiting for transfers between devices  10.9 us (13%)
  local copies, waits for them, and re-layouts  3.21 us (4%)
    ppermute x7, starting transfers between devices, from_bulk(): return lax.ppermute(value, 'bulk', [(j, to(j)) for j in range(peers)])  14.1 us
    all_to_all x1, starting transfers between devices, local(): recv = lax.all_to_all(send, 'bulk', 0, 0, tiled=True)  12 us
    all_to_all x1, starting transfers between devices, local(): back = lax.all_to_all(ret, 'bulk', 0, 0, tiled=True)  11.3 us
    pallas_call x1, Pallas kernels, local(): call(pair_kernel, (shape(peers, 16, SEG), shape(SEG, SEG)), [VMEM] * 3, [...  10.9 us
    pallas_call x1, Pallas kernels, local(): call(own_kernel, (jax.ShapeDtypeStruct((blocks, SEG, FEATURES), bf16), sh...  7 us
    ppermute x7, waiting for transfers between devices, from_bulk(): return lax.ppermute(value, 'bulk', [(j, to(j)) for j in range(peers)])  6.77 us
    ppermute x4, starting transfers between devices, from_slab(): lax.ppermute(value, 'slab', [(s, (s + back) % slabs) for s in range(slabs)])  5.46 us
    ppermute x4, waiting for transfers between devices, from_slab(): lax.ppermute(value, 'slab', [(s, (s + back) % slabs) for s in range(slabs)])  4.14 us
  transfers between devices with their start and end apart: 13, of which 6 were waited for; matrix products, arithmetic and copies ran while one was open for 0% of the time, Pallas kernels for 27%

profile of v7, /device:TPU:1, one launch (start us, length us, event | category | flops | bytes accessed | tf_op | source)
XLA Modules:
  0.0 85.3 jit_solution(11146494662459199018)
XLA Ops:
  0.0 2.4 %shard_map.118 = f32[32,48,128]{2,1,0:T(8,128)} custom-call(s32[2,192]{1,0:T(2,128)} %pairs_row.1, f32[3,3]{1,0:T(4,128)} %box.1, s32[3,192]{1,0:T(4,128)} %shift.1, s32[5,32]{1,0:T(8,128)} %bitcast.1, f32[3,4096]{1,0:T(4,128)} %refs_2_.3, f32[3,4096]{1,0:T(4,128)} %refs_3_.1, f32[3,4096]{1,0:T(4,128)} %refs_4_.3), custom_call_target="tpu_custom_call" | custom-call | flops 1000000 | bytes 1048576 | tf_op jit(solution)/shard_map/pallas_call | solution.py:420
  2.4 12.0 %all-to-all-start = ((f32[32,48,128]{2,1,0:T(8,128)}), f32[32,48,128]{2,1,0:T(8,128)S(1)}, u32[]{:S(2)}, u32[]{:S(2)}) async-start(f32[32,48,128]{2,1,0:T(8,128)} %shard_map.118), calls=%async_computation | async-start | bytes 1572864 | tf_op jit(solution)/shard_map/all_to_all | solution.py:430
  14.5 0.8 copy-done
  15.3 0.8 copy-done.2
  16.1 0.8 copy-done.4
  17.6 1.3 %shard_map.121 = f32[16,128]{1,0:T(8,128)S(1)} custom-call(s32[32]{0:T(128)S(1)} %copy-done.10, f32[3,4096]{1,0:T(4,128)S(1)} %copy-done, f32[3,4096]{1,0:T(4,128)S(1)} %copy-done.2, f32[3,4096]{1,0:T(4,128)S(1)} %copy-done.4), custom_call_target="tpu_custom_call" | custom-call | flops 1000000000 | bytes 1048576 | tf_op jit(solution)/shard_map/pallas_call | solution.py:432
  18.9 2.5 %collective-permute-start.2 = (f32[16,128]{1,0:T(8,128)S(1)}, f32[16,128]{1,0:T(8,128)S(1)}, u32[]{:S(2)}, u32[]{:S(2)}) collective-permute-start(f32[16,128]{1,0:T(8,128)S(1)} %shard_map.121), channel_id=1, source_target_pairs={{0,24},{1,25},{2,26},{3,27},{4,28},{5,29},{6,30},{7,31},{8,0},{9,1... | collective-permute-start | bytes 24584 | tf_op jit(solution)/shard_map/ppermute | solution.py:445
  21.4 1.7 %collective-permute-start.1 = (f32[16,128]{1,0:T(8,128)S(1)}, f32[16,128]{1,0:T(8,128)S(1)}, u32[]{:S(2)}, u32[]{:S(2)}) collective-permute-start(f32[16,128]{1,0:T(8,128)S(1)} %shard_map.121), channel_id=1, source_target_pairs={{0,16},{1,17},{2,18},{3,19},{4,20},{5,21},{6,22},{7,23},{8,24},{9,... | collective-permute-start | bytes 24584 | tf_op jit(solution)/shard_map/ppermute | solution.py:445
  23.1 2.3 %collective-permute-done = f32[16,128]{1,0:T(8,128)S(1)} collective-permute-done((f32[16,128]{1,0:T(8,128)S(1)}, f32[16,128]{1,0:T(8,128)S(1)}, u32[]{:S(2)}, u32[]{:S(2)}) %collective-permute-start) | collective-permute-done | bytes 8224 | tf_op jit(solution)/shard_map/ppermute | solution.py:445
  25.4 0.7 collective-permute-done.1
  26.1 4.8 %collective-permute-start.3 = (f32[16,128]{1,0:T(8,128)S(1)}, f32[16,128]{1,0:T(8,128)S(1)}, u32[]{:S(2)}, u32[]{:S(2)}) collective-permute-start(f32[16,128]{1,0:T(8,128)S(1)} %add_add_fusion.1), channel_id=1, source_target_pairs={{0,4},{1,5},{2,6},{3,7},{4,0},{5,1},{6,2},{7,3},{8,12},{9,13},{10,... | collective-permute-start | bytes 24584 | tf_op jit(solution)/shard_map/ppermute | solution.py:445
  31.6 3.8 %collective-permute-done.3 = f32[16,128]{1,0:T(8,128)S(1)} collective-permute-done((f32[16,128]{1,0:T(8,128)S(1)}, f32[16,128]{1,0:T(8,128)S(1)}, u32[]{:S(2)}, u32[]{:S(2)}) %collective-permute-start.3) | collective-permute-done | bytes 8224 | tf_op jit(solution)/shard_map/ppermute | solution.py:445
  35.4 2.0 %collective-permute-start.6 = (f32[16,128]{1,0:T(8,128)S(1)}, f32[16,128]{1,0:T(8,128)S(1)}, u32[]{:S(2)}, u32[]{:S(2)}) collective-permute-start(f32[16,128]{1,0:T(8,128)S(1)} %add.24), channel_id=1, source_target_pairs={{0,3},{1,4},{2,5},{3,6},{4,7},{5,0},{6,1},{7,2},{8,11},{9,12},{10,... | collective-permute-start | bytes 24584 | tf_op jit(solution)/shard_map/ppermute | solution.py:445
  37.4 0.8 collective-permute-start.4
  38.2 2.3 %collective-permute-start.5 = (f32[16,128]{1,0:T(8,128)S(1)}, f32[16,128]{1,0:T(8,128)S(1)}, u32[]{:S(2)}, u32[]{:S(2)}) collective-permute-start(f32[16,128]{1,0:T(8,128)S(1)} %add.24), channel_id=1, source_target_pairs={{0,2},{1,3},{2,4},{3,5},{4,6},{5,7},{6,0},{7,1},{8,10},{9,11},{10,... | collective-permute-start | bytes 24584 | tf_op jit(solution)/shard_map/ppermute | solution.py:445
  40.4 7.0 %shard_map.119 = (bf16[32,128,64]{2,1,0:T(8,128)(2,1)S(1)}, f32[128,128]{1,0:T(8,128)S(1)}, s32[8,512]{1,0:T(8,128)S(1)}) custom-call(s32[2,192]{1,0:T(2,128)S(1)} %copy-done.7, s32[3,192]{1,0:T(4,128)S(1)} %copy-done.6, f32[3,3]{1,0:T(4,128)S(1)} %copy-done.8, s32[1]{0:T(128)S(6)} %copy.13.count, f32[3,4096]{1,0:T(4,128)S(1)} %copy-done.1, ...), custom_call_target="tpu_custom_call" | custom-call | flops 1000000000 | bytes 1048576 | tf_op jit(solution)/shard_map/pallas_call | solution.py:451
  47.5 1.0 %collective-permute-start.7 = (f32[16,128]{1,0:T(8,128)S(1)}, f32[16,128]{1,0:T(8,128)S(1)}, u32[]{:S(2)}, u32[]{:S(2)}) collective-permute-start(f32[16,128]{1,0:T(8,128)S(1)} %add_add_fusion), channel_id=1, source_target_pairs={{0,128},{32,160},{64,192},{96,224},{128,0},{160,32},{192,64},{224,... | collective-permute-start | bytes 24584 | tf_op jit(solution)/shard_map/ppermute | solution.py:469
  48.6 10.9 %shard_map.120 = (f32[32,16,128]{2,1,0:T(8,128)}, f32[128,128]{1,0:T(8,128)S(1)}) custom-call(f32[32,48,128]{2,1,0:T(8,128)S(1)} %all-to-all-done.recv, bf16[32,128,64]{2,1,0:T(8,128)(2,1)S(1)} %get-tuple-element.12.features, f32[128,128]{1,0:T(8,128)S(1)} %get-tuple-element.13.near_own), custom_call_target="tpu_custom_call" | custom-call | flops 10000000000 | bytes 1048576 | tf_op jit(solution)/shard_map/pallas_call | solution.py:474
  59.4 11.3 %all-to-all-start.1 = ((f32[32,16,128]{2,1,0:T(8,128)}), f32[32,16,128]{2,1,0:T(8,128)S(1)}, u32[]{:S(2)}, u32[]{:S(2)}) async-start(f32[32,16,128]{2,1,0:T(8,128)} %get-tuple-element.15), calls=%async_computation.1 | async-start | bytes 524288 | tf_op jit(solution)/shard_map/all_to_all | solution.py:488
  70.8 3.7 %collective-permute-start.8 = (f32[32,128]{1,0:T(8,128)S(1)}, f32[32,128]{1,0:T(8,128)S(1)}, u32[]{:S(2)}, u32[]{:S(2)}) collective-permute-start(f32[32,128]{1,0:T(8,128)S(1)} %pad_maximum_fusion.refs_6_), channel_id=1, source_target_pairs={{0,32},{32,64},{64,96},{96,128},{128,160},{160,192},{192,224},{224... | collective-permute-start | bytes 49160 | tf_op jit(solution)/shard_map/ppermute | solution.py:469
  74.5 0.7 collective-permute-start.10
  75.4 3.4 %collective-permute-done.9.refs_8_ = f32[32,128]{1,0:T(8,128)S(1)} collective-permute-done((f32[32,128]{1,0:T(8,128)S(1)}, f32[32,128]{1,0:T(8,128)S(1)}, u32[]{:S(2)}, u32[]{:S(2)}) %collective-permute-start.9) | collective-permute-done | bytes 16416 | tf_op jit(solution)/shard_map/ppermute | solution.py:469
  79.4 4.1 %shard_map.122.far = f32[3,4096]{1,0:T(4,128)S(1)} custom-call(s32[32]{0:T(128)S(1)} %copy-done.11, f32[3,3]{1,0:T(4,128)S(1)} %copy-done.9, f32[3,4096]{1,0:T(4,128)S(1)} %copy-done.1, f32[3,4096]{1,0:T(4,128)S(1)} %copy-done.3, f32[3,4096]{1,0:T(4,128)S(1)} %copy-done.5, f32[84,10752]{1,0:T(8,128)} %refs_5_.3, f32[32,128]{1,0:T(8,128)S(1)} %pad_maximum_fusion.refs_6_, ...), custom_call_target="tpu_custom_call" | custom-call | flops 1000000000 | bytes 1048576 | tf_op jit(solution)/shard_map/pallas_call | solution.py:492
  83.5 1.8 %shard_map.123 = f32[3,4096]{1,0:T(4,128)} custom-call(f32[32,16,128]{2,1,0:T(8,128)S(1)} %all-to-all-done.1.back, f32[128,128]{1,0:T(8,128)S(1)} %get-tuple-element.16.near_all, f32[3,4096]{1,0:T(4,128)S(1)} %shard_map.122.far, s32[2,4096]{1,0:T(2,128)S(1)} %copy-done.12, s32[8,512]{1,0:T(8,128)S(1)} %get-tuple-element.18.left), custom_call_target="tpu_custom_call" | custom-call | flops 1000000000 | bytes 1048576 | tf_op jit(solution)/shard_map/pallas_call | solution.py:509
  (38 shorter events, 1.5 us)
Async XLA Ops:
  0.0 40.4 %copy-start.7 = (s32[2,192]{1,0:T(2,128)S(1)}, s32[2,192]{1,0:T(2,128)}, u32[]{:S(2)}) copy-start(s32[2,192]{1,0:T(2,128)} %pairs_row.1) | copy-start | bytes 4612
  0.0 40.4 %copy-start.8 = (f32[3,3]{1,0:T(4,128)S(1)}, f32[3,3]{1,0:T(4,128)}, u32[]{:S(2)}) copy-start(f32[3,3]{1,0:T(4,128)} %box.1) | copy-start | bytes 112
  0.0 40.4 %copy-start.6 = (s32[3,192]{1,0:T(4,128)S(1)}, s32[3,192]{1,0:T(4,128)}, u32[]{:S(2)}) copy-start(s32[3,192]{1,0:T(4,128)} %shift.1) | copy-start | bytes 6916
  0.0 40.4 %copy-start.1 = (f32[3,4096]{1,0:T(4,128)S(1)}, f32[3,4096]{1,0:T(4,128)}, u32[]{:S(2)}) copy-start(f32[3,4096]{1,0:T(4,128)} %refs_2_.3) | copy-start | bytes 147460
  2.4 46.1 %all-to-all-start = ((f32[32,48,128]{2,1,0:T(8,128)}), f32[32,48,128]{2,1,0:T(8,128)S(1)}, u32[]{:S(2)}, u32[]{:S(2)}) async-start(f32[32,48,128]{2,1,0:T(8,128)} %shard_map.118), calls=%async_computation | async-start | bytes 1572864 | tf_op jit(solution)/shard_map/all_to_all | solution.py:430
  14.5 0.8 copy-start
  15.3 0.8 copy-start.2
  18.9 4.2 %collective-permute-start.2 = (f32[16,128]{1,0:T(8,128)S(1)}, f32[16,128]{1,0:T(8,128)S(1)}, u32[]{:S(2)}, u32[]{:S(2)}) collective-permute-start(f32[16,128]{1,0:T(8,128)S(1)} %shard_map.121), channel_id=1, source_target_pairs={{0,24},{1,25},{2,26},{3,27},{4,28},{5,29},{6,30},{7,31},{8,0},{9,1... | collective-permute-start | bytes 24584 | tf_op jit(solution)/shard_map/ppermute | solution.py:445
  21.4 4.0 %collective-permute-start = (f32[16,128]{1,0:T(8,128)S(1)}, f32[16,128]{1,0:T(8,128)S(1)}, u32[]{:S(2)}, u32[]{:S(2)}) collective-permute-start(f32[16,128]{1,0:T(8,128)S(1)} %shard_map.121), channel_id=1, source_target_pairs={{0,8},{1,9},{2,10},{3,11},{4,12},{5,13},{6,14},{7,15},{8,16},{9,17... | collective-permute-start | bytes 24584 | tf_op jit(solution)/shard_map/ppermute | solution.py:445
  21.4 4.7 %collective-permute-start.1 = (f32[16,128]{1,0:T(8,128)S(1)}, f32[16,128]{1,0:T(8,128)S(1)}, u32[]{:S(2)}, u32[]{:S(2)}) collective-permute-start(f32[16,128]{1,0:T(8,128)S(1)} %shard_map.121), channel_id=1, source_target_pairs={{0,16},{1,17},{2,18},{3,19},{4,20},{5,21},{6,22},{7,23},{8,24},{9,... | collective-permute-start | bytes 24584 | tf_op jit(solution)/shard_map/ppermute | solution.py:445
  26.1 9.3 %collective-permute-start.3 = (f32[16,128]{1,0:T(8,128)S(1)}, f32[16,128]{1,0:T(8,128)S(1)}, u32[]{:S(2)}, u32[]{:S(2)}) collective-permute-start(f32[16,128]{1,0:T(8,128)S(1)} %add_add_fusion.1), channel_id=1, source_target_pairs={{0,4},{1,5},{2,6},{3,7},{4,0},{5,1},{6,2},{7,3},{8,12},{9,13},{10,... | collective-permute-start | bytes 24584 | tf_op jit(solution)/shard_map/ppermute | solution.py:445
  35.4 12.0 %collective-permute-start.6 = (f32[16,128]{1,0:T(8,128)S(1)}, f32[16,128]{1,0:T(8,128)S(1)}, u32[]{:S(2)}, u32[]{:S(2)}) collective-permute-start(f32[16,128]{1,0:T(8,128)S(1)} %add.24), channel_id=1, source_target_pairs={{0,3},{1,4},{2,5},{3,6},{4,7},{5,0},{6,1},{7,2},{8,11},{9,12},{10,... | collective-permute-start | bytes 24584 | tf_op jit(solution)/shard_map/ppermute | solution.py:445
  37.4 10.1 %collective-permute-start.4 = (f32[16,128]{1,0:T(8,128)S(1)}, f32[16,128]{1,0:T(8,128)S(1)}, u32[]{:S(2)}, u32[]{:S(2)}) collective-permute-start(f32[16,128]{1,0:T(8,128)S(1)} %add.24), channel_id=1, source_target_pairs={{0,1},{1,2},{2,3},{3,4},{4,5},{5,6},{6,7},{7,0},{8,9},{9,10},{10,1... | collective-permute-start | bytes 24584 | tf_op jit(solution)/shard_map/ppermute | solution.py:445
  38.2 9.3 %collective-permute-start.5 = (f32[16,128]{1,0:T(8,128)S(1)}, f32[16,128]{1,0:T(8,128)S(1)}, u32[]{:S(2)}, u32[]{:S(2)}) collective-permute-start(f32[16,128]{1,0:T(8,128)S(1)} %add.24), channel_id=1, source_target_pairs={{0,2},{1,3},{2,4},{3,5},{4,6},{5,7},{6,0},{7,1},{8,10},{9,11},{10,... | collective-permute-start | bytes 24584 | tf_op jit(solution)/shard_map/ppermute | solution.py:445
  47.5 11.9 %collective-permute-start.7 = (f32[16,128]{1,0:T(8,128)S(1)}, f32[16,128]{1,0:T(8,128)S(1)}, u32[]{:S(2)}, u32[]{:S(2)}) collective-permute-start(f32[16,128]{1,0:T(8,128)S(1)} %add_add_fusion), channel_id=1, source_target_pairs={{0,128},{32,160},{64,192},{96,224},{128,0},{160,32},{192,64},{224,... | collective-permute-start | bytes 24584 | tf_op jit(solution)/shard_map/ppermute | solution.py:469
  48.5 30.8 %copy-start.3 = (f32[3,4096]{1,0:T(4,128)S(1)}, f32[3,4096]{1,0:T(4,128)}, u32[]{:S(2)}) copy-start(f32[3,4096]{1,0:T(4,128)} %refs_3_.1) | copy-start | bytes 147460
  48.5 30.8 %copy-start.5 = (f32[3,4096]{1,0:T(4,128)S(1)}, f32[3,4096]{1,0:T(4,128)}, u32[]{:S(2)}) copy-start(f32[3,4096]{1,0:T(4,128)} %refs_4_.3) | copy-start | bytes 147460
  48.5 30.8 %copy-start.9 = (f32[3,3]{1,0:T(4,128)S(1)}, f32[3,3]{1,0:T(4,128)}, u32[]{:S(2)}) copy-start(f32[3,3]{1,0:T(4,128)} %refs_1_.3) | copy-start | bytes 112
  48.5 30.8 %copy-start.11 = (s32[32]{0:T(128)S(1)}, s32[32]{0:T(128)}, u32[]{:S(2)}) copy-start(s32[32]{0:T(128)} %refs_0_.3) | copy-start | bytes 388
  59.4 24.1 %copy-start.12 = (s32[2,4096]{1,0:T(2,128)S(1)}, s32[2,4096]{1,0:T(2,128)}, u32[]{:S(2)}) copy-start(s32[2,4096]{1,0:T(2,128)} %conn.1) | copy-start | bytes 98308
  59.4 24.1 %all-to-all-start.1 = ((f32[32,16,128]{2,1,0:T(8,128)}), f32[32,16,128]{2,1,0:T(8,128)S(1)}, u32[]{:S(2)}, u32[]{:S(2)}) async-start(f32[32,16,128]{2,1,0:T(8,128)} %get-tuple-element.15), calls=%async_computation.1 | async-start | bytes 524288 | tf_op jit(solution)/shard_map/all_to_all | solution.py:488
  70.8 4.6 %collective-permute-start.8 = (f32[32,128]{1,0:T(8,128)S(1)}, f32[32,128]{1,0:T(8,128)S(1)}, u32[]{:S(2)}, u32[]{:S(2)}) collective-permute-start(f32[32,128]{1,0:T(8,128)S(1)} %pad_maximum_fusion.refs_6_), channel_id=1, source_target_pairs={{0,32},{32,64},{64,96},{96,128},{128,160},{160,192},{192,224},{224... | collective-permute-start | bytes 49160 | tf_op jit(solution)/shard_map/ppermute | solution.py:469
  74.5 4.2 %collective-permute-start.9 = (f32[32,128]{1,0:T(8,128)S(1)}, f32[32,128]{1,0:T(8,128)S(1)}, u32[]{:S(2)}, u32[]{:S(2)}) collective-permute-start(f32[32,128]{1,0:T(8,128)S(1)} %pad_maximum_fusion.refs_6_), channel_id=1, source_target_pairs={{0,64},{32,96},{64,128},{96,160},{128,192},{160,224},{192,0},{224,... | collective-permute-start | bytes 49160 | tf_op jit(solution)/shard_map/ppermute | solution.py:469
  74.5 4.9 %collective-permute-start.10 = (f32[32,128]{1,0:T(8,128)S(1)}, f32[32,128]{1,0:T(8,128)S(1)}, u32[]{:S(2)}, u32[]{:S(2)}) collective-permute-start(f32[32,128]{1,0:T(8,128)S(1)} %pad_maximum_fusion.refs_6_), channel_id=1, source_target_pairs={{0,96},{32,128},{64,160},{96,192},{128,224},{160,0},{192,32},{224,... | collective-permute-start | bytes 49160 | tf_op jit(solution)/shard_map/ppermute | solution.py:469
  (2 other events, 1.5 us)

commit v8 on v6

--- a/solution.py
+++ b/solution.py
@@ -8,6 +8,7 @@
 SEG = 128
 CS = 16
 NM = 84
+TALL = 96
 SEND = 5
 LAST = 40
 MOMENTS = 45
@@ -316,21 +317,36 @@
     return jnp.concatenate([jnp.zeros((MOMENTS - LAST, SEG), f32), jnp.concatenate(groups, axis=1)], axis=0)
 
 
-def far_kernel_body(*refs):
-    raw, sources, out, scratch = refs[:6], refs[6:10], refs[10], refs[11:]
-    cell, stress, off, tan, bur, operator, sems, around, shifted, phi, pots = scratch
-    copies = fetch_all(raw, scratch[:6], sems)
-    for copy in copies[:5]:
+def far_parts_kernel(*refs):
+    raw, outs, scratch = refs[:5], refs[5:10], refs[10:]
+    stress, off, tan, bur, operator, sems, phi = scratch
+    out, op_high, op_low, phi_high, phi_low = outs
+    copies = fetch_all(raw, scratch[:5], sems)
+    for copy in copies[:4]:
         copy.wait()
+    phi[NM:TALL, :] = jnp.zeros((TALL - NM, phi.shape[1]), f32)
     fill_phi(phi, off)
-    half = len(sources)
-    count = 2 * half
+    phi_high[...], phi_low[...] = halves_of(phi[...])
+    b = [bur[i : i + 1, :] for i in range(3)]
+    t = [tan[i : i + 1, :] for i in range(3)]
+    sym = [[0.5 * (stress[i, j] + stress[j, i]) for j in range(3)] for i in range(3)]
+    trac = [sym[i][0] * b[0] + sym[i][1] * b[1] + sym[i][2] * b[2] for i in range(3)]
+    for i in range(3):
+        j, k = (i + 1) % 3, (i + 2) % 3
+        out[i : i + 1, :] = trac[j] * t[k] - trac[k] * t[j]
+    copies[4].wait()
+    none = jnp.zeros((TALL - NM, operator.shape[1]), f32)
+    op_high[...], op_low[...] = halves_of(jnp.concatenate([operator[...], none], axis=0))
+
+
+def far_kernel_body(cell, bur, applied, op_high, op_low, phi_high, phi_low, *rest):
+    sources, (out, around, shifted, pots) = rest[:-4], rest[-4:]
+    count = len(sources)
     cells = count * CS
     turned = jnp.concatenate([source[...] for source in sources], axis=0).T
     first = MOMENTS - LAST
     for q in range(count):
-        back = (count - q) % count
-        at = CS * (2 * (back % half) + back // half) + first
+        at = CS * ((count - q) % count) + first
         for g in range(8):
             piece = turned[CS * g : CS * (g + 1), at : at + GROUP]
             around[q * CS : (q + 1) * CS, GROUP * g : GROUP * (g + 1)] = piece
@@ -338,25 +354,18 @@
     shifted[:, 0:NM] = jnp.zeros((CS, NM), f32)
     for o in range(1, cells):
         shifted[:, o * NM : (o + 1) * NM] = around[cells - o : cells - o + CS, 0:NM]
-    copies[5].wait()
-    local_exp = dot_halves(operator[...], shifted[...], 1).T
+    high, low = halves_of(shifted[...])
+    made = dot_nt(op_high[...], jnp.concatenate([high, low], axis=0))
+    local_exp = (made[:, 0:CS] + made[:, CS:] + dot_nt(op_low[...], high)).T
     high, low = halves_of(local_exp)
-    phi_high, phi_low = halves_of(phi[...])
-    made = jnp.dot(jnp.concatenate([high, low], axis=0), phi_high, preferred_element_type=f32)
-    made = made[0:CS] + made[CS:]
-    pots[...] = made + jnp.dot(high, phi_low, preferred_element_type=f32)
-    b = [bur[i : i + 1, :] for i in range(3)]
-    t = [tan[i : i + 1, :] for i in range(3)]
-    sym = [[0.5 * (stress[i, j] + stress[j, i]) for j in range(3)] for i in range(3)]
-    trac = [sym[i][0] * b[0] + sym[i][1] * b[1] + sym[i][2] * b[2] for i in range(3)]
-    for i in range(3):
-        j, k = (i + 1) % 3, (i + 2) % 3
-        out[i : i + 1, :] = trac[j] * t[k] - trac[k] * t[j]
+    both = jnp.concatenate([high, low], axis=0)
+    made = jnp.dot(both, phi_high[...], preferred_element_type=f32)
+    pots[...] = made[0:CS] + made[CS:] + jnp.dot(high, phi_low[...], preferred_element_type=f32)
     row = iota((CS, SEG), 0)
     for block in range(cell.shape[0]):
         at = slice(block * SEG, (block + 1) * SEG)
         mine = jnp.where(row == cell[block], pots[:, at], 0.0)
-        out[:, at] += jnp.sum(mine, axis=0, keepdims=True) * bur[:, at]
+        out[:, at] = applied[:, at] + jnp.sum(mine, axis=0, keepdims=True) * bur[:, at]
 
 
 def final_kernel(back, near_all, far, conn, left, out, force, halves):
@@ -462,9 +471,7 @@
     def from_slab(value, back):
         return lax.ppermute(value, "slab", [(s, (s + back) % slabs) for s in range(slabs)])
 
-    half = slabs // 2
     moments = jnp.sum(recv[:, LAST:, :], axis=0)
-    other = from_slab(moments, half)
 
     ret, near = call(
         pair_kernel,
@@ -479,27 +486,34 @@
         10**10,
         16,
     )(recv, features, near_own)
-    ret, other = lax.optimization_barrier((ret, other))
+    ret, stress = lax.optimization_barrier((ret, applied_stress))
     back = lax.all_to_all(ret, "bulk", 0, 0, tiled=True)
-    two = jnp.concatenate([moments, other], axis=0)
-    sources = [two] + [from_slab(two, k) for k in range(1, half)]
-    raw = [block_cell, applied_stress]
+    sources = [moments] + [from_slab(moments, k) for k in range(1, slabs)]
+
+    halves = lambda width: [jax.ShapeDtypeStruct((TALL, width), bf16)] * 2
+    raw = [*segments, far_kernel]
+    parts = call(
+        far_parts_kernel,
+        (shape(3, segs), *halves(far_kernel.shape[1]), *halves(segs)),
+        [HBM] * 5,
+        [pltpu.SMEM(stress.shape, f32)]
+        + [pltpu.VMEM(x.shape, x.dtype) for x in raw]
+        + [pltpu.SemaphoreType.DMA((5,)), pltpu.VMEM((TALL, segs), f32)],
+        10**9,
+        48,
+    )(stress, *raw)
     far = call(
         far_kernel_body,
         shape(3, segs),
-        [HBM] * 6 + [VMEM] * half,
-        [pltpu.SMEM(x.shape, x.dtype) for x in raw]
-        + [pltpu.VMEM(x.shape, x.dtype) for x in segments + [far_kernel]]
-        + [
-            pltpu.SemaphoreType.DMA((6,)),
+        [SMEM] + [VMEM] * (6 + slabs),
+        [
             pltpu.VMEM((slabs * CS + CS, SEG), f32),
             pltpu.VMEM((CS, slabs * CS * NM), f32),
-            pltpu.VMEM((NM, segs), f32),
             pltpu.VMEM((CS, segs), f32),
         ],
         10**9,
-        52,
-    )(*raw, *segments, far_kernel, *sources)
+        16,
+    )(block_cell, burgers, *parts, *sources)
 
     return call(
         final_kernel,

time: 72.7 us -> 73.8 us (1.015); the launches traced: 71.3 us -> 73.5 us
  waiting for transfers between devices: 9.05 us -> 16 us
  local copies, waits for them, and re-layouts: 4.59 us -> 0.04 us
  Pallas kernels: 29.4 us -> 26.5 us
  starting transfers between devices: 27.4 us -> 30 us
    all_to_all x1, waiting for transfers between devices: 6.44 us -> 16 us  [local(): recv = lax.all_to_all(send, 'bulk', 0, 0, tiled=True)]
    pallas_call x1, Pallas kernels: 10.3 us -> 5.25 us  [local(): call(own_kernel, (jax.ShapeDtypeStruct((blocks, SEG, FEATURES), bf16), sh...]
    unnamed x24 -> x18, local copies, waits for them, and re-layouts: 4.59 us -> 0.04 us
    ppermute x4 -> x7, starting transfers between devices: 6.88 us -> 9.47 us  [from_slab(): lax.ppermute(value, 'slab', [(s, (s + back) % slabs) for s in range(slabs)])]
    ppermute x4 -> x7, waiting for transfers between devices: 2.6 us -> 0.02 us  [from_slab(): lax.ppermute(value, 'slab', [(s, (s + back) % slabs) for s in range(slabs)])]
    pallas_call x1 -> x2, Pallas kernels: 4.09 us -> 6.09 us  [the longest x1 3.05 us: local(): call(far_kernel_body, shape(3, segs), [SMEM] + [VMEM] * (6 + slabs), [plt...]
  transfers between devices with their start and end apart: 6 -> 9, of which waited for: 3 -> 1; matrix products, arithmetic and copies ran while one was open for 0% -> 0% of each run, Pallas kernels for 35% -> 15%
where the time goes in v8:
time: 73.8 us; the launch traced here: 73.5 us
  starting transfers between devices  30 us (41%)
  Pallas kernels  26.5 us (36%)
  waiting for transfers between devices  16 us (22%)
  between operations  0.87 us (1%)
    all_to_all x1, waiting for transfers between devices, local(): recv = lax.all_to_all(send, 'bulk', 0, 0, tiled=True)  16 us
    all_to_all x1, starting transfers between devices, local(): recv = lax.all_to_all(send, 'bulk', 0, 0, tiled=True)  12 us
    pallas_call x1, Pallas kernels, local(): call(pair_kernel, (shape(peers, 16, SEG), shape(SEG, SEG)), [VMEM] * 3, [...  10.4 us
    ppermute x7, starting transfers between devices, from_slab(): lax.ppermute(value, 'slab', [(s, (s + back) % slabs) for s in range(slabs)])  9.47 us
    all_to_all x1, starting transfers between devices, local(): back = lax.all_to_all(ret, 'bulk', 0, 0, tiled=True)  8.46 us
    pallas_call x1, Pallas kernels, local(): call(own_kernel, (jax.ShapeDtypeStruct((blocks, SEG, FEATURES), bf16), sh...  5.25 us
    pallas_call x1, Pallas kernels, local(): call(far_kernel_body, shape(3, segs), [SMEM] + [VMEM] * (6 + slabs), [plt...  3.05 us
    pallas_call x1, Pallas kernels, local(): call(far_parts_kernel, (shape(3, segs), *halves(far_kernel.shape[1]), *ha...  3.04 us
  transfers between devices with their start and end apart: 9, of which 1 were waited for; matrix products, arithmetic and copies ran while one was open for 0% of the time, Pallas kernels for 15%

profile of v8, /device:TPU:1, one launch (start us, length us, event | category | flops | bytes accessed | tf_op | source)
XLA Modules:
  0.0 73.5 jit_solution(10929836604885090264)
XLA Ops:
  0.0 2.9 %shard_map.118 = f32[32,56,128]{2,1,0:T(8,128)} custom-call(s32[2,192]{1,0:T(2,128)} %pairs_row.1, f32[3,3]{1,0:T(4,128)} %box.1, s32[32]{0:T(128)} %cell.1, s32[3,192]{1,0:T(4,128)} %shift.1, s32[5,32]{1,0:T(8,128)} %bitcast.1, f32[3,4096]{1,0:T(4,128)} %refs_1_.3, f32[3,4096]{1,0:T(4,128)} %refs_2_.3, f32[3,4096]{1,0:T(4,128)} %bur.3), custom_call_target="tpu_custom_call" | custom-call | flops 1000000 | bytes 1048576 | tf_op jit(solution)/shard_map/pallas_call | solution.py:441
  3.0 12.0 %all-to-all-start = ((f32[32,56,128]{2,1,0:T(8,128)}), f32[32,56,128]{2,1,0:T(8,128)S(1)}, u32[]{:S(2)}, u32[]{:S(2)}) async-start(f32[32,56,128]{2,1,0:T(8,128)} %shard_map.118), calls=%async_computation | async-start | bytes 1835008 | tf_op jit(solution)/shard_map/all_to_all | solution.py:452
  15.7 5.2 %shard_map.119 = (bf16[32,128,64]{2,1,0:T(8,128)(2,1)S(1)}, f32[128,128]{1,0:T(8,128)S(1)}, s32[8,512]{1,0:T(8,128)S(1)}) custom-call(s32[2,192]{1,0:T(2,128)S(1)} %copy-done.5, s32[3,192]{1,0:T(4,128)S(1)} %copy-done.3, f32[3,3]{1,0:T(4,128)S(1)} %copy-done.6, s32[1]{0:T(128)S(6)} %copy.13.count, f32[3,4096]{1,0:T(4,128)S(1)} %copy-done.1, ...), custom_call_target="tpu_custom_call" | custom-call | flops 1000000000 | bytes 1048576 | tf_op jit(solution)/shard_map/pallas_call | solution.py:454
  21.0 16.0 %all-to-all-done.recv = f32[32,56,128]{2,1,0:T(8,128)S(1)} async-done(((f32[32,56,128]{2,1,0:T(8,128)}), f32[32,56,128]{2,1,0:T(8,128)S(1)}, u32[]{:S(2)}, u32[]{:S(2)}) %all-to-all-start) | async-done | bytes 917536 | tf_op jit(solution)/shard_map/all_to_all | solution.py:452
  37.0 10.4 %shard_map.120 = (f32[32,16,128]{2,1,0:T(8,128)}, f32[128,128]{1,0:T(8,128)S(1)}) custom-call(f32[32,56,128]{2,1,0:T(8,128)S(1)} %all-to-all-done.recv, bf16[32,128,64]{2,1,0:T(8,128)(2,1)S(1)} %get-tuple-element.17.features, f32[128,128]{1,0:T(8,128)S(1)} %get-tuple-element.18.near_own), custom_call_target="tpu_custom_call" | custom-call | flops 10000000000 | bytes 1048576 | tf_op jit(solution)/shard_map/pallas_call | solution.py:476
  47.4 8.5 %all-to-all-start.1 = ((f32[32,16,128]{2,1,0:T(8,128)}), f32[32,16,128]{2,1,0:T(8,128)S(1)}, u32[]{:S(2)}, u32[]{:S(2)}) async-start(f32[32,16,128]{2,1,0:T(8,128)} %get-tuple-element.20), calls=%async_computation.1 | async-start | bytes 524288 | tf_op jit(solution)/shard_map/all_to_all | solution.py:490
  55.9 0.0 copy-start.7
  56.0 1.5 %collective-permute-start.6 = (f32[16,128]{1,0:T(8,128)S(1)}, f32[16,128]{1,0:T(8,128)S(1)}, u32[]{:S(2)}, u32[]{:S(2)}) collective-permute-start(f32[16,128]{1,0:T(8,128)S(1)} %slice_reduce_fusion.rest_0_), channel_id=1, source_target_pairs={{0,224},{32,0},{64,32},{96,64},{128,96},{160,128},{192,160},{224,1... | collective-permute-start | bytes 24584 | tf_op jit(solution)/shard_map/ppermute | solution.py:472
  57.4 2.5 %collective-permute-start.5 = (f32[16,128]{1,0:T(8,128)S(1)}, f32[16,128]{1,0:T(8,128)S(1)}, u32[]{:S(2)}, u32[]{:S(2)}) collective-permute-start(f32[16,128]{1,0:T(8,128)S(1)} %slice_reduce_fusion.rest_0_), channel_id=1, source_target_pairs={{0,192},{32,224},{64,0},{96,32},{128,64},{160,96},{192,128},{224,1... | collective-permute-start | bytes 24584 | tf_op jit(solution)/shard_map/ppermute | solution.py:472
  59.9 0.8 %collective-permute-start.4 = (f32[16,128]{1,0:T(8,128)S(1)}, f32[16,128]{1,0:T(8,128)S(1)}, u32[]{:S(2)}, u32[]{:S(2)}) collective-permute-start(f32[16,128]{1,0:T(8,128)S(1)} %slice_reduce_fusion.rest_0_), channel_id=1, source_target_pairs={{0,160},{32,192},{64,224},{96,0},{128,32},{160,64},{192,96},{224,1... | collective-permute-start | bytes 24584 | tf_op jit(solution)/shard_map/ppermute | solution.py:472
  60.7 1.6 %collective-permute-start.3 = (f32[16,128]{1,0:T(8,128)S(1)}, f32[16,128]{1,0:T(8,128)S(1)}, u32[]{:S(2)}, u32[]{:S(2)}) collective-permute-start(f32[16,128]{1,0:T(8,128)S(1)} %slice_reduce_fusion.rest_0_), channel_id=1, source_target_pairs={{0,128},{32,160},{64,192},{96,224},{128,0},{160,32},{192,64},{224,... | collective-permute-start | bytes 24584 | tf_op jit(solution)/shard_map/ppermute | solution.py:472
  62.3 1.7 %collective-permute-start.2 = (f32[16,128]{1,0:T(8,128)S(1)}, f32[16,128]{1,0:T(8,128)S(1)}, u32[]{:S(2)}, u32[]{:S(2)}) collective-permute-start(f32[16,128]{1,0:T(8,128)S(1)} %slice_reduce_fusion.rest_0_), channel_id=1, source_target_pairs={{0,96},{32,128},{64,160},{96,192},{128,224},{160,0},{192,32},{224,... | collective-permute-start | bytes 24584 | tf_op jit(solution)/shard_map/ppermute | solution.py:472
  64.0 0.0 collective-permute-done.6.rest_7_
  64.0 0.6 collective-permute-start.1
  64.6 0.0 collective-permute-done.5.rest_6_
  64.6 0.9 %collective-permute-start = (f32[16,128]{1,0:T(8,128)S(1)}, f32[16,128]{1,0:T(8,128)S(1)}, u32[]{:S(2)}, u32[]{:S(2)}) collective-permute-start(f32[16,128]{1,0:T(8,128)S(1)} %slice_reduce_fusion.rest_0_), channel_id=1, source_target_pairs={{0,32},{32,64},{64,96},{96,128},{128,160},{160,192},{192,224},{224... | collective-permute-start | bytes 24584 | tf_op jit(solution)/shard_map/ppermute | solution.py:472
  65.4 3.0 %shard_map.121 = (f32[3,4096]{1,0:T(4,128)S(1)}, bf16[96,10752]{1,0:T(8,128)(2,1)S(1)}, bf16[96,10752]{1,0:T(8,128)(2,1)S(1)}, bf16[96,4096]{1,0:T(8,128)(2,1)S(1)}, bf16[96,4096]{1,0:T(8,128)(2,1)S(1)}) custom-call(f32[3,3]{1,0:T(4,128)S(1)} %copy-done.4, f32[3,4096]{1,0:T(4,128)S(1)} %copy-done.1, f32[3,4096]{1,0:T(4,128)S(1)} %copy-done.2, ...), custom_call_target="tpu_custom_call" | custom-call | flops 1000000000 | bytes 1048576 | tf_op jit(solution)/shard_map/pallas_call | solution.py:495
  68.5 0.0 collective-permute-done.4.rest_5_
  68.5 0.0 collective-permute-done.3.rest_4_
  68.5 0.0 collective-permute-done.2.rest_3_
  68.5 0.0 collective-permute-done.1.rest_2_
  68.6 0.0 copy-start.8
  68.6 3.0 %shard_map.122.far = f32[3,4096]{1,0:T(4,128)S(1)} custom-call(s32[32]{0:T(128)S(1)} %copy-done.7, f32[3,4096]{1,0:T(4,128)S(1)} %copy-done, f32[3,4096]{1,0:T(4,128)S(1)} %get-tuple-element.23.applied, bf16[96,10752]{1,0:T(8,128)(2,1)S(1)} %get-tuple-element.24.op_high, bf16[96,10752]{1,0:T(8,128)(2,1)S(1)} %get-tuple-element.25.op_low, ...), custom_call_target="tpu_custom_call" | custom-call | flops 1000000000 | bytes 1048576 | tf_op jit(solution)/shard_map/pallas_call | solution.py:505
  71.6 1.8 %shard_map.123 = f32[3,4096]{1,0:T(4,128)} custom-call(f32[32,16,128]{2,1,0:T(8,128)S(1)} %all-to-all-done.1.back, f32[128,128]{1,0:T(8,128)S(1)} %get-tuple-element.21.near_all, f32[3,4096]{1,0:T(4,128)S(1)} %shard_map.122.far, s32[2,4096]{1,0:T(2,128)S(1)} %copy-done.8, s32[8,512]{1,0:T(8,128)S(1)} %get-tuple-element.28.left), custom_call_target="tpu_custom_call" | custom-call | flops 1000000000 | bytes 1048576 | tf_op jit(solution)/shard_map/pallas_call | solution.py:518
  (19 shorter events, 0.1 us)
Async XLA Ops:
  0.0 15.7 %copy-start = (f32[3,4096]{1,0:T(4,128)S(1)}, f32[3,4096]{1,0:T(4,128)}, u32[]{:S(2)}) copy-start(f32[3,4096]{1,0:T(4,128)} %bur.3) | copy-start | bytes 147460
  0.0 15.7 %copy-start.2 = (f32[3,4096]{1,0:T(4,128)S(1)}, f32[3,4096]{1,0:T(4,128)}, u32[]{:S(2)}) copy-start(f32[3,4096]{1,0:T(4,128)} %refs_2_.3) | copy-start | bytes 147460
  0.0 15.7 %copy-start.1 = (f32[3,4096]{1,0:T(4,128)S(1)}, f32[3,4096]{1,0:T(4,128)}, u32[]{:S(2)}) copy-start(f32[3,4096]{1,0:T(4,128)} %refs_1_.3) | copy-start | bytes 147460
  0.0 15.7 %copy-start.3 = (s32[3,192]{1,0:T(4,128)S(1)}, s32[3,192]{1,0:T(4,128)}, u32[]{:S(2)}) copy-start(s32[3,192]{1,0:T(4,128)} %shift.1) | copy-start | bytes 6916
  0.0 15.7 %copy-start.5 = (s32[2,192]{1,0:T(2,128)S(1)}, s32[2,192]{1,0:T(2,128)}, u32[]{:S(2)}) copy-start(s32[2,192]{1,0:T(2,128)} %pairs_row.1) | copy-start | bytes 4612
  0.0 15.7 %copy-start.6 = (f32[3,3]{1,0:T(4,128)S(1)}, f32[3,3]{1,0:T(4,128)}, u32[]{:S(2)}) copy-start(f32[3,3]{1,0:T(4,128)} %box.1) | copy-start | bytes 112
  3.0 34.0 %all-to-all-start = ((f32[32,56,128]{2,1,0:T(8,128)}), f32[32,56,128]{2,1,0:T(8,128)S(1)}, u32[]{:S(2)}, u32[]{:S(2)}) async-start(f32[32,56,128]{2,1,0:T(8,128)} %shard_map.118), calls=%async_computation | async-start | bytes 1835008 | tf_op jit(solution)/shard_map/all_to_all | solution.py:452
  37.0 28.4 %copy-start.4 = (f32[3,3]{1,0:T(4,128)S(1)}, f32[3,3]{1,0:T(4,128)}, u32[]{:S(2)}) copy-start(f32[3,3]{1,0:T(4,128)} %refs_0_.2) | copy-start | bytes 112
  47.4 24.2 %all-to-all-start.1 = ((f32[32,16,128]{2,1,0:T(8,128)}), f32[32,16,128]{2,1,0:T(8,128)S(1)}, u32[]{:S(2)}, u32[]{:S(2)}) async-start(f32[32,16,128]{2,1,0:T(8,128)} %get-tuple-element.20), calls=%async_computation.1 | async-start | bytes 524288 | tf_op jit(solution)/shard_map/all_to_all | solution.py:490
  55.9 12.6 %copy-start.7 = (s32[32]{0:T(128)S(1)}, s32[32]{0:T(128)}, u32[]{:S(2)}) copy-start(s32[32]{0:T(128)} %cell.1) | copy-start | bytes 388
  56.0 8.0 %collective-permute-start.6 = (f32[16,128]{1,0:T(8,128)S(1)}, f32[16,128]{1,0:T(8,128)S(1)}, u32[]{:S(2)}, u32[]{:S(2)}) collective-permute-start(f32[16,128]{1,0:T(8,128)S(1)} %slice_reduce_fusion.rest_0_), channel_id=1, source_target_pairs={{0,224},{32,0},{64,32},{96,64},{128,96},{160,128},{192,160},{224,1... | collective-permute-start | bytes 24584 | tf_op jit(solution)/shard_map/ppermute | solution.py:472
  57.4 7.2 %collective-permute-start.5 = (f32[16,128]{1,0:T(8,128)S(1)}, f32[16,128]{1,0:T(8,128)S(1)}, u32[]{:S(2)}, u32[]{:S(2)}) collective-permute-start(f32[16,128]{1,0:T(8,128)S(1)} %slice_reduce_fusion.rest_0_), channel_id=1, source_target_pairs={{0,192},{32,224},{64,0},{96,32},{128,64},{160,96},{192,128},{224,1... | collective-permute-start | bytes 24584 | tf_op jit(solution)/shard_map/ppermute | solution.py:472
  59.9 8.6 %collective-permute-start.4 = (f32[16,128]{1,0:T(8,128)S(1)}, f32[16,128]{1,0:T(8,128)S(1)}, u32[]{:S(2)}, u32[]{:S(2)}) collective-permute-start(f32[16,128]{1,0:T(8,128)S(1)} %slice_reduce_fusion.rest_0_), channel_id=1, source_target_pairs={{0,160},{32,192},{64,224},{96,0},{128,32},{160,64},{192,96},{224,1... | collective-permute-start | bytes 24584 | tf_op jit(solution)/shard_map/ppermute | solution.py:472
  60.7 7.8 %collective-permute-start.3 = (f32[16,128]{1,0:T(8,128)S(1)}, f32[16,128]{1,0:T(8,128)S(1)}, u32[]{:S(2)}, u32[]{:S(2)}) collective-permute-start(f32[16,128]{1,0:T(8,128)S(1)} %slice_reduce_fusion.rest_0_), channel_id=1, source_target_pairs={{0,128},{32,160},{64,192},{96,224},{128,0},{160,32},{192,64},{224,... | collective-permute-start | bytes 24584 | tf_op jit(solution)/shard_map/ppermute | solution.py:472
  62.3 6.3 %collective-permute-start.2 = (f32[16,128]{1,0:T(8,128)S(1)}, f32[16,128]{1,0:T(8,128)S(1)}, u32[]{:S(2)}, u32[]{:S(2)}) collective-permute-start(f32[16,128]{1,0:T(8,128)S(1)} %slice_reduce_fusion.rest_0_), channel_id=1, source_target_pairs={{0,96},{32,128},{64,160},{96,192},{128,224},{160,0},{192,32},{224,... | collective-permute-start | bytes 24584 | tf_op jit(solution)/shard_map/ppermute | solution.py:472
  64.0 4.5 %collective-permute-start.1 = (f32[16,128]{1,0:T(8,128)S(1)}, f32[16,128]{1,0:T(8,128)S(1)}, u32[]{:S(2)}, u32[]{:S(2)}) collective-permute-start(f32[16,128]{1,0:T(8,128)S(1)} %slice_reduce_fusion.rest_0_), channel_id=1, source_target_pairs={{0,64},{32,96},{64,128},{96,160},{128,192},{160,224},{192,0},{224,... | collective-permute-start | bytes 24584 | tf_op jit(solution)/shard_map/ppermute | solution.py:472
  64.6 4.0 %collective-permute-start = (f32[16,128]{1,0:T(8,128)S(1)}, f32[16,128]{1,0:T(8,128)S(1)}, u32[]{:S(2)}, u32[]{:S(2)}) collective-permute-start(f32[16,128]{1,0:T(8,128)S(1)} %slice_reduce_fusion.rest_0_), channel_id=1, source_target_pairs={{0,32},{32,64},{64,96},{96,128},{128,160},{160,192},{192,224},{224... | collective-permute-start | bytes 24584 | tf_op jit(solution)/shard_map/ppermute | solution.py:472
  68.6 3.1 %copy-start.8 = (s32[2,4096]{1,0:T(2,128)S(1)}, s32[2,4096]{1,0:T(2,128)}, u32[]{:S(2)}) copy-start(s32[2,4096]{1,0:T(2,128)} %conn.1) | copy-start | bytes 98308

commit v9 on v6

--- a/solution.py
+++ b/solution.py
@@ -178,11 +178,15 @@
 
 
 def fold(acc, near, others):
+    ones = jnp.ones((16, SEG), bf16)
+
     def pair(half, carry):
         at = pl.ds(pl.multiple_of(8 * half, 8), 8)
         rows = []
         for b in (2 * half, 2 * half + 1):
-            rows += [jnp.sum(acc[b, c].T, axis=0, keepdims=True) for c in range(3)]
+            rows += [jnp.sum(acc[b, c].T, axis=0, keepdims=True) for c in range(2)]
+            high, low = halves_of(acc[b, 2])
+            rows.append((dot_nt(ones, high) + dot_nt(ones, low))[0:1])
             rows.append(jnp.zeros((1, SEG), f32))
         near[at, :] = others[at, :] - jnp.concatenate(rows, axis=0)
         return carry
@@ -317,8 +321,8 @@
 
 
 def far_kernel_body(*refs):
-    raw, sources, out, scratch = refs[:6], refs[6:10], refs[10], refs[11:]
-    cell, stress, off, tan, bur, operator, sems, around, shifted, phi, pots = scratch
+    core, raw, sources, out, scratch = refs[0], refs[1:7], refs[7:11], refs[11], refs[12:]
+    cell, stress, off, tan, bur, operator, sems, wide, around, shifted, phi, pots = scratch
     copies = fetch_all(raw, scratch[:6], sems)
     for copy in copies[:5]:
         copy.wait()
@@ -329,12 +333,12 @@
     turned = jnp.concatenate([source[...] for source in sources], axis=0).T
     first = MOMENTS - LAST
     for q in range(count):
-        back = (count - q) % count
-        at = CS * (2 * (back % half) + back // half) + first
+        at = CS * (2 * ((count + q % 2 - q) // 2 % half) + q % 2) + first
         for g in range(8):
             piece = turned[CS * g : CS * (g + 1), at : at + GROUP]
-            around[q * CS : (q + 1) * CS, GROUP * g : GROUP * (g + 1)] = piece
-    around[cells : cells + CS, :] = around[0:CS, :]
+            wide[q * CS : (q + 1) * CS, GROUP * g : GROUP * (g + 1)] = piece
+    wide[cells : cells + 2 * CS, :] = wide[0 : 2 * CS, :]
+    around[...] = wide[pl.ds(pl.multiple_of(CS * core[0], CS), cells + CS), :]
     shifted[:, 0:NM] = jnp.zeros((CS, NM), f32)
     for o in range(1, cells):
         shifted[:, o * NM : (o + 1) * NM] = around[cells - o : cells - o + CS, 0:NM]
@@ -459,12 +463,10 @@
         12,
     )(pair_list, image_shift, box_matrix, pair_count, *segments, pair_list)
 
-    def from_slab(value, back):
-        return lax.ppermute(value, "slab", [(s, (s + back) % slabs) for s in range(slabs)])
-
     half = slabs // 2
+    core = lax.axis_index("slab") % 2
     moments = jnp.sum(recv[:, LAST:, :], axis=0)
-    other = from_slab(moments, half)
+    other = lax.ppermute(moments, "slab", [(s, s ^ 1) for s in range(slabs)])
 
     ret, near = call(
         pair_kernel,
@@ -481,17 +483,24 @@
     )(recv, features, near_own)
     ret, other = lax.optimization_barrier((ret, other))
     back = lax.all_to_all(ret, "bulk", 0, 0, tiled=True)
-    two = jnp.concatenate([moments, other], axis=0)
-    sources = [two] + [from_slab(two, k) for k in range(1, half)]
+    even, odd = jnp.where(core == 0, moments, other), jnp.where(core == 0, other, moments)
+    two = jnp.concatenate([even, odd], axis=0)
+
+    def from_chip(back):
+        to = [(s, (s + 2 * back) % slabs) for s in range(slabs)]
+        return lax.ppermute(two, "slab", to)
+
+    sources = [two] + [from_chip(k) for k in range(1, half)]
     raw = [block_cell, applied_stress]
     far = call(
         far_kernel_body,
         shape(3, segs),
-        [HBM] * 6 + [VMEM] * half,
+        [SMEM] + [HBM] * 6 + [VMEM] * half,
         [pltpu.SMEM(x.shape, x.dtype) for x in raw]
         + [pltpu.VMEM(x.shape, x.dtype) for x in segments + [far_kernel]]
         + [
             pltpu.SemaphoreType.DMA((6,)),
+            pltpu.VMEM((slabs * CS + 2 * CS, SEG), f32),
             pltpu.VMEM((slabs * CS + CS, SEG), f32),
             pltpu.VMEM((CS, slabs * CS * NM), f32),
             pltpu.VMEM((NM, segs), f32),
@@ -499,7 +508,7 @@
         ],
         10**9,
         52,
-    )(*raw, *segments, far_kernel, *sources)
+    )(jnp.full((1,), core, jnp.int32), *raw, *segments, far_kernel, *sources)
 
     return call(
         final_kernel,

time: 72.7 us -> 70.7 us (0.972)
  Pallas kernels: 29.4 us -> 22.8 us
  waiting for transfers between devices: 9.05 us -> 14.4 us
    all_to_all x1, waiting for transfers between devices: 6.44 us -> 12.6 us  [local(): recv = lax.all_to_all(send, 'bulk', 0, 0, tiled=True)]
    pallas_call x1, Pallas kernels: 10.3 us -> 4.09 us  [local(): call(own_kernel, (jax.ShapeDtypeStruct((blocks, SEG, FEATURES), bf16), sh...]
    all_to_all x1, starting transfers between devices: 8.47 us -> 4.58 us  [local(): back = lax.all_to_all(ret, 'bulk', 0, 0, tiled=True)]
    ppermute x4, starting transfers between devices: 6.88 us -> 10 us  [the longest x1 5.15 us: local(): other = lax.ppermute(moments, 'slab', [(s, s ^ 1) for s in range(slabs)])]
    ppermute x4, waiting for transfers between devices: 2.6 us -> 1.74 us  [the longest x3 1.74 us: from_chip(): return lax.ppermute(two, 'slab', to)]
  transfers between devices with their start and end apart: 6 -> 6, of which waited for: 3 -> 3; matrix products, arithmetic and copies ran while one was open for 0% -> 0% of each run, Pallas kernels for 35% -> 26%
where the time goes in v9:
time: 70.7 us; the launch traced here: 69.3 us
  starting transfers between devices  26.7 us (38%)
  Pallas kernels  22.8 us (32%)
  waiting for transfers between devices  14.4 us (20%)
  local copies, waits for them, and re-layouts  4.59 us (6%)
  between operations  0.8 us (1%)
    all_to_all x1, waiting for transfers between devices, local(): recv = lax.all_to_all(send, 'bulk', 0, 0, tiled=True)  12.6 us
    all_to_all x1, starting transfers between devices, local(): recv = lax.all_to_all(send, 'bulk', 0, 0, tiled=True)  12.1 us
    pallas_call x1, Pallas kernels, local(): call(pair_kernel, (shape(peers, 16, SEG), shape(SEG, SEG)), [VMEM] * 3, [...  9.92 us
    ppermute x1, starting transfers between devices, local(): other = lax.ppermute(moments, 'slab', [(s, s ^ 1) for s in range(slabs)])  5.15 us
    ppermute x3, starting transfers between devices, from_chip(): return lax.ppermute(two, 'slab', to)  4.89 us
    unnamed x24, local copies, waits for them, and re-layouts  4.59 us
    all_to_all x1, starting transfers between devices, local(): back = lax.all_to_all(ret, 'bulk', 0, 0, tiled=True)  4.58 us
    pallas_call x1, Pallas kernels, local(): call(far_kernel_body, shape(3, segs), [SMEM] + [HBM] * 6 + [VMEM] * half,...  4.1 us
  transfers between devices with their start and end apart: 6, of which 3 were waited for; matrix products, arithmetic and copies ran while one was open for 0% of the time, Pallas kernels for 26%

profile of v9, /device:TPU:1, one launch (start us, length us, event | category | flops | bytes accessed | tf_op | source)
XLA Modules:
  0.0 69.3 jit_solution(9263337309523524201)
XLA Ops:
  0.0 2.8 %shard_map.118 = f32[32,56,128]{2,1,0:T(8,128)} custom-call(s32[2,192]{1,0:T(2,128)} %pairs_row.1, f32[3,3]{1,0:T(4,128)} %box.1, s32[32]{0:T(128)} %refs_1_.3, s32[3,192]{1,0:T(4,128)} %shift.1, s32[5,32]{1,0:T(8,128)} %bitcast.2, f32[3,4096]{1,0:T(4,128)} %refs_3_.3, f32[3,4096]{1,0:T(4,128)} %refs_4_.1, f32[3,4096]{1,0:T(4,128)} %refs_5_.3), custom_call_target="tpu_custom_call" | custom-call | flops 1000000 | bytes 1048576 | tf_op jit(solution)/shard_map/pallas_call | solution.py:436
  2.8 12.1 %all-to-all-start = ((f32[32,56,128]{2,1,0:T(8,128)}), f32[32,56,128]{2,1,0:T(8,128)S(1)}, u32[]{:S(2)}, u32[]{:S(2)}) async-start(f32[32,56,128]{2,1,0:T(8,128)} %shard_map.118), calls=%async_computation | async-start | bytes 1835008 | tf_op jit(solution)/shard_map/all_to_all | solution.py:447
  15.6 0.0 copy-start
  15.6 0.8 %copy-done = f32[3,4096]{1,0:T(4,128)S(1)} copy-done((f32[3,4096]{1,0:T(4,128)S(1)}, f32[3,4096]{1,0:T(4,128)}, u32[]{:S(2)}) %copy-start) | copy-done | bytes 49176
  16.4 0.8 %copy-done.2 = f32[3,4096]{1,0:T(4,128)S(1)} copy-done((f32[3,4096]{1,0:T(4,128)S(1)}, f32[3,4096]{1,0:T(4,128)}, u32[]{:S(2)}) %copy-start.2) | copy-done | bytes 49176
  17.2 0.8 %copy-done.4 = f32[3,4096]{1,0:T(4,128)S(1)} copy-done((f32[3,4096]{1,0:T(4,128)S(1)}, f32[3,4096]{1,0:T(4,128)}, u32[]{:S(2)}) %copy-start.4) | copy-done | bytes 49176
  18.1 0.7 copy-done.6
  18.8 0.7 copy-done.7
  19.4 0.7 copy-done.8
  20.1 4.1 %shard_map.119 = (bf16[32,128,64]{2,1,0:T(8,128)(2,1)S(1)}, f32[128,128]{1,0:T(8,128)S(1)}, s32[8,512]{1,0:T(8,128)S(1)}) custom-call(s32[2,192]{1,0:T(2,128)S(1)} %copy-done.7, s32[3,192]{1,0:T(4,128)S(1)} %copy-done.6, f32[3,3]{1,0:T(4,128)S(1)} %copy-done.8, s32[1]{0:T(128)S(6)} %copy.13.count, f32[3,4096]{1,0:T(4,128)S(1)} %copy-done, ...), custom_call_target="tpu_custom_call" | custom-call | flops 1000000000 | bytes 1048576 | tf_op jit(solution)/shard_map/pallas_call | solution.py:449
  24.2 12.6 %all-to-all-done.recv = f32[32,56,128]{2,1,0:T(8,128)S(1)} async-done(((f32[32,56,128]{2,1,0:T(8,128)}), f32[32,56,128]{2,1,0:T(8,128)S(1)}, u32[]{:S(2)}, u32[]{:S(2)}) %all-to-all-start) | async-done | bytes 917536 | tf_op jit(solution)/shard_map/all_to_all | solution.py:447
  36.9 5.1 %collective-permute-start = (f32[16,128]{1,0:T(8,128)S(1)}, f32[16,128]{1,0:T(8,128)S(1)}, u32[]{:S(2)}, u32[]{:S(2)}) collective-permute-start(f32[16,128]{1,0:T(8,128)S(1)} %slice_reduce_fusion), channel_id=1, source_target_pairs={{0,32},{32,0},{64,96},{96,64},{128,160},{160,128},{192,224},{224,1... | collective-permute-start | bytes 24584 | tf_op jit(solution)/shard_map/ppermute | solution.py:469
  42.1 0.0 copy-start.10
  42.1 9.9 %shard_map.120 = (f32[32,16,128]{2,1,0:T(8,128)}, f32[128,128]{1,0:T(8,128)S(1)}) custom-call(f32[32,56,128]{2,1,0:T(8,128)S(1)} %all-to-all-done.recv, bf16[32,128,64]{2,1,0:T(8,128)(2,1)S(1)} %get-tuple-element.12.features, f32[128,128]{1,0:T(8,128)S(1)} %get-tuple-element.13.near_own), custom_call_target="tpu_custom_call" | custom-call | flops 10000000000 | bytes 1048576 | tf_op jit(solution)/shard_map/pallas_call | solution.py:471
  52.0 0.0 copy-start.11
  52.0 0.0 collective-permute-done
  52.0 4.6 %all-to-all-start.1 = ((f32[32,16,128]{2,1,0:T(8,128)}), f32[32,16,128]{2,1,0:T(8,128)S(1)}, u32[]{:S(2)}, u32[]{:S(2)}) async-start(f32[32,16,128]{2,1,0:T(8,128)} %get-tuple-element.15), calls=%async_computation.1 | async-start | bytes 524288 | tf_op jit(solution)/shard_map/all_to_all | solution.py:485
  56.6 1.3 %collective-permute-start.1 = (f32[32,128]{1,0:T(8,128)S(1)}, f32[32,128]{1,0:T(8,128)S(1)}, u32[]{:S(2)}, u32[]{:S(2)}) collective-permute-start(f32[32,128]{1,0:T(8,128)S(1)} %pad_maximum_fusion.refs_7_), channel_id=1, source_target_pairs={{0,64},{32,96},{64,128},{96,160},{128,192},{160,224},{192,0},{224,... | collective-permute-start | bytes 49160 | tf_op jit(solution)/shard_map/ppermute | solution.py:491
  57.9 2.5 %collective-permute-start.2 = (f32[32,128]{1,0:T(8,128)S(1)}, f32[32,128]{1,0:T(8,128)S(1)}, u32[]{:S(2)}, u32[]{:S(2)}) collective-permute-start(f32[32,128]{1,0:T(8,128)S(1)} %pad_maximum_fusion.refs_7_), channel_id=1, source_target_pairs={{0,128},{32,160},{64,192},{96,224},{128,0},{160,32},{192,64},{224,... | collective-permute-start | bytes 49160 | tf_op jit(solution)/shard_map/ppermute | solution.py:491
  60.4 1.1 %collective-permute-start.3 = (f32[32,128]{1,0:T(8,128)S(1)}, f32[32,128]{1,0:T(8,128)S(1)}, u32[]{:S(2)}, u32[]{:S(2)}) collective-permute-start(f32[32,128]{1,0:T(8,128)S(1)} %pad_maximum_fusion.refs_7_), channel_id=1, source_target_pairs={{0,192},{32,224},{64,0},{96,32},{128,64},{160,96},{192,128},{224,1... | collective-permute-start | bytes 49160 | tf_op jit(solution)/shard_map/ppermute | solution.py:491
  61.5 0.5 collective-permute-done.2.refs_9_
  62.0 1.3 %collective-permute-done.3.refs_10_ = f32[32,128]{1,0:T(8,128)S(1)} collective-permute-done((f32[32,128]{1,0:T(8,128)S(1)}, f32[32,128]{1,0:T(8,128)S(1)}, u32[]{:S(2)}, u32[]{:S(2)}) %collective-permute-start.3) | collective-permute-done | bytes 16416 | tf_op jit(solution)/shard_map/ppermute | solution.py:491
  63.3 4.1 %shard_map.121.far = f32[3,4096]{1,0:T(4,128)S(1)} custom-call(s32[1]{0:T(128)} %bitcast.1.refs_0_, s32[32]{0:T(128)S(1)} %copy-done.10, f32[3,3]{1,0:T(4,128)S(1)} %copy-done.9, f32[3,4096]{1,0:T(4,128)S(1)} %copy-done.1, f32[3,4096]{1,0:T(4,128)S(1)} %copy-done.3, f32[3,4096]{1,0:T(4,128)S(1)} %copy-done.5, f32[84,10752]{1,0:T(8,128)} %refs_6_.3, ...), custom_call_target="tpu_custom_call" | custom-call | flops 1000000000 | bytes 1048576 | tf_op jit(solution)/shard_map/pallas_call | solution.py:495
  67.4 1.8 %shard_map.122 = f32[3,4096]{1,0:T(4,128)} custom-call(f32[32,16,128]{2,1,0:T(8,128)S(1)} %all-to-all-done.1.back, f32[128,128]{1,0:T(8,128)S(1)} %get-tuple-element.16.near_all, f32[3,4096]{1,0:T(4,128)S(1)} %shard_map.121.far, s32[2,4096]{1,0:T(2,128)S(1)} %copy-done.11, s32[8,512]{1,0:T(8,128)S(1)} %get-tuple-element.18.left), custom_call_target="tpu_custom_call" | custom-call | flops 1000000000 | bytes 1048576 | tf_op jit(solution)/shard_map/pallas_call | solution.py:513
  (20 shorter events, 0.1 us)
Async XLA Ops:
  2.8 34.0 %all-to-all-start = ((f32[32,56,128]{2,1,0:T(8,128)}), f32[32,56,128]{2,1,0:T(8,128)S(1)}, u32[]{:S(2)}, u32[]{:S(2)}) async-start(f32[32,56,128]{2,1,0:T(8,128)} %shard_map.118), calls=%async_computation | async-start | bytes 1835008 | tf_op jit(solution)/shard_map/all_to_all | solution.py:447
  15.6 0.8 %copy-start = (f32[3,4096]{1,0:T(4,128)S(1)}, f32[3,4096]{1,0:T(4,128)}, u32[]{:S(2)}) copy-start(f32[3,4096]{1,0:T(4,128)} %refs_3_.3) | copy-start | bytes 147460
  16.4 0.8 %copy-start.2 = (f32[3,4096]{1,0:T(4,128)S(1)}, f32[3,4096]{1,0:T(4,128)}, u32[]{:S(2)}) copy-start(f32[3,4096]{1,0:T(4,128)} %refs_4_.1) | copy-start | bytes 147460
  17.2 0.8 %copy-start.4 = (f32[3,4096]{1,0:T(4,128)S(1)}, f32[3,4096]{1,0:T(4,128)}, u32[]{:S(2)}) copy-start(f32[3,4096]{1,0:T(4,128)} %refs_5_.3) | copy-start | bytes 147460
  18.1 0.7 copy-start.6
  18.8 0.7 copy-start.7
  19.4 0.7 copy-start.8
  36.9 15.1 %collective-permute-start = (f32[16,128]{1,0:T(8,128)S(1)}, f32[16,128]{1,0:T(8,128)S(1)}, u32[]{:S(2)}, u32[]{:S(2)}) collective-permute-start(f32[16,128]{1,0:T(8,128)S(1)} %slice_reduce_fusion), channel_id=1, source_target_pairs={{0,32},{32,0},{64,96},{96,64},{128,160},{160,128},{192,224},{224,1... | collective-permute-start | bytes 24584 | tf_op jit(solution)/shard_map/ppermute | solution.py:469
  42.0 21.2 %copy-start.1 = (f32[3,4096]{1,0:T(4,128)S(1)}, f32[3,4096]{1,0:T(4,128)}, u32[]{:S(2)}) copy-start(f32[3,4096]{1,0:T(4,128)} %refs_3_.3) | copy-start | bytes 147460
  42.0 21.2 %copy-start.3 = (f32[3,4096]{1,0:T(4,128)S(1)}, f32[3,4096]{1,0:T(4,128)}, u32[]{:S(2)}) copy-start(f32[3,4096]{1,0:T(4,128)} %refs_4_.1) | copy-start | bytes 147460
  42.0 21.2 %copy-start.5 = (f32[3,4096]{1,0:T(4,128)S(1)}, f32[3,4096]{1,0:T(4,128)}, u32[]{:S(2)}) copy-start(f32[3,4096]{1,0:T(4,128)} %refs_5_.3) | copy-start | bytes 147460
  42.1 21.2 %copy-start.9 = (f32[3,3]{1,0:T(4,128)S(1)}, f32[3,3]{1,0:T(4,128)}, u32[]{:S(2)}) copy-start(f32[3,3]{1,0:T(4,128)} %refs_2_.3) | copy-start | bytes 112
  42.1 21.2 %copy-start.10 = (s32[32]{0:T(128)S(1)}, s32[32]{0:T(128)}, u32[]{:S(2)}) copy-start(s32[32]{0:T(128)} %refs_1_.3) | copy-start | bytes 388
  52.0 15.4 %copy-start.11 = (s32[2,4096]{1,0:T(2,128)S(1)}, s32[2,4096]{1,0:T(2,128)}, u32[]{:S(2)}) copy-start(s32[2,4096]{1,0:T(2,128)} %conn.1) | copy-start | bytes 98308
  52.0 15.4 %all-to-all-start.1 = ((f32[32,16,128]{2,1,0:T(8,128)}), f32[32,16,128]{2,1,0:T(8,128)S(1)}, u32[]{:S(2)}, u32[]{:S(2)}) async-start(f32[32,16,128]{2,1,0:T(8,128)} %get-tuple-element.15), calls=%async_computation.1 | async-start | bytes 524288 | tf_op jit(solution)/shard_map/all_to_all | solution.py:485
  56.6 4.9 %collective-permute-start.1 = (f32[32,128]{1,0:T(8,128)S(1)}, f32[32,128]{1,0:T(8,128)S(1)}, u32[]{:S(2)}, u32[]{:S(2)}) collective-permute-start(f32[32,128]{1,0:T(8,128)S(1)} %pad_maximum_fusion.refs_7_), channel_id=1, source_target_pairs={{0,64},{32,96},{64,128},{96,160},{128,192},{160,224},{192,0},{224,... | collective-permute-start | bytes 49160 | tf_op jit(solution)/shard_map/ppermute | solution.py:491
  57.9 4.1 %collective-permute-start.2 = (f32[32,128]{1,0:T(8,128)S(1)}, f32[32,128]{1,0:T(8,128)S(1)}, u32[]{:S(2)}, u32[]{:S(2)}) collective-permute-start(f32[32,128]{1,0:T(8,128)S(1)} %pad_maximum_fusion.refs_7_), channel_id=1, source_target_pairs={{0,128},{32,160},{64,192},{96,224},{128,0},{160,32},{192,64},{224,... | collective-permute-start | bytes 49160 | tf_op jit(solution)/shard_map/ppermute | solution.py:491
  60.4 2.9 %collective-permute-start.3 = (f32[32,128]{1,0:T(8,128)S(1)}, f32[32,128]{1,0:T(8,128)S(1)}, u32[]{:S(2)}, u32[]{:S(2)}) collective-permute-start(f32[32,128]{1,0:T(8,128)S(1)} %pad_maximum_fusion.refs_7_), channel_id=1, source_target_pairs={{0,192},{32,224},{64,0},{96,32},{128,64},{160,96},{192,128},{224,1... | collective-permute-start | bytes 49160 | tf_op jit(solution)/shard_map/ppermute | solution.py:491

commit v10 on v9

--- a/solution.py
+++ b/solution.py
@@ -74,11 +74,10 @@
 
 def pack_kernel(*refs):
     sources, send, scratch = refs[:8], refs[8], refs[9:]
-    pairs, box, cell, shift, fetch, off, tan, bur, sems, table, phi, charged = scratch
+    pairs, box, cell, shift, fetch, off, tan, bur, sems, table, phi, charged, stage, done = scratch
     for copy in fetch_all(sources, scratch[:8], sems):
         copy.wait()
     fill_table(table, off, tan, bur, 2.0 * KAPPA, KAPPA)
-    packed = cell_moments(cell, off, tan, bur, phi, charged)
     vectors = shift_table(box, shift)
     peers = send.shape[0]
     wide = jnp.concatenate([fetch[...].astype(f32), jnp.zeros((SEND, SEG - peers), f32)], axis=1)
@@ -89,14 +88,25 @@
     row, lane = iota((ROWS - LAST, SEG), 0), iota((ROWS - LAST, SEG), 1)
     mark = (row == ROWS - LAST - 1) & (lane >= META)
     for p in range(peers):
+        for s in range(SEND):
+            k = p * SEND + s
+            vec = jnp.broadcast_to(vectors[:, k : k + 1], (8, SEG))
+            stage[p, 8 * s : 8 * s + 8, :] = table[0:8, lane_block(pairs[0, k])] - vec
+    heads, tails = (
+        pltpu.make_async_copy(stage.at[:, rows, :], send.at[:, rows, :], done.at[i])
+        for i, rows in enumerate((pl.ds(0, LAST), pl.ds(LAST, ROWS - LAST)))
+    )
+    heads.start()
+    packed = cell_moments(cell, off, tan, bur, phi, charged)
+    for p in range(peers):
         rest = jnp.where(mark, meta[p : p + 1, :], packed)
         for s in range(SEND):
-            k = p * SEND + s
-            at = lane_block(pairs[0, k])
-            vec = jnp.broadcast_to(vectors[:, k : k + 1], (8, SEG))
-            send[p, 8 * s : 8 * s + 8, :] = table[0:8, at] - vec
-            rest = jnp.where(row == s, table[8:9, at], rest)
-        send[p, LAST:ROWS, :] = rest
+            last = table[8:9, lane_block(pairs[0, p * SEND + s])]
+            rest = jnp.where(row == s, last, rest)
+        stage[p, LAST:ROWS, :] = rest
+    tails.start()
+    heads.wait()
+    tails.wait()
 
 
 def split(value):
@@ -397,12 +407,12 @@
             out[c : c + 1, g * SEG : (g + 1) * SEG] = whole[g : g + 1, :]
 
 
-def call(body, out_shape, in_specs, scratch, flops, size):
+def call(body, out_shape, in_specs, scratch, flops, size, out_spec=VMEM):
     return pl.pallas_call(
         body,
         out_shape=out_shape,
         in_specs=in_specs,
-        out_specs=jax.tree.map(lambda _: VMEM, out_shape),
+        out_specs=jax.tree.map(lambda _: out_spec, out_shape),
         scratch_shapes=scratch,
         compiler_params=pltpu.CompilerParams(vmem_limit_bytes=size << 20),
         cost_estimate=pl.CostEstimate(flops=flops, bytes_accessed=1 << 20, transcendentals=0),
@@ -440,9 +450,11 @@
         [pltpu.SMEM(x.shape, x.dtype) for x in raw]
         + [pltpu.VMEM(x.shape, x.dtype) for x in vectors]
         + [pltpu.SemaphoreType.DMA((8,))]
-        + [table, pltpu.VMEM((NM, segs), f32), pltpu.VMEM((CS, segs), f32)],
+        + [table, pltpu.VMEM((NM, segs), f32), pltpu.VMEM((CS, segs), f32)]
+        + [pltpu.VMEM((peers, ROWS, SEG), f32), pltpu.SemaphoreType.DMA((2,))],
         10**6,
         60,
+        HBM,
     )(*raw, *vectors)
     recv = lax.all_to_all(send, "bulk", 0, 0, tiled=True)
 

time: 70.7 us -> 70.6 us (level)
  waiting for transfers between devices: 14.4 us -> 12 us
  Pallas kernels: 22.8 us -> 25.1 us
    all_to_all x1, waiting for transfers between devices: 12.6 us -> 10.2 us  [local(): recv = lax.all_to_all(send, 'bulk', 0, 0, tiled=True)]
    pallas_call x1, Pallas kernels: 4.09 us -> 6.5 us  [local(): call(own_kernel, (jax.ShapeDtypeStruct((blocks, SEG, FEATURES), bf16), sh...]
  transfers between devices with their start and end apart: 6 -> 6, of which waited for: 3 -> 3; matrix products, arithmetic and copies ran while one was open for 0% -> 0% of each run, Pallas kernels for 26% -> 30%
where the time goes in v10:
time: 70.6 us; the launch traced here: 69.2 us
  starting transfers between devices  26.7 us (38%)
  Pallas kernels  25.1 us (36%)
  waiting for transfers between devices  12 us (17%)
  local copies, waits for them, and re-layouts  4.59 us (7%)
  between operations  0.8 us (1%)
    all_to_all x1, starting transfers between devices, local(): recv = lax.all_to_all(send, 'bulk', 0, 0, tiled=True)  12.1 us
    all_to_all x1, waiting for transfers between devices, local(): recv = lax.all_to_all(send, 'bulk', 0, 0, tiled=True)  10.2 us
    pallas_call x1, Pallas kernels, local(): call(pair_kernel, (shape(peers, 16, SEG), shape(SEG, SEG)), [VMEM] * 3, [...  9.91 us
    pallas_call x1, Pallas kernels, local(): call(own_kernel, (jax.ShapeDtypeStruct((blocks, SEG, FEATURES), bf16), sh...  6.5 us
    ppermute x1, starting transfers between devices, local(): other = lax.ppermute(moments, 'slab', [(s, s ^ 1) for s in range(slabs)])  5.15 us
    ppermute x3, starting transfers between devices, from_chip(): return lax.ppermute(two, 'slab', to)  4.89 us
    unnamed x24, local copies, waits for them, and re-layouts  4.59 us
    all_to_all x1, starting transfers between devices, local(): back = lax.all_to_all(ret, 'bulk', 0, 0, tiled=True)  4.58 us
  transfers between devices with their start and end apart: 6, of which 3 were waited for; matrix products, arithmetic and copies ran while one was open for 0% of the time, Pallas kernels for 30%

profile of v10, /device:TPU:1, one launch (start us, length us, event | category | flops | bytes accessed | tf_op | source)
XLA Modules:
  0.0 69.2 jit_solution(9246484418153880115)
XLA Ops:
  0.0 2.8 %shard_map.118 = f32[32,56,128]{2,1,0:T(8,128)} custom-call(s32[2,192]{1,0:T(2,128)} %pairs_row.1, f32[3,3]{1,0:T(4,128)} %box.1, s32[32]{0:T(128)} %refs_1_.3, s32[3,192]{1,0:T(4,128)} %shift.1, s32[5,32]{1,0:T(8,128)} %bitcast.2, f32[3,4096]{1,0:T(4,128)} %refs_3_.3, f32[3,4096]{1,0:T(4,128)} %refs_4_.1, f32[3,4096]{1,0:T(4,128)} %refs_5_.3), custom_call_target="tpu_custom_call" | custom-call | flops 1000000 | bytes 1048576 | tf_op jit(solution)/shard_map/pallas_call | solution.py:446
  2.8 12.1 %all-to-all-start = ((f32[32,56,128]{2,1,0:T(8,128)}), f32[32,56,128]{2,1,0:T(8,128)S(1)}, u32[]{:S(2)}, u32[]{:S(2)}) async-start(f32[32,56,128]{2,1,0:T(8,128)} %shard_map.118), calls=%async_computation | async-start | bytes 1835008 | tf_op jit(solution)/shard_map/all_to_all | solution.py:459
  15.5 0.0 copy-start
  15.5 0.8 %copy-done = f32[3,4096]{1,0:T(4,128)S(1)} copy-done((f32[3,4096]{1,0:T(4,128)S(1)}, f32[3,4096]{1,0:T(4,128)}, u32[]{:S(2)}) %copy-start) | copy-done | bytes 49176
  16.3 0.8 %copy-done.2 = f32[3,4096]{1,0:T(4,128)S(1)} copy-done((f32[3,4096]{1,0:T(4,128)S(1)}, f32[3,4096]{1,0:T(4,128)}, u32[]{:S(2)}) %copy-start.2) | copy-done | bytes 49176
  17.2 0.8 %copy-done.4 = f32[3,4096]{1,0:T(4,128)S(1)} copy-done((f32[3,4096]{1,0:T(4,128)S(1)}, f32[3,4096]{1,0:T(4,128)}, u32[]{:S(2)}) %copy-start.4) | copy-done | bytes 49176
  18.0 0.7 copy-done.6
  18.7 0.7 copy-done.7
  19.4 0.7 copy-done.8
  20.1 6.5 %shard_map.119 = (bf16[32,128,64]{2,1,0:T(8,128)(2,1)S(1)}, f32[128,128]{1,0:T(8,128)S(1)}, s32[8,512]{1,0:T(8,128)S(1)}) custom-call(s32[2,192]{1,0:T(2,128)S(1)} %copy-done.7, s32[3,192]{1,0:T(4,128)S(1)} %copy-done.6, f32[3,3]{1,0:T(4,128)S(1)} %copy-done.8, s32[1]{0:T(128)S(6)} %copy.13.count, f32[3,4096]{1,0:T(4,128)S(1)} %copy-done, ...), custom_call_target="tpu_custom_call" | custom-call | flops 1000000000 | bytes 1048576 | tf_op jit(solution)/shard_map/pallas_call | solution.py:461
  26.6 10.2 %all-to-all-done.recv = f32[32,56,128]{2,1,0:T(8,128)S(1)} async-done(((f32[32,56,128]{2,1,0:T(8,128)}), f32[32,56,128]{2,1,0:T(8,128)S(1)}, u32[]{:S(2)}, u32[]{:S(2)}) %all-to-all-start) | async-done | bytes 917536 | tf_op jit(solution)/shard_map/all_to_all | solution.py:459
  36.8 5.1 %collective-permute-start = (f32[16,128]{1,0:T(8,128)S(1)}, f32[16,128]{1,0:T(8,128)S(1)}, u32[]{:S(2)}, u32[]{:S(2)}) collective-permute-start(f32[16,128]{1,0:T(8,128)S(1)} %slice_reduce_fusion), channel_id=1, source_target_pairs={{0,32},{32,0},{64,96},{96,64},{128,160},{160,128},{192,224},{224,1... | collective-permute-start | bytes 24584 | tf_op jit(solution)/shard_map/ppermute | solution.py:481
  42.0 0.0 copy-start.10
  42.0 9.9 %shard_map.120 = (f32[32,16,128]{2,1,0:T(8,128)}, f32[128,128]{1,0:T(8,128)S(1)}) custom-call(f32[32,56,128]{2,1,0:T(8,128)S(1)} %all-to-all-done.recv, bf16[32,128,64]{2,1,0:T(8,128)(2,1)S(1)} %get-tuple-element.12.features, f32[128,128]{1,0:T(8,128)S(1)} %get-tuple-element.13.near_own), custom_call_target="tpu_custom_call" | custom-call | flops 10000000000 | bytes 1048576 | tf_op jit(solution)/shard_map/pallas_call | solution.py:483
  51.9 0.0 copy-start.11
  51.9 0.0 collective-permute-done
  52.0 4.6 %all-to-all-start.1 = ((f32[32,16,128]{2,1,0:T(8,128)}), f32[32,16,128]{2,1,0:T(8,128)S(1)}, u32[]{:S(2)}, u32[]{:S(2)}) async-start(f32[32,16,128]{2,1,0:T(8,128)} %get-tuple-element.15), calls=%async_computation.1 | async-start | bytes 524288 | tf_op jit(solution)/shard_map/all_to_all | solution.py:497
  56.6 1.3 %collective-permute-start.1 = (f32[32,128]{1,0:T(8,128)S(1)}, f32[32,128]{1,0:T(8,128)S(1)}, u32[]{:S(2)}, u32[]{:S(2)}) collective-permute-start(f32[32,128]{1,0:T(8,128)S(1)} %pad_maximum_fusion.refs_7_), channel_id=1, source_target_pairs={{0,64},{32,96},{64,128},{96,160},{128,192},{160,224},{192,0},{224,... | collective-permute-start | bytes 49160 | tf_op jit(solution)/shard_map/ppermute | solution.py:503
  57.9 2.5 %collective-permute-start.2 = (f32[32,128]{1,0:T(8,128)S(1)}, f32[32,128]{1,0:T(8,128)S(1)}, u32[]{:S(2)}, u32[]{:S(2)}) collective-permute-start(f32[32,128]{1,0:T(8,128)S(1)} %pad_maximum_fusion.refs_7_), channel_id=1, source_target_pairs={{0,128},{32,160},{64,192},{96,224},{128,0},{160,32},{192,64},{224,... | collective-permute-start | bytes 49160 | tf_op jit(solution)/shard_map/ppermute | solution.py:503
  60.3 1.1 %collective-permute-start.3 = (f32[32,128]{1,0:T(8,128)S(1)}, f32[32,128]{1,0:T(8,128)S(1)}, u32[]{:S(2)}, u32[]{:S(2)}) collective-permute-start(f32[32,128]{1,0:T(8,128)S(1)} %pad_maximum_fusion.refs_7_), channel_id=1, source_target_pairs={{0,192},{32,224},{64,0},{96,32},{128,64},{160,96},{192,128},{224,1... | collective-permute-start | bytes 49160 | tf_op jit(solution)/shard_map/ppermute | solution.py:503
  61.5 0.5 collective-permute-done.2.refs_9_
  62.0 1.2 %collective-permute-done.3.refs_10_ = f32[32,128]{1,0:T(8,128)S(1)} collective-permute-done((f32[32,128]{1,0:T(8,128)S(1)}, f32[32,128]{1,0:T(8,128)S(1)}, u32[]{:S(2)}, u32[]{:S(2)}) %collective-permute-start.3) | collective-permute-done | bytes 16416 | tf_op jit(solution)/shard_map/ppermute | solution.py:503
  63.2 4.1 %shard_map.121.far = f32[3,4096]{1,0:T(4,128)S(1)} custom-call(s32[1]{0:T(128)} %bitcast.1.refs_0_, s32[32]{0:T(128)S(1)} %copy-done.10, f32[3,3]{1,0:T(4,128)S(1)} %copy-done.9, f32[3,4096]{1,0:T(4,128)S(1)} %copy-done.1, f32[3,4096]{1,0:T(4,128)S(1)} %copy-done.3, f32[3,4096]{1,0:T(4,128)S(1)} %copy-done.5, f32[84,10752]{1,0:T(8,128)} %refs_6_.3, ...), custom_call_target="tpu_custom_call" | custom-call | flops 1000000000 | bytes 1048576 | tf_op jit(solution)/shard_map/pallas_call | solution.py:507
  67.4 1.8 %shard_map.122 = f32[3,4096]{1,0:T(4,128)} custom-call(f32[32,16,128]{2,1,0:T(8,128)S(1)} %all-to-all-done.1.back, f32[128,128]{1,0:T(8,128)S(1)} %get-tuple-element.16.near_all, f32[3,4096]{1,0:T(4,128)S(1)} %shard_map.121.far, s32[2,4096]{1,0:T(2,128)S(1)} %copy-done.11, s32[8,512]{1,0:T(8,128)S(1)} %get-tuple-element.18.left), custom_call_target="tpu_custom_call" | custom-call | flops 1000000000 | bytes 1048576 | tf_op jit(solution)/shard_map/pallas_call | solution.py:525
  (20 shorter events, 0.1 us)
Async XLA Ops:
  2.8 34.0 %all-to-all-start = ((f32[32,56,128]{2,1,0:T(8,128)}), f32[32,56,128]{2,1,0:T(8,128)S(1)}, u32[]{:S(2)}, u32[]{:S(2)}) async-start(f32[32,56,128]{2,1,0:T(8,128)} %shard_map.118), calls=%async_computation | async-start | bytes 1835008 | tf_op jit(solution)/shard_map/all_to_all | solution.py:459
  15.5 0.8 %copy-start = (f32[3,4096]{1,0:T(4,128)S(1)}, f32[3,4096]{1,0:T(4,128)}, u32[]{:S(2)}) copy-start(f32[3,4096]{1,0:T(4,128)} %refs_3_.3) | copy-start | bytes 147460
  16.3 0.8 %copy-start.2 = (f32[3,4096]{1,0:T(4,128)S(1)}, f32[3,4096]{1,0:T(4,128)}, u32[]{:S(2)}) copy-start(f32[3,4096]{1,0:T(4,128)} %refs_4_.1) | copy-start | bytes 147460
  17.2 0.8 %copy-start.4 = (f32[3,4096]{1,0:T(4,128)S(1)}, f32[3,4096]{1,0:T(4,128)}, u32[]{:S(2)}) copy-start(f32[3,4096]{1,0:T(4,128)} %refs_5_.3) | copy-start | bytes 147460
  18.0 0.7 copy-start.6
  18.7 0.7 copy-start.7
  19.4 0.7 copy-start.8
  36.8 15.1 %collective-permute-start = (f32[16,128]{1,0:T(8,128)S(1)}, f32[16,128]{1,0:T(8,128)S(1)}, u32[]{:S(2)}, u32[]{:S(2)}) collective-permute-start(f32[16,128]{1,0:T(8,128)S(1)} %slice_reduce_fusion), channel_id=1, source_target_pairs={{0,32},{32,0},{64,96},{96,64},{128,160},{160,128},{192,224},{224,1... | collective-permute-start | bytes 24584 | tf_op jit(solution)/shard_map/ppermute | solution.py:481
  42.0 21.2 %copy-start.1 = (f32[3,4096]{1,0:T(4,128)S(1)}, f32[3,4096]{1,0:T(4,128)}, u32[]{:S(2)}) copy-start(f32[3,4096]{1,0:T(4,128)} %refs_3_.3) | copy-start | bytes 147460
  42.0 21.2 %copy-start.3 = (f32[3,4096]{1,0:T(4,128)S(1)}, f32[3,4096]{1,0:T(4,128)}, u32[]{:S(2)}) copy-start(f32[3,4096]{1,0:T(4,128)} %refs_4_.1) | copy-start | bytes 147460
  42.0 21.2 %copy-start.5 = (f32[3,4096]{1,0:T(4,128)S(1)}, f32[3,4096]{1,0:T(4,128)}, u32[]{:S(2)}) copy-start(f32[3,4096]{1,0:T(4,128)} %refs_5_.3) | copy-start | bytes 147460
  42.0 21.2 %copy-start.9 = (f32[3,3]{1,0:T(4,128)S(1)}, f32[3,3]{1,0:T(4,128)}, u32[]{:S(2)}) copy-start(f32[3,3]{1,0:T(4,128)} %refs_2_.3) | copy-start | bytes 112
  42.0 21.2 %copy-start.10 = (s32[32]{0:T(128)S(1)}, s32[32]{0:T(128)}, u32[]{:S(2)}) copy-start(s32[32]{0:T(128)} %refs_1_.3) | copy-start | bytes 388
  51.9 15.4 %copy-start.11 = (s32[2,4096]{1,0:T(2,128)S(1)}, s32[2,4096]{1,0:T(2,128)}, u32[]{:S(2)}) copy-start(s32[2,4096]{1,0:T(2,128)} %conn.1) | copy-start | bytes 98308
  52.0 15.4 %all-to-all-start.1 = ((f32[32,16,128]{2,1,0:T(8,128)}), f32[32,16,128]{2,1,0:T(8,128)S(1)}, u32[]{:S(2)}, u32[]{:S(2)}) async-start(f32[32,16,128]{2,1,0:T(8,128)} %get-tuple-element.15), calls=%async_computation.1 | async-start | bytes 524288 | tf_op jit(solution)/shard_map/all_to_all | solution.py:497
  56.6 4.9 %collective-permute-start.1 = (f32[32,128]{1,0:T(8,128)S(1)}, f32[32,128]{1,0:T(8,128)S(1)}, u32[]{:S(2)}, u32[]{:S(2)}) collective-permute-start(f32[32,128]{1,0:T(8,128)S(1)} %pad_maximum_fusion.refs_7_), channel_id=1, source_target_pairs={{0,64},{32,96},{64,128},{96,160},{128,192},{160,224},{192,0},{224,... | collective-permute-start | bytes 49160 | tf_op jit(solution)/shard_map/ppermute | solution.py:503
  57.9 4.1 %collective-permute-start.2 = (f32[32,128]{1,0:T(8,128)S(1)}, f32[32,128]{1,0:T(8,128)S(1)}, u32[]{:S(2)}, u32[]{:S(2)}) collective-permute-start(f32[32,128]{1,0:T(8,128)S(1)} %pad_maximum_fusion.refs_7_), channel_id=1, source_target_pairs={{0,128},{32,160},{64,192},{96,224},{128,0},{160,32},{192,64},{224,... | collective-permute-start | bytes 49160 | tf_op jit(solution)/shard_map/ppermute | solution.py:503
  60.3 2.9 %collective-permute-start.3 = (f32[32,128]{1,0:T(8,128)S(1)}, f32[32,128]{1,0:T(8,128)S(1)}, u32[]{:S(2)}, u32[]{:S(2)}) collective-permute-start(f32[32,128]{1,0:T(8,128)S(1)} %pad_maximum_fusion.refs_7_), channel_id=1, source_target_pairs={{0,192},{32,224},{64,0},{96,32},{128,64},{160,96},{192,128},{224,1... | collective-permute-start | bytes 49160 | tf_op jit(solution)/shard_map/ppermute | solution.py:503

commit v11 on v10

--- a/solution.py
+++ b/solution.py
@@ -272,7 +272,7 @@
         ret[p, 15:16, :] = jnp.zeros((1, SEG), f32)
         return carry
 
-    lax.fori_loop(0, peers, peer, 0, unroll=8)
+    lax.fori_loop(0, peers, peer, 0, unroll=16)
     fold(acc, near, near_own)
 
 

time: 70.6 us -> 70.3 us (level)
  waiting for transfers between devices: 12 us -> 8.25 us
  Pallas kernels: 25.1 us -> 28.5 us
    pallas_call x1, Pallas kernels: 6.5 us -> 10.2 us  [local(): call(own_kernel, (jax.ShapeDtypeStruct((blocks, SEG, FEATURES), bf16), sh...]
    all_to_all x1, waiting for transfers between devices: 10.2 us -> 6.51 us  [local(): recv = lax.all_to_all(send, 'bulk', 0, 0, tiled=True)]
  transfers between devices with their start and end apart: 6 -> 6, of which waited for: 3 -> 3; matrix products, arithmetic and copies ran while one was open for 0% -> 0% of each run, Pallas kernels for 30% -> 35%
where the time goes in v11:
time: 70.3 us; the launch traced here: 68.9 us
  Pallas kernels  28.5 us (41%)
  starting transfers between devices  26.7 us (38%)
  waiting for transfers between devices  8.25 us (12%)
  local copies, waits for them, and re-layouts  4.59 us (7%)
  between operations  0.8 us (1%)
    all_to_all x1, starting transfers between devices, local(): recv = lax.all_to_all(send, 'bulk', 0, 0, tiled=True)  12.1 us
    pallas_call x1, Pallas kernels, local(): call(own_kernel, (jax.ShapeDtypeStruct((blocks, SEG, FEATURES), bf16), sh...  10.2 us
    pallas_call x1, Pallas kernels, local(): call(pair_kernel, (shape(peers, 16, SEG), shape(SEG, SEG)), [VMEM] * 3, [...  9.59 us
    all_to_all x1, waiting for transfers between devices, local(): recv = lax.all_to_all(send, 'bulk', 0, 0, tiled=True)  6.51 us
    ppermute x1, starting transfers between devices, local(): other = lax.ppermute(moments, 'slab', [(s, s ^ 1) for s in range(slabs)])  5.15 us
    ppermute x3, starting transfers between devices, from_chip(): return lax.ppermute(two, 'slab', to)  4.88 us
    all_to_all x1, starting transfers between devices, local(): back = lax.all_to_all(ret, 'bulk', 0, 0, tiled=True)  4.59 us
    unnamed x24, local copies, waits for them, and re-layouts  4.59 us
  transfers between devices with their start and end apart: 6, of which 3 were waited for; matrix products, arithmetic and copies ran while one was open for 0% of the time, Pallas kernels for 35%

profile of v11, /device:TPU:1, one launch (start us, length us, event | category | flops | bytes accessed | tf_op | source)
XLA Modules:
  0.0 68.9 jit_solution(12589259439806296991)
XLA Ops:
  0.0 2.8 %shard_map.118 = f32[32,56,128]{2,1,0:T(8,128)} custom-call(s32[2,192]{1,0:T(2,128)} %pairs_row.1, f32[3,3]{1,0:T(4,128)} %box.1, s32[32]{0:T(128)} %refs_1_.3, s32[3,192]{1,0:T(4,128)} %shift.1, s32[5,32]{1,0:T(8,128)} %bitcast.2, f32[3,4096]{1,0:T(4,128)} %refs_3_.3, f32[3,4096]{1,0:T(4,128)} %refs_4_.1, f32[3,4096]{1,0:T(4,128)} %refs_5_.3), custom_call_target="tpu_custom_call" | custom-call | flops 1000000 | bytes 1048576 | tf_op jit(solution)/shard_map/pallas_call | solution.py:446
  2.8 12.1 %all-to-all-start = ((f32[32,56,128]{2,1,0:T(8,128)}), f32[32,56,128]{2,1,0:T(8,128)S(1)}, u32[]{:S(2)}, u32[]{:S(2)}) async-start(f32[32,56,128]{2,1,0:T(8,128)} %shard_map.118), calls=%async_computation | async-start | bytes 1835008 | tf_op jit(solution)/shard_map/all_to_all | solution.py:459
  15.5 0.0 copy-start
  15.5 0.8 %copy-done = f32[3,4096]{1,0:T(4,128)S(1)} copy-done((f32[3,4096]{1,0:T(4,128)S(1)}, f32[3,4096]{1,0:T(4,128)}, u32[]{:S(2)}) %copy-start) | copy-done | bytes 49176
  16.4 0.8 %copy-done.2 = f32[3,4096]{1,0:T(4,128)S(1)} copy-done((f32[3,4096]{1,0:T(4,128)S(1)}, f32[3,4096]{1,0:T(4,128)}, u32[]{:S(2)}) %copy-start.2) | copy-done | bytes 49176
  17.2 0.8 %copy-done.4 = f32[3,4096]{1,0:T(4,128)S(1)} copy-done((f32[3,4096]{1,0:T(4,128)S(1)}, f32[3,4096]{1,0:T(4,128)}, u32[]{:S(2)}) %copy-start.4) | copy-done | bytes 49176
  18.0 0.7 copy-done.6
  18.7 0.7 copy-done.7
  19.4 0.7 copy-done.8
  20.1 10.2 %shard_map.119 = (bf16[32,128,64]{2,1,0:T(8,128)(2,1)S(1)}, f32[128,128]{1,0:T(8,128)S(1)}, s32[8,512]{1,0:T(8,128)S(1)}) custom-call(s32[2,192]{1,0:T(2,128)S(1)} %copy-done.7, s32[3,192]{1,0:T(4,128)S(1)} %copy-done.6, f32[3,3]{1,0:T(4,128)S(1)} %copy-done.8, s32[1]{0:T(128)S(6)} %copy.13.count, f32[3,4096]{1,0:T(4,128)S(1)} %copy-done, ...), custom_call_target="tpu_custom_call" | custom-call | flops 1000000000 | bytes 1048576 | tf_op jit(solution)/shard_map/pallas_call | solution.py:461
  30.3 6.5 %all-to-all-done.recv = f32[32,56,128]{2,1,0:T(8,128)S(1)} async-done(((f32[32,56,128]{2,1,0:T(8,128)}), f32[32,56,128]{2,1,0:T(8,128)S(1)}, u32[]{:S(2)}, u32[]{:S(2)}) %all-to-all-start) | async-done | bytes 917536 | tf_op jit(solution)/shard_map/all_to_all | solution.py:459
  36.8 5.1 %collective-permute-start = (f32[16,128]{1,0:T(8,128)S(1)}, f32[16,128]{1,0:T(8,128)S(1)}, u32[]{:S(2)}, u32[]{:S(2)}) collective-permute-start(f32[16,128]{1,0:T(8,128)S(1)} %slice_reduce_fusion), channel_id=1, source_target_pairs={{0,32},{32,0},{64,96},{96,64},{128,160},{160,128},{192,224},{224,1... | collective-permute-start | bytes 24584 | tf_op jit(solution)/shard_map/ppermute | solution.py:481
  42.0 0.0 copy-start.10
  42.0 9.6 %shard_map.120 = (f32[32,16,128]{2,1,0:T(8,128)}, f32[128,128]{1,0:T(8,128)S(1)}) custom-call(f32[32,56,128]{2,1,0:T(8,128)S(1)} %all-to-all-done.recv, bf16[32,128,64]{2,1,0:T(8,128)(2,1)S(1)} %get-tuple-element.12.features, f32[128,128]{1,0:T(8,128)S(1)} %get-tuple-element.13.near_own), custom_call_target="tpu_custom_call" | custom-call | flops 10000000000 | bytes 1048576 | tf_op jit(solution)/shard_map/pallas_call | solution.py:483
  51.6 0.0 copy-start.11
  51.6 0.0 collective-permute-done
  51.6 4.6 %all-to-all-start.1 = ((f32[32,16,128]{2,1,0:T(8,128)}), f32[32,16,128]{2,1,0:T(8,128)S(1)}, u32[]{:S(2)}, u32[]{:S(2)}) async-start(f32[32,16,128]{2,1,0:T(8,128)} %get-tuple-element.15), calls=%async_computation.1 | async-start | bytes 524288 | tf_op jit(solution)/shard_map/all_to_all | solution.py:497
  56.3 1.3 %collective-permute-start.1 = (f32[32,128]{1,0:T(8,128)S(1)}, f32[32,128]{1,0:T(8,128)S(1)}, u32[]{:S(2)}, u32[]{:S(2)}) collective-permute-start(f32[32,128]{1,0:T(8,128)S(1)} %pad_maximum_fusion.refs_7_), channel_id=1, source_target_pairs={{0,64},{32,96},{64,128},{96,160},{128,192},{160,224},{192,0},{224,... | collective-permute-start | bytes 49160 | tf_op jit(solution)/shard_map/ppermute | solution.py:503
  57.5 2.5 %collective-permute-start.2 = (f32[32,128]{1,0:T(8,128)S(1)}, f32[32,128]{1,0:T(8,128)S(1)}, u32[]{:S(2)}, u32[]{:S(2)}) collective-permute-start(f32[32,128]{1,0:T(8,128)S(1)} %pad_maximum_fusion.refs_7_), channel_id=1, source_target_pairs={{0,128},{32,160},{64,192},{96,224},{128,0},{160,32},{192,64},{224,... | collective-permute-start | bytes 49160 | tf_op jit(solution)/shard_map/ppermute | solution.py:503
  60.0 1.1 %collective-permute-start.3 = (f32[32,128]{1,0:T(8,128)S(1)}, f32[32,128]{1,0:T(8,128)S(1)}, u32[]{:S(2)}, u32[]{:S(2)}) collective-permute-start(f32[32,128]{1,0:T(8,128)S(1)} %pad_maximum_fusion.refs_7_), channel_id=1, source_target_pairs={{0,192},{32,224},{64,0},{96,32},{128,64},{160,96},{192,128},{224,1... | collective-permute-start | bytes 49160 | tf_op jit(solution)/shard_map/ppermute | solution.py:503
  61.2 0.5 collective-permute-done.2.refs_9_
  61.6 1.3 %collective-permute-done.3.refs_10_ = f32[32,128]{1,0:T(8,128)S(1)} collective-permute-done((f32[32,128]{1,0:T(8,128)S(1)}, f32[32,128]{1,0:T(8,128)S(1)}, u32[]{:S(2)}, u32[]{:S(2)}) %collective-permute-start.3) | collective-permute-done | bytes 16416 | tf_op jit(solution)/shard_map/ppermute | solution.py:503
  62.9 4.1 %shard_map.121.far = f32[3,4096]{1,0:T(4,128)S(1)} custom-call(s32[1]{0:T(128)} %bitcast.1.refs_0_, s32[32]{0:T(128)S(1)} %copy-done.10, f32[3,3]{1,0:T(4,128)S(1)} %copy-done.9, f32[3,4096]{1,0:T(4,128)S(1)} %copy-done.1, f32[3,4096]{1,0:T(4,128)S(1)} %copy-done.3, f32[3,4096]{1,0:T(4,128)S(1)} %copy-done.5, f32[84,10752]{1,0:T(8,128)} %refs_6_.3, ...), custom_call_target="tpu_custom_call" | custom-call | flops 1000000000 | bytes 1048576 | tf_op jit(solution)/shard_map/pallas_call | solution.py:507
  67.0 1.8 %shard_map.122 = f32[3,4096]{1,0:T(4,128)} custom-call(f32[32,16,128]{2,1,0:T(8,128)S(1)} %all-to-all-done.1.back, f32[128,128]{1,0:T(8,128)S(1)} %get-tuple-element.16.near_all, f32[3,4096]{1,0:T(4,128)S(1)} %shard_map.121.far, s32[2,4096]{1,0:T(2,128)S(1)} %copy-done.11, s32[8,512]{1,0:T(8,128)S(1)} %get-tuple-element.18.left), custom_call_target="tpu_custom_call" | custom-call | flops 1000000000 | bytes 1048576 | tf_op jit(solution)/shard_map/pallas_call | solution.py:525
  (20 shorter events, 0.1 us)
Async XLA Ops:
  2.8 34.0 %all-to-all-start = ((f32[32,56,128]{2,1,0:T(8,128)}), f32[32,56,128]{2,1,0:T(8,128)S(1)}, u32[]{:S(2)}, u32[]{:S(2)}) async-start(f32[32,56,128]{2,1,0:T(8,128)} %shard_map.118), calls=%async_computation | async-start | bytes 1835008 | tf_op jit(solution)/shard_map/all_to_all | solution.py:459
  15.5 0.8 %copy-start = (f32[3,4096]{1,0:T(4,128)S(1)}, f32[3,4096]{1,0:T(4,128)}, u32[]{:S(2)}) copy-start(f32[3,4096]{1,0:T(4,128)} %refs_3_.3) | copy-start | bytes 147460
  16.3 0.8 %copy-start.2 = (f32[3,4096]{1,0:T(4,128)S(1)}, f32[3,4096]{1,0:T(4,128)}, u32[]{:S(2)}) copy-start(f32[3,4096]{1,0:T(4,128)} %refs_4_.1) | copy-start | bytes 147460
  17.2 0.8 %copy-start.4 = (f32[3,4096]{1,0:T(4,128)S(1)}, f32[3,4096]{1,0:T(4,128)}, u32[]{:S(2)}) copy-start(f32[3,4096]{1,0:T(4,128)} %refs_5_.3) | copy-start | bytes 147460
  18.0 0.7 copy-start.6
  18.7 0.7 copy-start.7
  19.4 0.7 copy-start.8
  36.8 14.8 %collective-permute-start = (f32[16,128]{1,0:T(8,128)S(1)}, f32[16,128]{1,0:T(8,128)S(1)}, u32[]{:S(2)}, u32[]{:S(2)}) collective-permute-start(f32[16,128]{1,0:T(8,128)S(1)} %slice_reduce_fusion), channel_id=1, source_target_pairs={{0,32},{32,0},{64,96},{96,64},{128,160},{160,128},{192,224},{224,1... | collective-permute-start | bytes 24584 | tf_op jit(solution)/shard_map/ppermute | solution.py:481
  42.0 20.9 %copy-start.1 = (f32[3,4096]{1,0:T(4,128)S(1)}, f32[3,4096]{1,0:T(4,128)}, u32[]{:S(2)}) copy-start(f32[3,4096]{1,0:T(4,128)} %refs_3_.3) | copy-start | bytes 147460
  42.0 20.9 %copy-start.3 = (f32[3,4096]{1,0:T(4,128)S(1)}, f32[3,4096]{1,0:T(4,128)}, u32[]{:S(2)}) copy-start(f32[3,4096]{1,0:T(4,128)} %refs_4_.1) | copy-start | bytes 147460
  42.0 20.9 %copy-start.5 = (f32[3,4096]{1,0:T(4,128)S(1)}, f32[3,4096]{1,0:T(4,128)}, u32[]{:S(2)}) copy-start(f32[3,4096]{1,0:T(4,128)} %refs_5_.3) | copy-start | bytes 147460
  42.0 20.9 %copy-start.9 = (f32[3,3]{1,0:T(4,128)S(1)}, f32[3,3]{1,0:T(4,128)}, u32[]{:S(2)}) copy-start(f32[3,3]{1,0:T(4,128)} %refs_2_.3) | copy-start | bytes 112
  42.0 20.9 %copy-start.10 = (s32[32]{0:T(128)S(1)}, s32[32]{0:T(128)}, u32[]{:S(2)}) copy-start(s32[32]{0:T(128)} %refs_1_.3) | copy-start | bytes 388
  51.6 15.4 %copy-start.11 = (s32[2,4096]{1,0:T(2,128)S(1)}, s32[2,4096]{1,0:T(2,128)}, u32[]{:S(2)}) copy-start(s32[2,4096]{1,0:T(2,128)} %conn.1) | copy-start | bytes 98308
  51.6 15.4 %all-to-all-start.1 = ((f32[32,16,128]{2,1,0:T(8,128)}), f32[32,16,128]{2,1,0:T(8,128)S(1)}, u32[]{:S(2)}, u32[]{:S(2)}) async-start(f32[32,16,128]{2,1,0:T(8,128)} %get-tuple-element.15), calls=%async_computation.1 | async-start | bytes 524288 | tf_op jit(solution)/shard_map/all_to_all | solution.py:497
  56.3 4.9 %collective-permute-start.1 = (f32[32,128]{1,0:T(8,128)S(1)}, f32[32,128]{1,0:T(8,128)S(1)}, u32[]{:S(2)}, u32[]{:S(2)}) collective-permute-start(f32[32,128]{1,0:T(8,128)S(1)} %pad_maximum_fusion.refs_7_), channel_id=1, source_target_pairs={{0,64},{32,96},{64,128},{96,160},{128,192},{160,224},{192,0},{224,... | collective-permute-start | bytes 49160 | tf_op jit(solution)/shard_map/ppermute | solution.py:503
  57.5 4.1 %collective-permute-start.2 = (f32[32,128]{1,0:T(8,128)S(1)}, f32[32,128]{1,0:T(8,128)S(1)}, u32[]{:S(2)}, u32[]{:S(2)}) collective-permute-start(f32[32,128]{1,0:T(8,128)S(1)} %pad_maximum_fusion.refs_7_), channel_id=1, source_target_pairs={{0,128},{32,160},{64,192},{96,224},{128,0},{160,32},{192,64},{224,... | collective-permute-start | bytes 49160 | tf_op jit(solution)/shard_map/ppermute | solution.py:503
  60.0 2.9 %collective-permute-start.3 = (f32[32,128]{1,0:T(8,128)S(1)}, f32[32,128]{1,0:T(8,128)S(1)}, u32[]{:S(2)}, u32[]{:S(2)}) collective-permute-start(f32[32,128]{1,0:T(8,128)S(1)} %pad_maximum_fusion.refs_7_), channel_id=1, source_target_pairs={{0,192},{32,224},{64,0},{96,32},{128,64},{160,96},{192,128},{224,1... | collective-permute-start | bytes 49160 | tf_op jit(solution)/shard_map/ppermute | solution.py:503
